TPU v7x, 512 devices: a whole 4x8x8 slice. The times are simulated.
512 devices in a mesh: blk: 32 (over z_hi, y), uly: 8 (over x, core), rep: 2 (over z_lo).
Axes of the slice: x: 4, y: 8, z: 8 (z_hi: 4, z_lo: 2; z = z_hi * 2 + z_lo), core: 2. Of those that a mesh axis runs over, the one named last changes fastest.
Arguments:
- query_mantissa: bfloat16 [65536, 4096], P(('rep', 'blk', 'uly')), parts along dimension 0, may hold values from -8 to 8
- key_mantissa: bfloat16 [65536, 4096], P(('rep', 'blk', 'uly')), parts along dimension 0, may hold values from -16 to 16
- value_mantissa: bfloat16 [65536, 4096], P(('rep', 'blk', 'uly')), parts along dimension 0, may hold values from -48 to 48
- query_exponent: int32 [65536, 32], P(('rep', 'blk', 'uly')), parts along dimension 0, may hold values from -1 to 1
- key_exponent: int32 [65536, 32], P(('rep', 'blk', 'uly')), parts along dimension 0, may hold values from -1 to 1
- value_exponent: int32 [65536, 32], P(('rep', 'blk', 'uly')), parts along dimension 0, may hold values from -1 to 1
- merge_map: int32 [65536], P(('rep', 'blk', 'uly')), parts along dimension 0, may hold values from 0 to 7, as said below
Outputs:
- attended: bfloat16 [65536, 4096], P(('rep', 'blk', 'uly')), parts along dimension 0
There are 2 independent parts, one for each index of `rep`. A program takes and returns all parts, laid end to end along the dimension named above; each array names one. Nothing has to cross between parts.
Inputs may be any that keep to these rules, and one draw needn't show every extreme that they name: `merge_map`: within each aligned block of 128 tokens (one device's tokens) every value from 0 to 7 occurs at least once.
All inputs are finite; a program needn't handle non-finite values.
Results may differ from a plain program's by a relative error of at most 0.012.
The roundings to bfloat16 on the way count: a program that leaves them out, or rounds other values in their place, can miss the bound.
Values may be sent and summed in bfloat16 or wider, within the bound.
No kernel may reach another device: no remote copies, remote signals or barrier semaphores. Data moves between devices by JAX's collectives and lax.ppermute only.
A program may use at most 64 MiB of HBM per device.

v0:
```python
import math

import jax
import jax.numpy as jnp
from jax import lax
from jax.sharding import PartitionSpec as P

HD = 128
RATIO = 16


def sylvester(order_size):
    indices = jnp.arange(order_size, dtype=jnp.int32)
    sign_table = jnp.ones((order_size, order_size), jnp.float32)
    for bit_index in range(order_size.bit_length() - 1):
        bit_value = indices // 2**bit_index % 2
        sign_table = sign_table * (
            1.0 - 2.0 * (bit_value[:, None] * bit_value[None, :]).astype(jnp.float32)
        )
    return sign_table


def rotate(mantissa, exponent, hadamard_table):
    token_count = exponent.shape[0]
    head_count = exponent.shape[1]
    scaling = jnp.exp2(exponent.astype(jnp.float32))
    scaled = (
        mantissa.astype(jnp.float32).reshape(token_count, head_count, HD) * scaling[:, :, None]
    ).astype(jnp.bfloat16)
    rotated = jnp.dot(
        scaled.reshape(token_count * head_count, HD),
        hadamard_table,
        preferred_element_type=jnp.float32,
    )
    return rotated.reshape(token_count, head_count * HD)


def merge_rows(rotated, onehot, counts, inverse_root):
    summed = jnp.dot(
        onehot, rotated, precision=lax.Precision.HIGHEST, preferred_element_type=jnp.float32
    )
    return (summed / counts[:, None] * inverse_root).astype(jnp.bfloat16)


def tiled_counts(counts, group_size):
    return jnp.broadcast_to(counts.astype(jnp.bfloat16)[:, None], (counts.shape[0], group_size))


def make_fold(queries):
    row_count = queries.shape[0]
    local_heads = queries.shape[1] // HD
    block_rows = math.gcd(row_count, 512)
    block_count = row_count // block_rows
    inverse_root = 1.0 / math.sqrt(HD)

    def fold_piece(carry, piece, start):
        row_max, totals, accumulated = carry
        key_rows, value_rows, count_rows = piece
        log_counts = jnp.log(count_rows[:, 0].astype(jnp.float32))
        next_max = []
        next_totals = []
        next_accum = []
        for head_index in range(local_heads):
            first_column = head_index * HD
            head_keys = key_rows[:, first_column : first_column + HD]
            head_values = value_rows[:, first_column : first_column + HD]
            head_queries = queries[:, first_column : first_column + HD].reshape(
                block_count, block_rows, HD
            )

            def one_block(block_args):
                query_block, max_block, total_block, accum_block = block_args
                scores = (
                    lax.dot_general(
                        query_block,
                        head_keys,
                        (((1,), (1,)), ((), ())),
                        preferred_element_type=jnp.float32,
                    )
                    * inverse_root
                    + log_counts[None, :]
                )
                new_max = jnp.maximum(max_block, jnp.max(scores, axis=1))
                rescale = jnp.exp(max_block - new_max)
                weights = jnp.exp(scores - new_max[:, None])
                new_total = total_block * rescale + jnp.sum(weights, axis=1)
                new_accum = accum_block * rescale[:, None] + jnp.dot(
                    weights.astype(jnp.bfloat16), head_values, preferred_element_type=jnp.float32
                )
                return (new_max, new_total, new_accum)

            block_max, block_total, block_accum = lax.map(
                one_block,
                (
                    head_queries,
                    row_max[head_index].reshape(block_count, block_rows),
                    totals[head_index].reshape(block_count, block_rows),
                    accumulated[head_index].reshape(block_count, block_rows, HD),
                ),
            )
            next_max.append(block_max.reshape(row_count))
            next_totals.append(block_total.reshape(row_count))
            next_accum.append(block_accum.reshape(row_count, HD))
        return (jnp.stack(next_max), jnp.stack(next_totals), jnp.stack(next_accum))

    initial = (
        jnp.full((local_heads, row_count), -1e30, jnp.float32),
        jnp.zeros((local_heads, row_count), jnp.float32),
        jnp.zeros((local_heads, row_count, HD), jnp.float32),
    )
    return (fold_piece, initial)


def finish(carry):
    row_max, totals, accumulated = carry
    local_heads = accumulated.shape[0]
    row_count = accumulated.shape[1]
    normed = accumulated / totals[:, :, None]
    return (
        jnp.transpose(normed, (1, 0, 2)).reshape(row_count, local_heads * HD).astype(jnp.bfloat16)
    )


def per_device(
    query_mantissa,
    key_mantissa,
    value_mantissa,
    query_exponent,
    key_exponent,
    value_exponent,
    merge_map,
):
    token_count = query_mantissa.shape[0]
    merged = token_count // RATIO
    inverse_root = 1.0 / math.sqrt(HD)
    hadamard_table = sylvester(HD).astype(jnp.bfloat16)
    queries = (rotate(query_mantissa, query_exponent, hadamard_table) * inverse_root).astype(
        jnp.bfloat16
    )
    onehot = (merge_map[None, :] == jnp.arange(merged, dtype=jnp.int32)[:, None]).astype(
        jnp.float32
    )
    counts = jnp.sum(onehot, axis=1)
    key_rows = merge_rows(
        rotate(key_mantissa, key_exponent, hadamard_table), onehot, counts, inverse_root
    )
    value_rows = merge_rows(
        rotate(value_mantissa, value_exponent, hadamard_table), onehot, counts, inverse_root
    )
    spread = tiled_counts(counts, lax.axis_size("uly"))
    head_queries, head_keys, head_values, head_counts = (
        lax.all_to_all(queries, "uly", split_axis=1, concat_axis=0, tiled=True),
        lax.all_to_all(key_rows, "uly", split_axis=1, concat_axis=0, tiled=True),
        lax.all_to_all(value_rows, "uly", split_axis=1, concat_axis=0, tiled=True),
        lax.all_to_all(spread, "uly", split_axis=1, concat_axis=0, tiled=True),
    )
    fold_piece, initial = make_fold(head_queries)
    carry = fold_piece(
        initial,
        (
            lax.all_gather(head_keys, "blk", axis=0, tiled=True),
            lax.all_gather(head_values, "blk", axis=0, tiled=True),
            lax.all_gather(head_counts, "blk", axis=0, tiled=True),
        ),
        jnp.int32(0),
    )
    attended = lax.all_to_all(finish(carry), "uly", split_axis=0, concat_axis=1, tiled=True)
    return attended


def solution(mesh):
    placed = (
        P(("rep", "blk", "uly"), None),
        P(("rep", "blk", "uly"), None),
        P(("rep", "blk", "uly"), None),
        P(("rep", "blk", "uly"), None),
        P(("rep", "blk", "uly"), None),
        P(("rep", "blk", "uly"), None),
        P(("rep", "blk", "uly")),
    )
    return jax.shard_map(
        per_device,
        mesh=mesh,
        in_specs=placed,
        out_specs=P(("rep", "blk", "uly"), None),
        check_vma=False,
    )
```

profile of v0, /device:TPU:1, one launch (start us, length us, event | category | flops | bytes accessed | tf_op | source)
XLA Modules:
  0.0 294.2 jit_solution(16944059783245572483)
XLA Ops:
  6.6 1.5 reshape.546
  9.0 2.2 fusion.86
  11.2 1.8 reshape.532
  14.0 14.8 %all_to_all.86 = bf16[8,8,512]{2,0,1:T(8,128)(2,1)} all-to-all(bf16[8,8,512]{2,0,1:T(8,128)(2,1)S(1)} %bitcast.145), channel_id=1, replica_groups=mesh['blk'=32,'uly'=8,'rep'=2] {'uly'}, dimensions={1} | all-to-all | bytes 131072 | tf_op jit(solution)/shard_map/all_to_all | solution.py:153
  29.5 2.2 fusion.87
  31.7 1.8 reshape.535
  34.4 8.7 %all_to_all.87 = bf16[8,8,512]{2,0,1:T(8,128)(2,1)} all-to-all(bf16[8,8,512]{2,0,1:T(8,128)(2,1)S(1)} %bitcast.146), channel_id=1, replica_groups=mesh['blk'=32,'uly'=8,'rep'=2] {'uly'}, dimensions={1} | all-to-all | bytes 131072 | tf_op jit(solution)/shard_map/all_to_all | solution.py:154
  43.7 3.9 %all-to-all-start.2 = ((bf16[8,8,1]{0,2,1:T(2,128)(2,1)}), bf16[8,8,1]{0,2,1:T(2,128)(2,1)S(1)}, u32[]{:S(2)}, u32[]{:S(2)}) async-start(bf16[8,8,1]{0,2,1:T(2,128)(2,1)} %broadcast_in_dim.18), calls=%async_computation.2 | async-start | bytes 8192 | tf_op jit(solution)/shard_map/all_to_all | solution.py:155
  49.8 1.3 copy.47
  51.1 1.1 all-to-all-done.2
  52.2 4.2 %all-to-all-start = ((bf16[128,8,512]{2,0,1:T(8,128)(2,1)}), bf16[128,8,512]{2,0,1:T(8,128)(2,1)S(1)}, u32[]{:S(2)}, u32[]{:S(2)}) async-start(bf16[128,8,512]{2,0,1:T(8,128)(2,1)} %copy.47), calls=%async_computation | async-start | bytes 2097152 | tf_op jit(solution)/shard_map/all_to_all | solution.py:152
  56.4 1.3 dynamic-slice
  58.6 71.0 %all-reduce = bf16[2048]{0:T(1024)(128)(2,1)S(1)} all-reduce(bf16[2048]{0:T(1024)(128)(2,1)S(1)} %dynamic-update-slice), channel_id=1, replica_groups=mesh['blk'=32,'uly'=8,'rep'=2] {'blk'}, use_global_device_ids=true, to_apply=%add | all-reduce | flops 2048 | bytes 8192
  129.8 1.7 fusion.100
  131.6 66.2 %all-gather.5.cloned.1.call-done = bf16[2048,512]{1,0:T(8,128)(2,1)} async-done(((bf16[64,512]{1,0:T(8,128)(2,1)}), bf16[2048,512]{1,0:T(8,128)(2,1)}) %all-gather.5.cloned.1.call-update) | async-done | bytes 2097168 | tf_op jit(solution)/shard_map/all_gather | solution.py:162
  197.8 2.9 fusion.99
  201.6 15.5 %while.51 = (s32[]{:T(128)}, f32[2,512]{1,0:T(2,128)S(1)}, f32[2,512,128]{2,1,0:T(8,128)}, bf16[2,512,128]{2,1,0:T(8,128)(2,1)S(1)}, bf16[2048,128]{1,0:T(8,128)...) while((s32[]{:T(128)}, f32[2,512]{1,0:T(2,128)S(1)}, ...), condition=%wide.region_16.17_spmd, body=%wide.region_13.16_spmd.sunk | while | flops 548472320 | bytes 30853260 | solution.py:92
  202.4 1.9 copy-done
  204.3 0.9 fusion.158
  205.3 4.0 %fusion.159 = f32[2,512,128]{2,1,0:T(8,128)} fusion(f32[2,512,128]{2,1,0:T(8,128)} %get-tuple-element.470, s32[]{:T(128)S(6)} %copy.73, bf16[2048,128]{1,0:T(8,128)(2,1)} %get-tuple-element.483, f32[512,2048]{1,0:T(8,128)} %copy-done, f32[512]{0:T(512)S(1)} %broadcast_maximum_fusion.11, f32[2048]{0:T(1024)S(1)} %get-tuple-element.482, ...), kind=kOutput, calls=%fused_computation.59.clone.1 | convolution fusion | flops 272695296 | bytes 4993028 | tf_op jit(solution)/shard_map/while/body/eval_jaxpr/dot_general | solution.py:87
  210.1 1.9 copy-done
  212.1 0.9 fusion.158
  213.0 4.0 %fusion.159 = f32[2,512,128]{2,1,0:T(8,128)} fusion(f32[2,512,128]{2,1,0:T(8,128)} %get-tuple-element.470, s32[]{:T(128)S(6)} %copy.73, bf16[2048,128]{1,0:T(8,128)(2,1)} %get-tuple-element.483, f32[512,2048]{1,0:T(8,128)} %copy-done, f32[512]{0:T(512)S(1)} %broadcast_maximum_fusion.11, f32[2048]{0:T(1024)S(1)} %get-tuple-element.482, ...), kind=kOutput, calls=%fused_computation.59.clone.1 | convolution fusion | flops 272695296 | bytes 4993028 | tf_op jit(solution)/shard_map/while/body/eval_jaxpr/dot_general | solution.py:87
  217.1 1.2 copy.53
  218.4 14.1 %while.50 = (s32[]{:T(128)}, f32[2,512]{1,0:T(2,128)S(1)}, f32[2,512,128]{2,1,0:T(8,128)S(1)}, bf16[2,512,128]{2,1,0:T(8,128)(2,1)S(1)}, bf16[2048,128]{1,0:T(8,...) while((s32[]{:T(128)}, f32[2,512]{1,0:T(2,128)S(1)}, ...), condition=%wide.region_12.13_spmd, body=%wide.region_9.12_spmd.sunk | while | flops 548472320 | bytes 30853260 | solution.py:92
  219.2 1.9 copy-done.1
  221.1 0.9 fusion.152
  222.1 3.3 %fusion.153 = f32[2,512,128]{2,1,0:T(8,128)S(1)} fusion(f32[2,512,128]{2,1,0:T(8,128)S(1)} %get-tuple-element.497, s32[]{:T(128)S(6)} %copy.82, bf16[2048,128]{1,0:T(8,128)(2,1)} %get-tuple-element.510, f32[512,2048]{1,0:T(8,128)} %copy-done.1, f32[512]{0:T(512)S(1)} %broadcast_maximum_fusion.10, f32[2048]{0:T(1024)S(1)} %get-tuple-element.509, ...), kind=kOutput, calls=%fused_computation.42.clone.1 | convolution fusion | flops 272695296 | bytes 4993028 | tf_op jit(solution)/shard_map/while/body/eval_jaxpr/dot_general | solution.py:87
  226.3 1.9 copy-done.1
  228.2 0.9 fusion.152
  229.2 3.3 %fusion.153 = f32[2,512,128]{2,1,0:T(8,128)S(1)} fusion(f32[2,512,128]{2,1,0:T(8,128)S(1)} %get-tuple-element.497, s32[]{:T(128)S(6)} %copy.82, bf16[2048,128]{1,0:T(8,128)(2,1)} %get-tuple-element.510, f32[512,2048]{1,0:T(8,128)} %copy-done.1, f32[512]{0:T(512)S(1)} %broadcast_maximum_fusion.10, f32[2048]{0:T(1024)S(1)} %get-tuple-element.509, ...), kind=kOutput, calls=%fused_computation.42.clone.1 | convolution fusion | flops 272695296 | bytes 4993028 | tf_op jit(solution)/shard_map/while/body/eval_jaxpr/dot_general | solution.py:87
  232.5 1.0 copy.52
  233.5 14.0 %while.49 = (s32[]{:T(128)}, f32[2,512]{1,0:T(2,128)S(1)}, f32[2,512,128]{2,1,0:T(8,128)S(1)}, bf16[2,512,128]{2,1,0:T(8,128)(2,1)S(1)}, bf16[2048,128]{1,0:T(8,...) while((s32[]{:T(128)}, f32[2,512]{1,0:T(2,128)S(1)}, ...), condition=%wide.region_8.9_spmd, body=%wide.region_5.8_spmd.sunk | while | flops 548472320 | bytes 32950440 | solution.py:92
  234.4 1.9 copy-done.2
  236.3 0.9 fusion.146
  237.3 3.2 %fusion.147 = f32[2,512,128]{2,1,0:T(8,128)S(1)} fusion(f32[2,512,128]{2,1,0:T(8,128)S(1)} %get-tuple-element.524, s32[]{:T(128)S(6)} %copy.91, bf16[2048,128]{1,0:T(8,128)(2,1)S(1)} %copy-done.8, f32[512,2048]{1,0:T(8,128)} %copy-done.2, f32[512]{0:T(512)S(1)} %broadcast_maximum_fusion.9, f32[2048]{0:T(1024)S(1)} %get-tuple-element.536, ...), kind=kOutput, calls=%fused_computation.25.clone.1 | convolution fusion | flops 272695296 | bytes 4993028 | tf_op jit(solution)/shard_map/while/body/eval_jaxpr/dot_general | solution.py:87
  241.4 1.9 copy-done.2
  243.3 0.9 fusion.146
  244.3 3.2 %fusion.147 = f32[2,512,128]{2,1,0:T(8,128)S(1)} fusion(f32[2,512,128]{2,1,0:T(8,128)S(1)} %get-tuple-element.524, s32[]{:T(128)S(6)} %copy.91, bf16[2048,128]{1,0:T(8,128)(2,1)S(1)} %copy-done.8, f32[512,2048]{1,0:T(8,128)} %copy-done.2, f32[512]{0:T(512)S(1)} %broadcast_maximum_fusion.9, f32[2048]{0:T(1024)S(1)} %get-tuple-element.536, ...), kind=kOutput, calls=%fused_computation.25.clone.1 | convolution fusion | flops 272695296 | bytes 4993028 | tf_op jit(solution)/shard_map/while/body/eval_jaxpr/dot_general | solution.py:87
  247.8 14.0 %while.48 = (s32[]{:T(128)}, f32[2,512]{1,0:T(2,128)S(1)}, f32[2,512,128]{2,1,0:T(8,128)S(1)}, bf16[2,512,128]{2,1,0:T(8,128)(2,1)S(1)}, bf16[2048,128]{1,0:T(8,...) while((s32[]{:T(128)}, f32[2,512]{1,0:T(2,128)S(1)}, ...), condition=%wide.region_4.5_spmd, body=%wide.region_1.4_spmd.sunk | while | flops 548472320 | bytes 32950440 | solution.py:92
  248.6 1.9 copy-done.3
  250.5 0.9 fusion.140
  251.6 3.2 %fusion.141 = f32[2,512,128]{2,1,0:T(8,128)S(1)} fusion(f32[2,512,128]{2,1,0:T(8,128)S(1)} %get-tuple-element.551, s32[]{:T(128)S(6)} %copy.100, bf16[2048,128]{1,0:T(8,128)(2,1)S(1)} %copy-done.7, f32[512,2048]{1,0:T(8,128)} %copy-done.3, f32[512]{0:T(512)S(1)} %broadcast_maximum_fusion.8, f32[2048]{0:T(1024)S(1)} %get-tuple-element.563, ...), kind=kOutput, calls=%fused_computation.8.clone.1 | convolution fusion | flops 272695296 | bytes 4993028 | tf_op jit(solution)/shard_map/while/body/eval_jaxpr/dot_general | solution.py:87
  255.6 1.9 copy-done.3
  257.5 0.9 fusion.140
  258.5 3.2 %fusion.141 = f32[2,512,128]{2,1,0:T(8,128)S(1)} fusion(f32[2,512,128]{2,1,0:T(8,128)S(1)} %get-tuple-element.551, s32[]{:T(128)S(6)} %copy.100, bf16[2048,128]{1,0:T(8,128)(2,1)S(1)} %copy-done.7, f32[512,2048]{1,0:T(8,128)} %copy-done.3, f32[512]{0:T(512)S(1)} %broadcast_maximum_fusion.8, f32[2048]{0:T(1024)S(1)} %get-tuple-element.563, ...), kind=kOutput, calls=%fused_computation.8.clone.1 | convolution fusion | flops 272695296 | bytes 4993028 | tf_op jit(solution)/shard_map/while/body/eval_jaxpr/dot_general | solution.py:87
  262.7 23.3 %all_to_all.88 = bf16[8,128,512]{1,2,0:T(8,128)(2,1)S(1)} all-to-all(bf16[8,128,512]{1,2,0:T(8,128)(2,1)S(1)} %copy.54), channel_id=1, replica_groups=mesh['blk'=32,'uly'=8,'rep'=2] {'uly'}, dimensions={0} | all-to-all | bytes 2097152 | tf_op jit(solution)/shard_map/all_to_all | solution.py:167
  286.1 1.3 copy.55
  (112 shorter events, 15.7 us)
Async XLA Ops:
  6.5 123.3 %all-gather.3.cloned.1.call-start = ((), (), s32[]{:S(2)}) async-start(), calls=%async_computation.5 | async-start | bytes 2162688 | tf_op jit(solution)/shard_map/all_gather | solution.py:161
  9.0 4.1 %copy-start.11 = (s32[128]{0:T(128)S(1)}, s32[128]{0:T(128)}, u32[]{:S(2)}) copy-start(s32[128]{0:T(128)} %param.21) | copy-start | bytes 1540
  11.2 17.6 %copy-start.5 = (bf16[128,4096]{1,0:T(8,128)(2,1)S(1)}, bf16[128,4096]{1,0:T(8,128)(2,1)}, u32[]{:S(2)}) copy-start(bf16[128,4096]{1,0:T(8,128)(2,1)} %param.17) | copy-start | bytes 3145732
  11.2 18.1 %copy-start.9 = (s32[128,32]{0,1:T(8,128)S(1)}, s32[128,32]{0,1:T(8,128)}, u32[]{:S(2)}) copy-start(s32[128,32]{0,1:T(8,128)} %param.20) | copy-start | bytes 49156
  28.8 169.0 %all-gather.5.cloned.1.call-start = ((), (), s32[]{:S(2)}) async-start(), calls=%async_computation.6 | async-start | bytes 2162688 | tf_op jit(solution)/shard_map/all_gather | solution.py:162
  31.7 15.9 %copy-start.6 = (bf16[128,4096]{1,0:T(8,128)(2,1)S(1)}, bf16[128,4096]{1,0:T(8,128)(2,1)}, u32[]{:S(2)}) copy-start(bf16[128,4096]{1,0:T(8,128)(2,1)} %param.15) | copy-start | bytes 3145732
  31.7 16.3 %copy-start.10 = (s32[128,32]{0,1:T(8,128)S(1)}, s32[128,32]{0,1:T(8,128)}, u32[]{:S(2)}) copy-start(s32[128,32]{0,1:T(8,128)} %param.18) | copy-start | bytes 49156
  43.7 8.5 %all-to-all-start.2 = ((bf16[8,8,1]{0,2,1:T(2,128)(2,1)}), bf16[8,8,1]{0,2,1:T(2,128)(2,1)S(1)}, u32[]{:S(2)}, u32[]{:S(2)}) async-start(bf16[8,8,1]{0,2,1:T(2,128)(2,1)} %broadcast_in_dim.18), calls=%async_computation.2 | async-start | bytes 8192 | tf_op jit(solution)/shard_map/all_to_all | solution.py:155
  52.2 77.4 %all-to-all-start = ((bf16[128,8,512]{2,0,1:T(8,128)(2,1)}), bf16[128,8,512]{2,0,1:T(8,128)(2,1)S(1)}, u32[]{:S(2)}, u32[]{:S(2)}) async-start(bf16[128,8,512]{2,0,1:T(8,128)(2,1)} %copy.47), calls=%async_computation | async-start | bytes 2097152 | tf_op jit(solution)/shard_map/all_to_all | solution.py:152
  202.4 1.9 copy-start
  210.1 1.9 copy-start
  219.2 1.9 copy-start.1
  226.2 1.9 copy-start.1
  233.6 3.8 %copy-start.8 = (bf16[2048,128]{1,0:T(8,128)(2,1)S(1)}, bf16[2048,128]{1,0:T(8,128)(2,1)}, u32[]{:S(2)}) copy-start(bf16[2048,128]{1,0:T(8,128)(2,1)} %get-tuple-element.537) | copy-start | bytes 1572868 | tf_op jit(solution)/shard_map/while
  234.4 1.9 copy-start.2
  240.5 3.8 %copy-start.8 = (bf16[2048,128]{1,0:T(8,128)(2,1)S(1)}, bf16[2048,128]{1,0:T(8,128)(2,1)}, u32[]{:S(2)}) copy-start(bf16[2048,128]{1,0:T(8,128)(2,1)} %get-tuple-element.537) | copy-start | bytes 1572868 | tf_op jit(solution)/shard_map/while
  241.3 1.9 copy-start.2
  247.8 14.3 %copy-start.4 = (f32[1,1024,128]{1,2,0:T(8,128)S(1)}, f32[1,1024,128]{1,2,0:T(8,128)}, u32[]{:S(2)}) copy-start(f32[1,1024,128]{1,2,0:T(8,128)} %copy.52) | copy-start | bytes 1572868
  247.8 3.8 %copy-start.7 = (bf16[2048,128]{1,0:T(8,128)(2,1)S(1)}, bf16[2048,128]{1,0:T(8,128)(2,1)}, u32[]{:S(2)}) copy-start(bf16[2048,128]{1,0:T(8,128)(2,1)} %get-tuple-element.564) | copy-start | bytes 1572868 | tf_op jit(solution)/shard_map/while
  248.6 1.9 copy-start.3
  254.8 3.8 %copy-start.7 = (bf16[2048,128]{1,0:T(8,128)(2,1)S(1)}, bf16[2048,128]{1,0:T(8,128)(2,1)}, u32[]{:S(2)}) copy-start(bf16[2048,128]{1,0:T(8,128)(2,1)} %get-tuple-element.564) | copy-start | bytes 1572868 | tf_op jit(solution)/shard_map/while
  255.6 1.9 copy-start.3
Sparse Core Ops, SparseCore 0:
  28.9 82.7 all-gather.2
  114.9 82.8 all-gather.4
where the time goes:
time: 295 us; the launch traced here: 294 us
  blocking collectives  118 us (40%)
  waiting for transfers between devices  67.4 us (23%)
  matrix products  40.8 us (14%)
  local copies, waits for them, and re-layouts  36.7 us (12%)
  between operations  14.3 us (5%)
  other arithmetic  8.84 us (3%)
  starting transfers between devices  8.14 us (3%)
    unnamed x1, blocking collectives  71 us
    all_gather x1, waiting for transfers between devices, per_device(): lax.all_gather(head_values, 'blk', axis=0, tiled=True)  66.2 us
    dot_general x8, matrix products, one_block(): jnp.dot(weights.astype(jnp.bfloat16), head_values, preferred_element_type...  27.4 us
    all_to_all x1, blocking collectives, per_device(): lax.all_to_all(finish(carry), 'uly', split_axis=0, concat_axis=1, tiled=T...  23.3 us
    while x24, local copies, waits for them, and re-layouts  15.5 us
    all_to_all x1, blocking collectives, per_device(): lax.all_to_all(key_rows, 'uly', split_axis=1, concat_axis=0, tiled=True)  14.8 us
    all_to_all x1, blocking collectives, per_device(): lax.all_to_all(value_rows, 'uly', split_axis=1, concat_axis=0, tiled=True)  8.67 us
    reduce_sum x8, other arithmetic, one_block(): new_total = total_block * rescale + jnp.sum(weights, axis=1)  7.54 us
  transfers between devices with their start and end apart: 4, of which 2 were waited for; matrix products, arithmetic and copies ran while one was open for 4% of the time, Pallas kernels for 0%

commit v1 on v0

v1 whole, which is shorter than its diff:
```python
import math

import jax
import jax.numpy as jnp
import numpy as np
from jax import lax
from jax.experimental import pallas as pl
from jax.experimental.pallas import tpu as pltpu
from jax.sharding import Mesh
from jax.sharding import PartitionSpec as P

HD = 128
MERGED = 8
ZH, Y, X, CORE = 4, 8, 4, 2
GROUP = ("zh", "x", "core")
SCALE = 1.0 / math.sqrt(HD)
LOG2E = math.log2(math.e)


def sylvester(size):
    index = np.arange(size)
    both = index[:, None] & index[None, :]
    odd = np.zeros_like(both)
    for bit in range(size.bit_length() - 1):
        odd ^= (both >> bit) & 1
    return (1 - 2 * odd).astype(np.float32)


def prepare_merged_kernel(key_ref, value_ref, key_exp_ref, value_exp_ref, map_ref, table_ref, out_ref, sums):
    tokens = key_ref.shape[0]
    heads = key_exp_ref.shape[1]
    slot = lax.broadcasted_iota(jnp.int32, (MERGED, tokens), 0)
    onehot = (map_ref[...] == slot).astype(jnp.float32)
    counts = jnp.sum(onehot, axis=1, keepdims=True)
    count_rows = jnp.broadcast_to(counts, (MERGED, HD)).astype(jnp.bfloat16)
    for index, (mantissa_ref, exp_ref) in enumerate(((key_ref, key_exp_ref), (value_ref, value_exp_ref))):
        scaling = jnp.exp2(exp_ref[...].astype(jnp.float32)).T
        for head in range(heads):
            chosen = (onehot * scaling[head : head + 1, :]).astype(jnp.bfloat16)
            sums[pl.ds((index * heads + head) * MERGED, MERGED), :] = jnp.dot(
                chosen, mantissa_ref[:, head * HD : (head + 1) * HD], preferred_element_type=jnp.float32
            )
    rotated = jnp.dot(
        sums[...], table_ref[...], precision=lax.Precision.HIGHEST, preferred_element_type=jnp.float32
    ).reshape(2, heads, MERGED, HD)
    merged = (rotated / counts[None, None, :, :] * SCALE).astype(jnp.bfloat16)
    for head in range(heads):
        out_ref[head, 0:MERGED, :] = merged[0, head]
        out_ref[head, MERGED : 2 * MERGED, :] = merged[1, head]
        out_ref[head, 2 * MERGED : 3 * MERGED, :] = count_rows


def prepare_merged(key, value, key_exp, value_exp, merge_map, table):
    heads = key_exp.shape[1]
    return pl.pallas_call(
        prepare_merged_kernel,
        out_shape=jax.ShapeDtypeStruct((heads, 3 * MERGED, HD), jnp.bfloat16),
        scratch_shapes=[pltpu.VMEM((2 * heads * MERGED, HD), jnp.float32)],
        compiler_params=pltpu.CompilerParams(vmem_limit_bytes=24 * 2**20),
        cost_estimate=pl.CostEstimate(flops=2**27, bytes_accessed=2**21, transcendentals=0),
        name="prepare_merged",
    )(key, value, key_exp, value_exp, merge_map.reshape(1, -1), table)


def prepare_queries_kernel(query_ref, exp_ref, table_ref, out_ref):
    heads = exp_ref.shape[1]
    scaling = jnp.exp2(exp_ref[...].astype(jnp.float32)) * SCALE
    for head in range(heads):
        rotated = jnp.dot(
            query_ref[:, head * HD : (head + 1) * HD], table_ref[...], preferred_element_type=jnp.float32
        )
        out_ref[head] = (rotated * scaling[:, head : head + 1]).astype(jnp.bfloat16)


def prepare_queries(query, query_exp, table):
    tokens = query.shape[0]
    heads = query_exp.shape[1]
    return pl.pallas_call(
        prepare_queries_kernel,
        out_shape=jax.ShapeDtypeStruct((heads, tokens, HD), jnp.bfloat16),
        compiler_params=pltpu.CompilerParams(vmem_limit_bytes=16 * 2**20),
        cost_estimate=pl.CostEstimate(flops=2**27, bytes_accessed=2**21, transcendentals=0),
        name="prepare_queries",
    )(query, query_exp, table)


def repack_kernel(in_ref, out_ref):
    sources = in_ref.shape[0]
    half = sources // 2
    rows = half * MERGED
    ones = jnp.full((16, HD), 1.0 / HD, jnp.bfloat16)
    for part in range(2):
        block = in_ref[part * half : (part + 1) * half]
        out_ref[part, 0:rows, :] = block[:, 0:MERGED, :].reshape(rows, HD)
        out_ref[part, rows : 2 * rows, :] = block[:, MERGED : 2 * MERGED, :].reshape(rows, HD)
        spread = block[:, 2 * MERGED : 3 * MERGED, :].reshape(rows, HD)
        counts = lax.dot_general(ones, spread, (((1,), (1,)), ((), ())), preferred_element_type=jnp.float32)
        out_ref[part, 2 * rows : 2 * rows + 16, :] = counts.astype(jnp.bfloat16)


def repack(received):
    sources = received.shape[0]
    rows = sources * MERGED // 2
    return pl.pallas_call(
        repack_kernel,
        out_shape=jax.ShapeDtypeStruct((2, 2 * rows + 16, HD), jnp.bfloat16),
        cost_estimate=pl.CostEstimate(flops=2**20, bytes_accessed=2**18, transcendentals=0),
        name="repack",
    )(received)


def attend_kernel(parts, *refs):
    query_ref = refs[0]
    piece_refs = refs[1 : 1 + parts]
    out_ref, keys, values, logs = refs[1 + parts :]

    @pl.when(pl.program_id(0) == 0)
    def _():
        place = 0
        for piece_ref in piece_refs:
            for half in range(piece_ref.shape[0]):
                rows = HD
                keys[place : place + rows, :] = piece_ref[half, 0:rows, :]
                values[place : place + rows, :] = piece_ref[half, rows : 2 * rows, :]
                counts = piece_ref[half, 2 * rows : 2 * rows + 16, :].astype(jnp.float32)
                logs[:, place : place + rows] = jnp.log(counts[0:8]) * LOG2E
                place += rows

    scores = lax.dot_general(
        query_ref[...], keys[...], (((1,), (1,)), ((), ())), preferred_element_type=jnp.float32
    )
    scores = scores * (SCALE * LOG2E) + logs[0:1, :]
    row_max = jnp.max(scores, axis=1, keepdims=True)
    weights = jnp.exp2(scores - row_max)
    denominator = jnp.sum(weights, axis=1, keepdims=True)
    mixed = jnp.dot(weights.astype(jnp.bfloat16), values[...], preferred_element_type=jnp.float32)
    out_ref[...] = (mixed / denominator).astype(jnp.bfloat16)


def attend(queries, pieces, slots, block=512):
    rows = queries.shape[0]
    parts = len(pieces)
    return pl.pallas_call(
        lambda *refs: attend_kernel(parts, *refs),
        grid=(rows // block,),
        in_specs=[pl.BlockSpec((block, HD), lambda i: (i, 0))]
        + [pl.BlockSpec(piece.shape, lambda i: (0, 0, 0)) for piece in pieces],
        out_specs=pl.BlockSpec((block, HD), lambda i: (i, 0)),
        out_shape=jax.ShapeDtypeStruct((rows, HD), jnp.bfloat16),
        scratch_shapes=[
            pltpu.VMEM((slots, HD), jnp.bfloat16),
            pltpu.VMEM((slots, HD), jnp.bfloat16),
            pltpu.VMEM((8, slots), jnp.float32),
        ],
        compiler_params=pltpu.CompilerParams(vmem_limit_bytes=40 * 2**20),
        cost_estimate=pl.CostEstimate(
            flops=4 * rows * slots * HD, bytes_accessed=4 * rows * HD, transcendentals=rows * slots
        ),
        name="attend",
    )(queries, *pieces)


def unfold_kernel(in_ref, out_ref):
    for head in range(in_ref.shape[0]):
        out_ref[:, head * HD : (head + 1) * HD] = in_ref[head]


def unfold(attended):
    heads, tokens, _ = attended.shape
    return pl.pallas_call(
        unfold_kernel,
        out_shape=jax.ShapeDtypeStruct((tokens, heads * HD), jnp.bfloat16),
        name="unfold",
    )(attended)


def shifted(size, by):
    return [(index, (index + by) % size) for index in range(size)]


def per_device(
    query_mantissa,
    key_mantissa,
    value_mantissa,
    query_exponent,
    key_exponent,
    value_exponent,
    merge_map,
):
    tokens = query_mantissa.shape[0]
    heads = query_exponent.shape[1]
    table = jnp.asarray(sylvester(HD))
    merged = prepare_merged(key_mantissa, value_mantissa, key_exponent, value_exponent, merge_map, table)
    queries = prepare_queries(query_mantissa, query_exponent, table.astype(jnp.bfloat16))
    received = lax.all_to_all(merged, GROUP, split_axis=0, concat_axis=0, tiled=True)
    queries, received = lax.optimization_barrier((queries, received))
    head_queries = lax.all_to_all(queries, GROUP, split_axis=0, concat_axis=0, tiled=True)
    own = repack(received)
    up = down = own
    pieces = [own]
    for step in range(1, Y // 2):
        up = lax.ppermute(up, "y", shifted(Y, 1))
        down = lax.ppermute(down, "y", shifted(Y, -1))
        pieces += [up, down]
    pieces.append(lax.ppermute(up[0:1], "y", shifted(Y, 1)))
    pieces.append(lax.ppermute(down[1:2], "y", shifted(Y, -1)))
    attended = attend(head_queries.reshape(heads * tokens, HD), pieces, Y * heads * MERGED)
    returned = lax.all_to_all(attended.reshape(heads, tokens, HD), GROUP, split_axis=0, concat_axis=0, tiled=True)
    return unfold(returned)


def solution(mesh):
    fine = Mesh(mesh.devices.reshape(ZH, Y, X, CORE, 2), ("zh", "y", "x", "core", "rep"))
    tokens = P(("rep", "zh", "y", "x", "core"), None)
    return jax.shard_map(
        per_device,
        mesh=fine,
        in_specs=(tokens,) * 6 + (P(("rep", "zh", "y", "x", "core")),),
        out_specs=tokens,
        check_vma=False,
    )
```

time: 295 us -> 141 us (0.48)
  blocking collectives: 118 us -> 41.3 us
  waiting for transfers between devices: 67.4 us -> 15.8 us
  matrix products: 40.8 us -> 0 us
  starting transfers between devices: 8.14 us -> 46.9 us
  local copies, waits for them, and re-layouts: 36.7 us -> 5.48 us
  Pallas kernels: 0 us -> 30.9 us
  between operations: 14.3 us -> 0.18 us
  other arithmetic: 8.84 us -> 0 us
    unnamed x1 -> x0, blocking collectives: 71 us -> none
    all_gather x2 -> x0, waiting for transfers between devices: 66.3 us -> none  [the longest x1 66.2 us: per_device(): lax.all_gather(head_values, 'blk', axis=0, tiled=True)]
    dot_general x21 -> x0, matrix products: 40.8 us -> none  [the longest x8 27.4 us: one_block(): jnp.dot(weights.astype(jnp.bfloat16), head_values, preferred_element_type...]
    pallas_call x0 -> x5, Pallas kernels: none -> 30.9 us  [the longest x1 23.3 us: attend(): pl.pallas_call(lambda *refs: attend_kernel(parts, *refs), grid=(rows // b...]
    ppermute x0 -> x8, starting transfers between devices: none -> 28.6 us  [the longest x3 15.7 us: per_device(): down = lax.ppermute(down, 'y', shifted(Y, -1))]
    while x24 -> x0, local copies, waits for them, and re-layouts: 15.5 us -> none
    all_to_all x2, starting transfers between devices: 8.09 us -> 18.3 us  [the longest x1 14.6 us: per_device(): lax.all_to_all(merged, GROUP, split_axis=0, concat_axis=0, tiled=True)]
    all_to_all x2, waiting for transfers between devices: 1.09 us -> 10.1 us  [the longest x1 10.1 us: per_device(): lax.all_to_all(merged, GROUP, split_axis=0, concat_axis=0, tiled=True)]
  transfers between devices with their start and end apart: 4 -> 10, of which waited for: 2 -> 5; matrix products, arithmetic and copies ran while one was open for 4% -> 0% of each run, Pallas kernels for 0% -> 2%
where the time goes in v1:
time: 141 us
  starting transfers between devices  46.9 us (33%)
  blocking collectives  41.3 us (29%)
  Pallas kernels  30.9 us (22%)
  waiting for transfers between devices  15.8 us (11%)
  local copies, waits for them, and re-layouts  5.48 us (4%)
    all_to_all x1, blocking collectives, per_device(): lax.all_to_all(attended.reshape(heads, tokens, HD), GROUP, split_axis=0,...  41.3 us
    pallas_call x1, Pallas kernels, attend(): pl.pallas_call(lambda *refs: attend_kernel(parts, *refs), grid=(rows // b...  23.3 us
    ppermute x3, starting transfers between devices, per_device(): down = lax.ppermute(down, 'y', shifted(Y, -1))  15.7 us
    all_to_all x1, starting transfers between devices, per_device(): lax.all_to_all(merged, GROUP, split_axis=0, concat_axis=0, tiled=True)  14.6 us
    all_to_all x1, waiting for transfers between devices, per_device(): lax.all_to_all(merged, GROUP, split_axis=0, concat_axis=0, tiled=True)  10.1 us
    ppermute x3, starting transfers between devices, per_device(): up = lax.ppermute(up, 'y', shifted(Y, 1))  5.75 us
    unnamed x23, local copies, waits for them, and re-layouts  5.47 us
    ppermute x1, starting transfers between devices, per_device(): pieces.append(lax.ppermute(down[1:2], 'y', shifted(Y, -1)))  5.28 us
  transfers between devices with their start and end apart: 10, of which 5 were waited for; matrix products, arithmetic and copies ran while one was open for 0% of the time, Pallas kernels for 2%

profile of v1, /device:TPU:1, one launch (start us, length us, event | category | flops | bytes accessed | tf_op | source)
XLA Modules:
  0.0 140.5 jit_solution(13626547489498639047)
XLA Ops:
  0.0 0.0 copy-start.4
  0.0 0.0 copy-start.8
  0.0 0.9 copy.10.key_exp_ref
  0.9 0.0 copy-done.8
  0.9 0.1 copy.11.value_exp_ref
  1.0 0.0 copy-start.6
  1.0 0.0 copy-done.4
  1.0 0.6 copy-done.6
  1.6 0.0 copy-start
  1.6 1.2 copy-done
  2.9 0.0 copy-start.1
  2.9 1.2 copy-done.1
  4.1 0.0 copy-start.2
  4.1 1.7 %prepare_merged.1 = bf16[32,24,128]{2,1,0:T(8,128)(2,1)} custom-call(bf16[128,4096]{1,0:T(8,128)(2,1)S(1)} %copy-done, bf16[128,4096]{1,0:T(8,128)(2,1)S(1)} %copy-done.1, s32[128,32]{1,0:T(8,128)S(1)} %copy.10.key_exp_ref, s32[128,32]{1,0:T(8,128)S(1)} %copy.11.value_exp_ref, s32[1,128]{1,0:T(1,128)S(1)} %bitcast.5, f32[128,128]{1,0:T(8,128)S(1)} %copy-done.4), custom_call_target="tpu_custom_call" | custom-call | flops 134217728 | bytes 2097152 | tf_op jit(solution)/shard_map/prepare_merged/pallas_call | solution.py:55
  5.7 0.0 copy-start.9
  5.7 14.6 %all-to-all-start = ((bf16[32,24,128]{2,1,0:T(8,128)(2,1)}), bf16[32,24,128]{2,1,0:T(8,128)(2,1)S(1)}, u32[]{:S(2)}, u32[]{:S(2)}) async-start(bf16[32,24,128]{2,1,0:T(8,128)(2,1)} %prepare_merged.1), calls=%async_computation | async-start | bytes 393216 | tf_op jit(solution)/shard_map/all_to_all | solution.py:195
  20.3 0.0 copy-done.9
  20.3 0.0 copy-start.5
  20.3 0.1 copy.9.exp_ref
  20.4 0.0 copy-done.2
  20.4 0.6 copy-done.5
  21.1 1.7 %prepare_queries.1 = bf16[32,128,128]{2,1,0:T(8,128)(2,1)} custom-call(bf16[128,4096]{1,0:T(8,128)(2,1)S(1)} %copy-done.2, s32[128,32]{1,0:T(8,128)S(1)} %copy.9.exp_ref, bf16[128,128]{1,0:T(8,128)(2,1)S(1)} %copy-done.5), custom_call_target="tpu_custom_call" | custom-call | flops 134217728 | bytes 2097152 | tf_op jit(solution)/shard_map/prepare_queries/pallas_call | solution.py:78
  22.7 10.1 %all-to-all-done.in_ref = bf16[32,24,128]{2,1,0:T(8,128)(2,1)S(1)} async-done(((bf16[32,24,128]{2,1,0:T(8,128)(2,1)}), bf16[32,24,128]{2,1,0:T(8,128)(2,1)S(1)}, u32[]{:S(2)}, u32[]{:S(2)}) %all-to-all-start) | async-done | bytes 196640 | tf_op jit(solution)/shard_map/all_to_all | solution.py:195
  32.9 0.0 copy-start.7
  32.9 0.7 copy-done.7
  33.5 3.7 %all-to-all-start.1 = ((bf16[32,128,128]{2,1,0:T(8,128)(2,1)}), bf16[32,128,128]{2,1,0:T(8,128)(2,1)S(1)}, u32[]{:S(2)}, u32[]{:S(2)}) async-start(bf16[32,128,128]{2,1,0:T(8,128)(2,1)} %prepare_queries.1), calls=%async_computation.1 | async-start | bytes 2097152 | tf_op jit(solution)/shard_map/all_to_all | solution.py:197
  37.3 1.7 %repack.1.refs_1_ = bf16[2,272,128]{2,1,0:T(8,128)(2,1)} custom-call(bf16[32,24,128]{2,1,0:T(8,128)(2,1)} %copy-done.7), custom_call_target="tpu_custom_call" | custom-call | flops 1048576 | bytes 262144 | tf_op jit(solution)/shard_map/repack/pallas_call | solution.py:104
  39.0 5.2 %collective-permute-start.1 = (bf16[2,272,128]{2,1,0:T(8,128)(2,1)}, bf16[2,272,128]{2,1,0:T(8,128)(2,1)S(1)}, u32[]{:S(2)}, u32[]{:S(2)}) collective-permute-start(bf16[2,272,128]{2,1,0:T(8,128)(2,1)} %repack.1.refs_1_), channel_id=1, source_target_pairs={{0,112},{16,0},{32,16},{48,32},{64,48},{80,64},{96,80},{112,96},{1... | collective-permute-start | bytes 417800 | tf_op jit(solution)/shard_map/ppermute | solution.py:203
  44.2 1.9 %collective-permute-start = (bf16[2,272,128]{2,1,0:T(8,128)(2,1)}, bf16[2,272,128]{2,1,0:T(8,128)(2,1)S(1)}, u32[]{:S(2)}, u32[]{:S(2)}) collective-permute-start(bf16[2,272,128]{2,1,0:T(8,128)(2,1)} %repack.1.refs_1_), channel_id=1, source_target_pairs={{0,16},{16,32},{32,48},{48,64},{64,80},{80,96},{96,112},{112,0},{1... | collective-permute-start | bytes 417800 | tf_op jit(solution)/shard_map/ppermute | solution.py:202
  46.1 1.1 collective-permute-done.1.refs_3_
  47.3 5.2 %collective-permute-start.3 = (bf16[2,272,128]{2,1,0:T(8,128)(2,1)S(1)}, bf16[2,272,128]{2,1,0:T(8,128)(2,1)S(1)}, u32[]{:S(2)}, u32[]{:S(2)}) collective-permute-start(bf16[2,272,128]{2,1,0:T(8,128)(2,1)S(1)} %collective-permute-done.1.refs_3_), channel_id=1, source_target_pairs={{0,112},{16,0},{32,16},{48,32},{64,48},{80,64},{96,80},{112,96},{1... | collective-permute-start | bytes 417800 | tf_op jit(solution)/shard_map/ppermute | solution.py:203
  52.5 0.0 collective-permute-done.refs_2_
  52.5 1.9 %collective-permute-start.2 = (bf16[2,272,128]{2,1,0:T(8,128)(2,1)S(1)}, bf16[2,272,128]{2,1,0:T(8,128)(2,1)S(1)}, u32[]{:S(2)}, u32[]{:S(2)}) collective-permute-start(bf16[2,272,128]{2,1,0:T(8,128)(2,1)S(1)} %collective-permute-done.refs_2_), channel_id=1, source_target_pairs={{0,16},{16,32},{32,48},{48,64},{64,80},{80,96},{96,112},{112,0},{1... | collective-permute-start | bytes 417800 | tf_op jit(solution)/shard_map/ppermute | solution.py:202
  54.4 0.1 collective-permute-done.3.refs_5_
  54.5 5.3 %collective-permute-start.5 = (bf16[2,272,128]{2,1,0:T(8,128)(2,1)S(1)}, bf16[2,272,128]{2,1,0:T(8,128)(2,1)S(1)}, u32[]{:S(2)}, u32[]{:S(2)}) collective-permute-start(bf16[2,272,128]{2,1,0:T(8,128)(2,1)S(1)} %collective-permute-done.3.refs_5_), channel_id=1, source_target_pairs={{0,112},{16,0},{32,16},{48,32},{64,48},{80,64},{96,80},{112,96},{1... | collective-permute-start | bytes 417800 | tf_op jit(solution)/shard_map/ppermute | solution.py:203
  59.8 0.0 collective-permute-done.2.refs_4_
  59.8 1.9 %collective-permute-start.4 = (bf16[2,272,128]{2,1,0:T(8,128)(2,1)S(1)}, bf16[2,272,128]{2,1,0:T(8,128)(2,1)S(1)}, u32[]{:S(2)}, u32[]{:S(2)}) collective-permute-start(bf16[2,272,128]{2,1,0:T(8,128)(2,1)S(1)} %collective-permute-done.2.refs_4_), channel_id=1, source_target_pairs={{0,16},{16,32},{32,48},{48,64},{64,80},{80,96},{96,112},{112,0},{1... | collective-permute-start | bytes 417800 | tf_op jit(solution)/shard_map/ppermute | solution.py:202
  61.7 0.1 collective-permute-done.5.refs_7_
  61.8 5.3 %collective-permute-start.7 = (bf16[1,272,128]{2,1,0:T(8,128)(2,1)S(1)}, bf16[1,272,128]{2,1,0:T(8,128)(2,1)S(1)}, u32[]{:S(2)}, u32[]{:S(2)}) collective-permute-start(bf16[1,272,128]{2,1,0:T(8,128)(2,1)S(1)} %slice.9), channel_id=1, source_target_pairs={{0,112},{16,0},{32,16},{48,32},{64,48},{80,64},{96,80},{112,96},{1... | collective-permute-start | bytes 208904 | tf_op jit(solution)/shard_map/ppermute | solution.py:206
  67.1 0.0 collective-permute-done.4.refs_6_
  67.1 1.9 %collective-permute-start.6 = (bf16[1,272,128]{2,1,0:T(8,128)(2,1)S(1)}, bf16[1,272,128]{2,1,0:T(8,128)(2,1)S(1)}, u32[]{:S(2)}, u32[]{:S(2)}) collective-permute-start(bf16[1,272,128]{2,1,0:T(8,128)(2,1)S(1)} %slice.8), channel_id=1, source_target_pairs={{0,16},{16,32},{32,48},{48,64},{64,80},{80,96},{96,112},{112,0},{1... | collective-permute-start | bytes 208904 | tf_op jit(solution)/shard_map/ppermute | solution.py:205
  69.0 0.0 collective-permute-done.7.refs_9_
  69.1 4.3 %collective-permute-done.6.refs_8_ = bf16[1,272,128]{2,1,0:T(8,128)(2,1)S(1)} collective-permute-done((bf16[1,272,128]{2,1,0:T(8,128)(2,1)S(1)}, bf16[1,272,128]{2,1,0:T(8,128)(2,1)S(1)}, u32[]{:S(2)}, u32[]{:S(2)}) %collective-permute-start.6) | collective-permute-done | bytes 69664 | tf_op jit(solution)/shard_map/ppermute | solution.py:205
  73.4 0.0 all-to-all-done.1
  73.4 0.0 copy-done.3
  73.4 23.3 %attend.1 = bf16[4096,128]{1,0:T(8,128)(2,1)S(1)} custom-call(bf16[4096,128]{1,0:T(8,128)(2,1)S(1)} %bitcast.3, bf16[2,272,128]{2,1,0:T(8,128)(2,1)S(1)} %copy-done.3, bf16[2,272,128]{2,1,0:T(8,128)(2,1)S(1)} %collective-permute-done.refs_2_, bf16[2,272,128]{2,1,0:T(8,128)(2,1)S(1)} %collective-permute-done.1.refs_3_, ...), custom_call_target="tpu_custom_call" | custom-call | flops 4294967296 | bytes 2097152 | tf_op jit(solution)/shard_map/attend/pallas_call | solution.py:143
  96.7 41.3 %all_to_all.15.in_ref = bf16[32,128,128]{2,1,0:T(8,128)(2,1)} all-to-all(bf16[32,128,128]{2,1,0:T(8,128)(2,1)S(1)} %bitcast.4), channel_id=1, replica_groups=mesh['zh'=4,'y'=8,'x'=4,'core'=2,'rep'=2] {'zh','x','core'}, dimensions={0} | all-to-all | bytes 2097152 | tf_op jit(solution)/shard_map/all_to_all | solution.py:208
  138.0 2.5 %unfold.1 = bf16[128,4096]{1,0:T(8,128)(2,1)} custom-call(bf16[32,128,128]{2,1,0:T(8,128)(2,1)} %all_to_all.15.in_ref), custom_call_target="tpu_custom_call" | custom-call | tf_op jit(solution)/shard_map/unfold/pallas_call | solution.py:170
  (3 shorter events, 0.0 us)
Async XLA Ops:
  0.0 1.0 copy-start.4
  0.0 0.9 copy-start.8
  1.0 0.7 copy-start.6
  1.6 1.2 copy-start
  2.9 1.2 copy-start.1
  4.1 16.3 %copy-start.2 = (bf16[128,4096]{1,0:T(8,128)(2,1)S(1)}, bf16[128,4096]{1,0:T(8,128)(2,1)}, u32[]{:S(2)}) copy-start(bf16[128,4096]{1,0:T(8,128)(2,1)} %query_ref.1) | copy-start | bytes 3145732
  5.7 14.6 %copy-start.9 = (s32[128,32]{0,1:T(8,128)S(1)}, s32[128,32]{0,1:T(8,128)}, u32[]{:S(2)}) copy-start(s32[128,32]{0,1:T(8,128)} %param.11) | copy-start | bytes 49156
  5.7 27.1 %all-to-all-start = ((bf16[32,24,128]{2,1,0:T(8,128)(2,1)}), bf16[32,24,128]{2,1,0:T(8,128)(2,1)S(1)}, u32[]{:S(2)}, u32[]{:S(2)}) async-start(bf16[32,24,128]{2,1,0:T(8,128)(2,1)} %prepare_merged.1), calls=%async_computation | async-start | bytes 393216 | tf_op jit(solution)/shard_map/all_to_all | solution.py:195
  20.3 0.8 copy-start.5
  32.9 0.7 copy-start.7
  33.5 39.8 %all-to-all-start.1 = ((bf16[32,128,128]{2,1,0:T(8,128)(2,1)}), bf16[32,128,128]{2,1,0:T(8,128)(2,1)S(1)}, u32[]{:S(2)}, u32[]{:S(2)}) async-start(bf16[32,128,128]{2,1,0:T(8,128)(2,1)} %prepare_queries.1), calls=%async_computation.1 | async-start | bytes 2097152 | tf_op jit(solution)/shard_map/all_to_all | solution.py:197
  39.0 34.4 %copy-start.3 = (bf16[2,272,128]{2,1,0:T(8,128)(2,1)S(1)}, bf16[2,272,128]{2,1,0:T(8,128)(2,1)}, u32[]{:S(2)}) copy-start(bf16[2,272,128]{2,1,0:T(8,128)(2,1)} %repack.1.refs_1_) | copy-start | bytes 417796
  39.0 8.3 %collective-permute-start.1 = (bf16[2,272,128]{2,1,0:T(8,128)(2,1)}, bf16[2,272,128]{2,1,0:T(8,128)(2,1)S(1)}, u32[]{:S(2)}, u32[]{:S(2)}) collective-permute-start(bf16[2,272,128]{2,1,0:T(8,128)(2,1)} %repack.1.refs_1_), channel_id=1, source_target_pairs={{0,112},{16,0},{32,16},{48,32},{64,48},{80,64},{96,80},{112,96},{1... | collective-permute-start | bytes 417800 | tf_op jit(solution)/shard_map/ppermute | solution.py:203
  44.2 8.3 %collective-permute-start = (bf16[2,272,128]{2,1,0:T(8,128)(2,1)}, bf16[2,272,128]{2,1,0:T(8,128)(2,1)S(1)}, u32[]{:S(2)}, u32[]{:S(2)}) collective-permute-start(bf16[2,272,128]{2,1,0:T(8,128)(2,1)} %repack.1.refs_1_), channel_id=1, source_target_pairs={{0,16},{16,32},{32,48},{48,64},{64,80},{80,96},{96,112},{112,0},{1... | collective-permute-start | bytes 417800 | tf_op jit(solution)/shard_map/ppermute | solution.py:202
  47.3 7.2 %collective-permute-start.3 = (bf16[2,272,128]{2,1,0:T(8,128)(2,1)S(1)}, bf16[2,272,128]{2,1,0:T(8,128)(2,1)S(1)}, u32[]{:S(2)}, u32[]{:S(2)}) collective-permute-start(bf16[2,272,128]{2,1,0:T(8,128)(2,1)S(1)} %collective-permute-done.1.refs_3_), channel_id=1, source_target_pairs={{0,112},{16,0},{32,16},{48,32},{64,48},{80,64},{96,80},{112,96},{1... | collective-permute-start | bytes 417800 | tf_op jit(solution)/shard_map/ppermute | solution.py:203
  52.5 7.3 %collective-permute-start.2 = (bf16[2,272,128]{2,1,0:T(8,128)(2,1)S(1)}, bf16[2,272,128]{2,1,0:T(8,128)(2,1)S(1)}, u32[]{:S(2)}, u32[]{:S(2)}) collective-permute-start(bf16[2,272,128]{2,1,0:T(8,128)(2,1)S(1)} %collective-permute-done.refs_2_), channel_id=1, source_target_pairs={{0,16},{16,32},{32,48},{48,64},{64,80},{80,96},{96,112},{112,0},{1... | collective-permute-start | bytes 417800 | tf_op jit(solution)/shard_map/ppermute | solution.py:202
  54.5 7.3 %collective-permute-start.5 = (bf16[2,272,128]{2,1,0:T(8,128)(2,1)S(1)}, bf16[2,272,128]{2,1,0:T(8,128)(2,1)S(1)}, u32[]{:S(2)}, u32[]{:S(2)}) collective-permute-start(bf16[2,272,128]{2,1,0:T(8,128)(2,1)S(1)} %collective-permute-done.3.refs_5_), channel_id=1, source_target_pairs={{0,112},{16,0},{32,16},{48,32},{64,48},{80,64},{96,80},{112,96},{1... | collective-permute-start | bytes 417800 | tf_op jit(solution)/shard_map/ppermute | solution.py:203
  59.8 7.3 %collective-permute-start.4 = (bf16[2,272,128]{2,1,0:T(8,128)(2,1)S(1)}, bf16[2,272,128]{2,1,0:T(8,128)(2,1)S(1)}, u32[]{:S(2)}, u32[]{:S(2)}) collective-permute-start(bf16[2,272,128]{2,1,0:T(8,128)(2,1)S(1)} %collective-permute-done.2.refs_4_), channel_id=1, source_target_pairs={{0,16},{16,32},{32,48},{48,64},{64,80},{80,96},{96,112},{112,0},{1... | collective-permute-start | bytes 417800 | tf_op jit(solution)/shard_map/ppermute | solution.py:202
  61.8 7.2 %collective-permute-start.7 = (bf16[1,272,128]{2,1,0:T(8,128)(2,1)S(1)}, bf16[1,272,128]{2,1,0:T(8,128)(2,1)S(1)}, u32[]{:S(2)}, u32[]{:S(2)}) collective-permute-start(bf16[1,272,128]{2,1,0:T(8,128)(2,1)S(1)} %slice.9), channel_id=1, source_target_pairs={{0,112},{16,0},{32,16},{48,32},{64,48},{80,64},{96,80},{112,96},{1... | collective-permute-start | bytes 208904 | tf_op jit(solution)/shard_map/ppermute | solution.py:206
  67.1 6.3 %collective-permute-start.6 = (bf16[1,272,128]{2,1,0:T(8,128)(2,1)S(1)}, bf16[1,272,128]{2,1,0:T(8,128)(2,1)S(1)}, u32[]{:S(2)}, u32[]{:S(2)}) collective-permute-start(bf16[1,272,128]{2,1,0:T(8,128)(2,1)S(1)} %slice.8), channel_id=1, source_target_pairs={{0,16},{16,32},{32,48},{48,64},{64,80},{80,96},{96,112},{112,0},{1... | collective-permute-start | bytes 208904 | tf_op jit(solution)/shard_map/ppermute | solution.py:205

commit v2 on v1

v2 whole, which is shorter than its diff:
```python
import math

import jax
import jax.numpy as jnp
import numpy as np
from jax import lax
from jax.experimental import pallas as pl
from jax.experimental.pallas import tpu as pltpu
from jax.sharding import Mesh
from jax.sharding import PartitionSpec as P

HD = 128
MERGED = 8
ZH, Y, X, CORE = 4, 8, 4, 2
GROUP = ("zh", "x", "core")
SCALE = 1.0 / math.sqrt(HD)
LOG2E = math.log2(math.e)


def sylvester(size):
    index = np.arange(size)
    both = index[:, None] & index[None, :]
    odd = np.zeros_like(both)
    for bit in range(size.bit_length() - 1):
        odd ^= (both >> bit) & 1
    return (1 - 2 * odd).astype(np.float32)


def prepare_merged_kernel(
    key_ref, value_ref, key_exp_ref, value_exp_ref, map_ref, table_ref, out_ref, sums, key_held, value_held, arrived
):
    tokens, width = key_held.shape
    heads = width // HD
    chunks = arrived.shape[1]
    piece = width // chunks
    slot = lax.broadcasted_iota(jnp.int32, (MERGED, tokens), 0)
    onehot = (map_ref[...] == slot).astype(jnp.float32)
    counts = jnp.sum(onehot, axis=1, keepdims=True)
    count_rows = jnp.broadcast_to(counts, (MERGED, HD)).astype(jnp.bfloat16)
    sides = ((key_ref, key_held, key_exp_ref), (value_ref, value_held, value_exp_ref))

    def copy(side, chunk):
        columns = pl.ds(chunk * piece, piece)
        return pltpu.make_async_copy(
            sides[side][0].at[:, columns], sides[side][1].at[:, columns], arrived.at[side, chunk]
        )

    for side in range(2):
        for chunk in range(chunks):
            copy(side, chunk).start()
    for side in range(2):
        scaling = jnp.exp2(sides[side][2][...].astype(jnp.float32))
        for head in range(heads):
            if head * HD % piece == 0:
                copy(side, head * HD // piece).wait()
            chosen = (onehot * scaling[head : head + 1, :]).astype(jnp.bfloat16)
            sums[pl.ds((side * heads + head) * MERGED, MERGED), :] = jnp.dot(
                chosen, sides[side][1][:, head * HD : (head + 1) * HD], preferred_element_type=jnp.float32
            )
    rotated = jnp.dot(
        sums[...], table_ref[...], precision=lax.Precision.HIGHEST, preferred_element_type=jnp.float32
    ).reshape(2, heads, MERGED, HD)
    merged = (rotated / counts[None, None, :, :] * SCALE).astype(jnp.bfloat16)
    for head in range(heads):
        out_ref[head, 0:MERGED, :] = merged[0, head]
        out_ref[head, MERGED : 2 * MERGED, :] = merged[1, head]
        out_ref[head, 2 * MERGED : 3 * MERGED, :] = count_rows


def prepare_merged(key, value, key_exp, value_exp, merge_map, table, chunks=4):
    heads = key_exp.shape[0]
    whole = pl.BlockSpec(memory_space=pltpu.VMEM)
    return pl.pallas_call(
        prepare_merged_kernel,
        in_specs=[pl.BlockSpec(memory_space=pl.ANY)] * 2 + [whole] * 4,
        out_specs=whole,
        out_shape=jax.ShapeDtypeStruct((heads, 3 * MERGED, HD), jnp.bfloat16),
        scratch_shapes=[
            pltpu.VMEM((2 * heads * MERGED, HD), jnp.float32),
            pltpu.VMEM(key.shape, jnp.bfloat16),
            pltpu.VMEM(value.shape, jnp.bfloat16),
            pltpu.SemaphoreType.DMA((2, chunks)),
        ],
        compiler_params=pltpu.CompilerParams(vmem_limit_bytes=56 * 2**20),
        cost_estimate=pl.CostEstimate(flops=2**27, bytes_accessed=2**21, transcendentals=0),
        name="prepare_merged",
    )(key, value, key_exp, value_exp, merge_map.reshape(1, -1), table)


def prepare_queries_kernel(query_ref, exp_ref, table_ref, out_ref):
    heads = exp_ref.shape[0]
    scaling = (jnp.exp2(exp_ref[...].astype(jnp.float32)) * SCALE).T
    for head in range(heads):
        rotated = jnp.dot(
            query_ref[:, head * HD : (head + 1) * HD], table_ref[...], preferred_element_type=jnp.float32
        )
        out_ref[head] = (rotated * scaling[:, head : head + 1]).astype(jnp.bfloat16)


def prepare_queries(query, query_exp, table):
    tokens = query.shape[0]
    heads = query_exp.shape[0]
    return pl.pallas_call(
        prepare_queries_kernel,
        out_shape=jax.ShapeDtypeStruct((heads, tokens, HD), jnp.bfloat16),
        compiler_params=pltpu.CompilerParams(vmem_limit_bytes=16 * 2**20),
        cost_estimate=pl.CostEstimate(flops=2**27, bytes_accessed=2**21, transcendentals=0),
        name="prepare_queries",
    )(query, query_exp, table)


def repack_kernel(in_ref, out_ref):
    rows = in_ref.shape[0] * MERGED
    out_ref[0, 0:rows, :] = in_ref[:, 0:MERGED, :].reshape(rows, HD)
    out_ref[0, rows : 2 * rows, :] = in_ref[:, MERGED : 2 * MERGED, :].reshape(rows, HD)
    spread = in_ref[:, 2 * MERGED : 3 * MERGED, :].reshape(rows, HD)
    ones = jnp.full((8, HD), 1.0 / HD, jnp.bfloat16)
    counts = lax.dot_general(ones, spread, (((1,), (1,)), ((), ())), preferred_element_type=jnp.float32)
    out_ref[0, 2 * rows :, :] = jnp.concatenate(
        [counts[:, part * HD : (part + 1) * HD] for part in range(rows // HD)], axis=0
    ).astype(jnp.bfloat16)


def repack(received):
    rows = received.shape[0] * MERGED
    return pl.pallas_call(
        repack_kernel,
        out_shape=jax.ShapeDtypeStruct((1, 2 * rows + 8 * (rows // HD), HD), jnp.bfloat16),
        cost_estimate=pl.CostEstimate(flops=2**20, bytes_accessed=2**18, transcendentals=0),
        name="repack",
    )(received)


def attend_kernel(parts, sub, *refs):
    query_ref = refs[0]
    piece_refs = refs[1 : 1 + parts]
    out_ref, keys, values, logs = refs[1 + parts :]

    @pl.when(pl.program_id(0) == 0)
    def _():
        place = 0
        rows = 2 * HD
        for piece_ref in piece_refs:
            for block in range(piece_ref.shape[0]):
                keys[place : place + rows, :] = piece_ref[block, 0:rows, :]
                values[place : place + rows, 0:HD] = piece_ref[block, rows : 2 * rows, :]
                counts = piece_ref[block, 2 * rows : 2 * rows + 16, :].astype(jnp.float32)
                logs[:, place : place + HD] = jnp.log(counts[0:8]) * LOG2E
                logs[:, place + HD : place + rows] = jnp.log(counts[8:16]) * LOG2E
                place += rows
        values[:, HD:] = jnp.ones((place, HD), jnp.bfloat16)

    for start in range(0, query_ref.shape[0], sub):
        scores = lax.dot_general(
            query_ref[start : start + sub, :],
            keys[...],
            (((1,), (1,)), ((), ())),
            preferred_element_type=jnp.float32,
        )
        scores = scores * (SCALE * LOG2E) + logs[0:1, :]
        weights = jnp.exp2(scores - jnp.max(scores, axis=1, keepdims=True)).astype(jnp.bfloat16)
        mixed = jnp.dot(weights, values[...], preferred_element_type=jnp.float32)
        out_ref[start : start + sub, :] = (mixed[:, 0:HD] / mixed[:, HD:]).astype(jnp.bfloat16)


def attend(queries, pieces, slots, block=2048, sub=256):
    rows = queries.shape[0]
    parts = len(pieces)
    return pl.pallas_call(
        lambda *refs: attend_kernel(parts, sub, *refs),
        grid=(rows // block,),
        in_specs=[pl.BlockSpec((block, HD), lambda i: (i, 0))]
        + [pl.BlockSpec(piece.shape, lambda i: (0, 0, 0)) for piece in pieces],
        out_specs=pl.BlockSpec((block, HD), lambda i: (i, 0)),
        out_shape=jax.ShapeDtypeStruct((rows, HD), jnp.bfloat16),
        scratch_shapes=[
            pltpu.VMEM((slots, HD), jnp.bfloat16),
            pltpu.VMEM((slots, 2 * HD), jnp.bfloat16),
            pltpu.VMEM((8, slots), jnp.float32),
        ],
        compiler_params=pltpu.CompilerParams(vmem_limit_bytes=56 * 2**20),
        cost_estimate=pl.CostEstimate(
            flops=4 * rows * slots * HD, bytes_accessed=4 * rows * HD, transcendentals=rows * slots
        ),
        name="attend",
    )(queries, *pieces)


def unfold_kernel(in_ref, out_ref):
    for head in range(in_ref.shape[0]):
        out_ref[:, head * HD : (head + 1) * HD] = in_ref[head]


def unfold(attended, steps=4):
    heads, tokens, _ = attended.shape
    group = heads // steps
    return pl.pallas_call(
        unfold_kernel,
        grid=(steps,),
        in_specs=[pl.BlockSpec((group, tokens, HD), lambda i: (i, 0, 0))],
        out_specs=pl.BlockSpec((tokens, group * HD), lambda i: (0, i)),
        out_shape=jax.ShapeDtypeStruct((tokens, heads * HD), jnp.bfloat16),
        name="unfold",
    )(attended)


def shifted(size, by):
    return [(index, (index + by) % size) for index in range(size)]


def per_device(
    query_mantissa,
    key_mantissa,
    value_mantissa,
    query_exponent,
    key_exponent,
    value_exponent,
    merge_map,
):
    tokens = query_mantissa.shape[0]
    heads = query_exponent.shape[1]
    table = jnp.asarray(sylvester(HD))
    merged = prepare_merged(key_mantissa, value_mantissa, key_exponent.T, value_exponent.T, merge_map, table)
    merged, query_mantissa = lax.optimization_barrier((merged, query_mantissa))
    queries = prepare_queries(query_mantissa, query_exponent.T, table.astype(jnp.bfloat16))
    received = lax.all_to_all(merged, GROUP, split_axis=0, concat_axis=0, tiled=True)
    head_queries = lax.all_to_all(queries, GROUP, split_axis=0, concat_axis=0, tiled=True)
    same = lax.all_gather(repack(received), "yA", axis=0, tiled=True)
    up = lax.ppermute(same[0:2], ("yA", "yB"), shifted(Y, 1))
    down = lax.ppermute(same[2:4], ("yA", "yB"), shifted(Y, -1))
    attended = attend(head_queries.reshape(heads * tokens, HD), (same, up, down), Y * heads * MERGED)
    returned = lax.all_to_all(attended.reshape(heads, tokens, HD), GROUP, split_axis=0, concat_axis=0, tiled=True)
    return unfold(returned)


def solution(mesh):
    fine = Mesh(mesh.devices.reshape(ZH, Y // 2, 2, X, CORE, 2), ("zh", "yA", "yB", "x", "core", "rep"))
    tokens = P(("rep", "zh", "yA", "yB", "x", "core"), None)
    return jax.shard_map(
        per_device,
        mesh=fine,
        in_specs=(tokens,) * 6 + (P(("rep", "zh", "yA", "yB", "x", "core")),),
        out_specs=tokens,
        check_vma=False,
    )
```

time: 141 us -> 128 us (0.908)
  starting transfers between devices: 46.9 us -> 24.6 us
  blocking collectives: 41.3 us -> 60.4 us
  Pallas kernels: 30.9 us -> 25.5 us
  local copies, waits for them, and re-layouts: 5.48 us -> 2.58 us
  waiting for transfers between devices: 15.8 us -> 14.1 us
    ppermute x8 -> x2, starting transfers between devices: 28.6 us -> 6.48 us  [the longest x1 4.57 us: per_device(): down = lax.ppermute(same[2:4], ('yA', 'yB'), shifted(Y, -1))]
    all_gather x0 -> x1, blocking collectives: none -> 17.8 us  [per_device(): same = lax.all_gather(repack(received), 'yA', axis=0, tiled=True)]
    pallas_call x4, Pallas kernels: 29.2 us -> 23.7 us  [the longest x1 14.1 us: attend(): pl.pallas_call(lambda *refs: attend_kernel(parts, sub, *refs), grid=(rows...]
    unnamed x23 -> x16, local copies, waits for them, and re-layouts: 5.47 us -> 2.55 us
    ppermute x8 -> x2, waiting for transfers between devices: 5.63 us -> 3.38 us  [the longest x1 1.91 us: per_device(): up = lax.ppermute(same[0:2], ('yA', 'yB'), shifted(Y, 1))]
  transfers between devices with their start and end apart: 10 -> 4, of which waited for: 5 -> 3; matrix products, arithmetic and copies ran while one was open for 0% -> 0% of each run, Pallas kernels for 2% -> 3%
where the time goes in v2:
time: 128 us; the launch traced here: 127 us
  blocking collectives  60.4 us (47%)
  Pallas kernels  25.5 us (20%)
  starting transfers between devices  24.6 us (19%)
  waiting for transfers between devices  14.1 us (11%)
  local copies, waits for them, and re-layouts  2.58 us (2%)
    all_to_all x1, blocking collectives, per_device(): lax.all_to_all(attended.reshape(heads, tokens, HD), GROUP, split_axis=0,...  42.6 us
    all_gather x1, blocking collectives, per_device(): same = lax.all_gather(repack(received), 'yA', axis=0, tiled=True)  17.8 us
    all_to_all x1, starting transfers between devices, per_device(): lax.all_to_all(merged, GROUP, split_axis=0, concat_axis=0, tiled=True)  14.4 us
    pallas_call x1, Pallas kernels, attend(): pl.pallas_call(lambda *refs: attend_kernel(parts, sub, *refs), grid=(rows...  14.1 us
    all_to_all x1, waiting for transfers between devices, per_device(): lax.all_to_all(merged, GROUP, split_axis=0, concat_axis=0, tiled=True)  10.7 us
    ppermute x1, starting transfers between devices, per_device(): down = lax.ppermute(same[2:4], ('yA', 'yB'), shifted(Y, -1))  4.57 us
    pallas_call x1, Pallas kernels, prepare_merged(): pl.pallas_call(prepare_merged_kernel, in_specs=[pl.BlockSpec(memory_space...  4.43 us
    all_to_all x1, starting transfers between devices, per_device(): lax.all_to_all(queries, GROUP, split_axis=0, concat_axis=0, tiled=True)  3.72 us
  transfers between devices with their start and end apart: 4, of which 3 were waited for; matrix products, arithmetic and copies ran while one was open for 0% of the time, Pallas kernels for 3%

profile of v2, /device:TPU:1, one launch (start us, length us, event | category | flops | bytes accessed | tf_op | source)
XLA Modules:
  0.0 127.4 jit_solution(10539897301899335436)
XLA Ops:
  0.0 0.0 copy-start
  0.0 4.4 %prepare_merged.1 = bf16[32,24,128]{2,1,0:T(8,128)(2,1)} custom-call(bf16[128,4096]{1,0:T(8,128)(2,1)} %key_ref.1, bf16[128,4096]{1,0:T(8,128)(2,1)} %value_ref.1, s32[32,128]{1,0:T(8,128)} %bitcast.9, s32[32,128]{1,0:T(8,128)} %bitcast.10, s32[1,128]{1,0:T(1,128)} %bitcast.11, f32[128,128]{1,0:T(8,128)} %constant.2.clone.table_ref), custom_call_target="tpu_custom_call" | custom-call | flops 134217728 | bytes 2097152 | tf_op jit(solution)/shard_map/prepare_merged/pallas_call | solution.py:73
  4.4 0.0 copy-start.1
  4.4 0.0 copy-start.2
  4.5 14.4 %all-to-all-start.1 = ((bf16[32,24,128]{2,1,0:T(8,128)(2,1)}), bf16[32,24,128]{2,1,0:T(8,128)(2,1)S(1)}, u32[]{:S(2)}, u32[]{:S(2)}) async-start(bf16[32,24,128]{2,1,0:T(8,128)(2,1)} %prepare_merged.1), calls=%async_computation.1 | async-start | bytes 393216 | tf_op jit(solution)/shard_map/all_to_all | solution.py:226
  18.9 0.0 copy-done
  18.9 0.0 copy-done.1
  18.9 0.0 copy-done.2
  18.9 1.8 %prepare_queries.1 = bf16[32,128,128]{2,1,0:T(8,128)(2,1)} custom-call(bf16[128,4096]{1,0:T(8,128)(2,1)S(1)} %copy-done, s32[32,128]{1,0:T(8,128)S(1)} %bitcast.6, bf16[128,128]{1,0:T(8,128)(2,1)S(1)} %copy-done.1), custom_call_target="tpu_custom_call" | custom-call | flops 134217728 | bytes 2097152 | tf_op jit(solution)/shard_map/prepare_queries/pallas_call | solution.py:103
  20.7 10.7 %all-to-all-done.1.in_ref = bf16[32,24,128]{2,1,0:T(8,128)(2,1)S(1)} async-done(((bf16[32,24,128]{2,1,0:T(8,128)(2,1)}), bf16[32,24,128]{2,1,0:T(8,128)(2,1)S(1)}, u32[]{:S(2)}, u32[]{:S(2)}) %all-to-all-start.1) | async-done | bytes 196640 | tf_op jit(solution)/shard_map/all_to_all | solution.py:226
  31.5 0.0 copy-start.5
  31.5 0.7 copy-done.5
  32.2 3.7 %all-to-all-start = ((bf16[32,128,128]{2,1,0:T(8,128)(2,1)}), bf16[32,128,128]{2,1,0:T(8,128)(2,1)S(1)}, u32[]{:S(2)}, u32[]{:S(2)}) async-start(bf16[32,128,128]{2,1,0:T(8,128)(2,1)} %prepare_queries.1), calls=%async_computation | async-start | bytes 2097152 | tf_op jit(solution)/shard_map/all_to_all | solution.py:227
  35.9 1.7 %repack.1 = bf16[1,528,128]{2,1,0:T(8,128)(2,1)} custom-call(bf16[32,24,128]{2,1,0:T(8,128)(2,1)} %copy-done.5), custom_call_target="tpu_custom_call" | custom-call | flops 1048576 | bytes 262144 | tf_op jit(solution)/shard_map/repack/pallas_call | solution.py:126
  37.6 17.8 %all_gather.3.refs_1_ = bf16[4,528,128]{2,1,0:T(8,128)(2,1)S(1)} all-gather(bf16[1,528,128]{2,1,0:T(8,128)(2,1)} %repack.1), channel_id=1, replica_groups=mesh['zh'=4,'yA'=4,'yB'=2,'x'=4,'core'=2,'rep'=2] {'yA'}, dimensions={0}, use_global_device_ids=true | all-gather | bytes 675840 | tf_op jit(solution)/shard_map/all_gather | solution.py:228
  55.4 0.0 copy-start.3
  55.5 0.8 copy-done.3
  56.3 1.9 %collective-permute-start = (bf16[2,528,128]{2,1,0:T(8,128)(2,1)S(1)}, bf16[2,528,128]{2,1,0:T(8,128)(2,1)S(1)}, u32[]{:S(2)}, u32[]{:S(2)}) collective-permute-start(bf16[2,528,128]{2,1,0:T(8,128)(2,1)S(1)} %get-tuple-element.10), channel_id=1, source_target_pairs={{0,16},{16,32},{32,48},{48,64},{64,80},{80,96},{96,112},{112,0},{1... | collective-permute-start | bytes 811016 | tf_op jit(solution)/shard_map/ppermute | solution.py:229
  58.2 4.6 %collective-permute-start.1 = (bf16[2,528,128]{2,1,0:T(8,128)(2,1)S(1)}, bf16[2,528,128]{2,1,0:T(8,128)(2,1)S(1)}, u32[]{:S(2)}, u32[]{:S(2)}) collective-permute-start(bf16[2,528,128]{2,1,0:T(8,128)(2,1)S(1)} %get-tuple-element.9), channel_id=1, source_target_pairs={{0,112},{16,0},{32,16},{48,32},{64,48},{80,64},{96,80},{112,96},{1... | collective-permute-start | bytes 811016 | tf_op jit(solution)/shard_map/ppermute | solution.py:230
  62.8 1.9 %collective-permute-done.refs_2_ = bf16[2,528,128]{2,1,0:T(8,128)(2,1)S(1)} collective-permute-done((bf16[2,528,128]{2,1,0:T(8,128)(2,1)S(1)}, bf16[2,528,128]{2,1,0:T(8,128)(2,1)S(1)}, u32[]{:S(2)}, u32[]{:S(2)}) %collective-permute-start) | collective-permute-done | bytes 270368 | tf_op jit(solution)/shard_map/ppermute | solution.py:229
  64.7 0.0 copy-start.6
  64.7 1.5 %collective-permute-done.1.refs_3_ = bf16[2,528,128]{2,1,0:T(8,128)(2,1)S(1)} collective-permute-done((bf16[2,528,128]{2,1,0:T(8,128)(2,1)S(1)}, bf16[2,528,128]{2,1,0:T(8,128)(2,1)S(1)}, u32[]{:S(2)}, u32[]{:S(2)}) %collective-permute-start.1) | collective-permute-done | bytes 270368 | tf_op jit(solution)/shard_map/ppermute | solution.py:230
  66.2 0.0 copy-start.7
  66.2 0.0 all-to-all-done
  66.2 0.0 copy-start.4
  66.2 0.0 copy-done.6
  66.2 0.7 copy-done.7
  66.9 0.3 copy-done.4
  67.2 14.1 %attend.1 = bf16[4096,128]{1,0:T(8,128)(2,1)} custom-call(bf16[4096,128]{1,0:T(8,128)(2,1)} %bitcast.7, bf16[4,528,128]{2,1,0:T(8,128)(2,1)} %copy-done.3, bf16[2,528,128]{2,1,0:T(8,128)(2,1)} %copy-done.6, bf16[2,528,128]{2,1,0:T(8,128)(2,1)} %copy-done.7), custom_call_target="tpu_custom_call" | custom-call | flops 4294967296 | bytes 2097152 | tf_op jit(solution)/shard_map/attend/pallas_call | solution.py:169
  81.3 42.6 %all_to_all.15.in_ref = bf16[32,128,128]{2,1,0:T(8,128)(2,1)} all-to-all(bf16[32,128,128]{2,1,0:T(8,128)(2,1)} %bitcast.8), channel_id=1, replica_groups=mesh['zh'=4,'yA'=4,'yB'=2,'x'=4,'core'=2,'rep'=2] {'zh','x','core'}, dimensions={0} | all-to-all | bytes 2097152 | tf_op jit(solution)/shard_map/all_to_all | solution.py:232
  123.9 3.5 %unfold.1 = bf16[128,4096]{1,0:T(8,128)(2,1)} custom-call(bf16[32,128,128]{2,1,0:T(8,128)(2,1)} %all_to_all.15.in_ref), custom_call_target="tpu_custom_call" | custom-call | tf_op jit(solution)/shard_map/unfold/pallas_call | solution.py:197
  (1 shorter events, 0.0 us)
Async XLA Ops:
  0.0 18.9 %copy-start = (bf16[128,4096]{1,0:T(8,128)(2,1)S(1)}, bf16[128,4096]{1,0:T(8,128)(2,1)}, u32[]{:S(2)}) copy-start(bf16[128,4096]{1,0:T(8,128)(2,1)} %query_ref) | copy-start | bytes 3145732
  4.4 14.5 %copy-start.1 = (bf16[128,128]{1,0:T(8,128)(2,1)S(1)}, bf16[128,128]{1,0:T(8,128)(2,1)}, u32[]{:S(2)}) copy-start(bf16[128,128]{1,0:T(8,128)(2,1)} %constant.10.table_ref) | copy-start | bytes 98308
  4.4 14.5 %copy-start.2 = (s32[128,32]{0,1:T(8,128)S(1)}, s32[128,32]{0,1:T(8,128)}, u32[]{:S(2)}) copy-start(s32[128,32]{0,1:T(8,128)} %param.11) | copy-start | bytes 49156
  4.5 27.0 %all-to-all-start.1 = ((bf16[32,24,128]{2,1,0:T(8,128)(2,1)}), bf16[32,24,128]{2,1,0:T(8,128)(2,1)S(1)}, u32[]{:S(2)}, u32[]{:S(2)}) async-start(bf16[32,24,128]{2,1,0:T(8,128)(2,1)} %prepare_merged.1), calls=%async_computation.1 | async-start | bytes 393216 | tf_op jit(solution)/shard_map/all_to_all | solution.py:226
  31.5 0.7 copy-start.5
  32.2 34.0 %all-to-all-start = ((bf16[32,128,128]{2,1,0:T(8,128)(2,1)}), bf16[32,128,128]{2,1,0:T(8,128)(2,1)S(1)}, u32[]{:S(2)}, u32[]{:S(2)}) async-start(bf16[32,128,128]{2,1,0:T(8,128)(2,1)} %prepare_queries.1), calls=%async_computation | async-start | bytes 2097152 | tf_op jit(solution)/shard_map/all_to_all | solution.py:227
  55.4 0.8 copy-start.3
  56.3 8.4 %collective-permute-start = (bf16[2,528,128]{2,1,0:T(8,128)(2,1)S(1)}, bf16[2,528,128]{2,1,0:T(8,128)(2,1)S(1)}, u32[]{:S(2)}, u32[]{:S(2)}) collective-permute-start(bf16[2,528,128]{2,1,0:T(8,128)(2,1)S(1)} %get-tuple-element.10), channel_id=1, source_target_pairs={{0,16},{16,32},{32,48},{48,64},{64,80},{80,96},{96,112},{112,0},{1... | collective-permute-start | bytes 811016 | tf_op jit(solution)/shard_map/ppermute | solution.py:229
  58.2 8.0 %collective-permute-start.1 = (bf16[2,528,128]{2,1,0:T(8,128)(2,1)S(1)}, bf16[2,528,128]{2,1,0:T(8,128)(2,1)S(1)}, u32[]{:S(2)}, u32[]{:S(2)}) collective-permute-start(bf16[2,528,128]{2,1,0:T(8,128)(2,1)S(1)} %get-tuple-element.9), channel_id=1, source_target_pairs={{0,112},{16,0},{32,16},{48,32},{64,48},{80,64},{96,80},{112,96},{1... | collective-permute-start | bytes 811016 | tf_op jit(solution)/shard_map/ppermute | solution.py:230
  64.7 1.5 %copy-start.6 = (bf16[2,528,128]{2,1,0:T(8,128)(2,1)}, bf16[2,528,128]{2,1,0:T(8,128)(2,1)S(1)}, u32[]{:S(2)}) copy-start(bf16[2,528,128]{2,1,0:T(8,128)(2,1)S(1)} %collective-permute-done.refs_2_) | copy-start | bytes 811012
  66.2 0.7 copy-start.7
  66.2 1.1 copy-start.4

commit v3 on v2

v3 whole, which is shorter than its diff:
```python
import math

import jax
import jax.numpy as jnp
import numpy as np
from jax import lax
from jax.experimental import pallas as pl
from jax.experimental.pallas import tpu as pltpu
from jax.sharding import Mesh
from jax.sharding import PartitionSpec as P

HD = 128
MERGED = 8
ZH, Y, X, CORE = 4, 8, 4, 2
GROUP = ("yB", "x", "core")
RING = ("zh", "yA", "core")
SCALE = 1.0 / math.sqrt(HD)
LOG2E = math.log2(math.e)


def sylvester(size):
    index = np.arange(size)
    both = index[:, None] & index[None, :]
    odd = np.zeros_like(both)
    for bit in range(size.bit_length() - 1):
        odd ^= (both >> bit) & 1
    return (1 - 2 * odd).astype(np.float32)


def prepare_merged_kernel(
    key_ref, value_ref, key_exp_ref, value_exp_ref, map_ref, table_ref, out_ref, sums, key_held, value_held, arrived
):
    tokens, width = key_held.shape
    heads = width // HD
    chunks = arrived.shape[1]
    piece = width // chunks
    slot = lax.broadcasted_iota(jnp.int32, (MERGED, tokens), 0)
    onehot = (map_ref[...] == slot).astype(jnp.float32)
    counts = jnp.sum(onehot, axis=1, keepdims=True)
    count_rows = jnp.broadcast_to(counts, (MERGED, HD)).astype(jnp.bfloat16)
    sides = ((key_ref, key_held, key_exp_ref), (value_ref, value_held, value_exp_ref))

    def copy(side, chunk):
        columns = pl.ds(chunk * piece, piece)
        return pltpu.make_async_copy(
            sides[side][0].at[:, columns], sides[side][1].at[:, columns], arrived.at[side, chunk]
        )

    for side in range(2):
        for chunk in range(chunks):
            copy(side, chunk).start()
    for side in range(2):
        scaling = jnp.exp2(sides[side][2][...].astype(jnp.float32))
        for head in range(heads):
            if head * HD % piece == 0:
                copy(side, head * HD // piece).wait()
            chosen = (onehot * scaling[head : head + 1, :]).astype(jnp.bfloat16)
            sums[pl.ds((side * heads + head) * MERGED, MERGED), :] = jnp.dot(
                chosen, sides[side][1][:, head * HD : (head + 1) * HD], preferred_element_type=jnp.float32
            )
    rotated = jnp.dot(
        sums[...], table_ref[...], precision=lax.Precision.HIGHEST, preferred_element_type=jnp.float32
    ).reshape(2, heads, MERGED, HD)
    merged = (rotated / counts[None, None, :, :] * SCALE).astype(jnp.bfloat16)
    pair = out_ref.shape[1] // (2 * MERGED)
    for head in range(heads):
        target, place = head // pair, head % pair * 2 * MERGED
        out_ref[target, place : place + MERGED, :] = merged[0, head]
        out_ref[target, place + MERGED : place + 2 * MERGED, :] = merged[1, head]
    for target in range(heads // pair):
        out_ref[target, pair * 2 * MERGED :, :] = count_rows


def prepare_merged(key, value, key_exp, value_exp, merge_map, table, targets, chunks=4):
    heads = key_exp.shape[0]
    rows = heads // targets * 2 * MERGED + MERGED
    whole = pl.BlockSpec(memory_space=pltpu.VMEM)
    return pl.pallas_call(
        prepare_merged_kernel,
        in_specs=[pl.BlockSpec(memory_space=pl.ANY)] * 2 + [whole] * 4,
        out_specs=whole,
        out_shape=jax.ShapeDtypeStruct((targets, rows, HD), jnp.bfloat16),
        scratch_shapes=[
            pltpu.VMEM((2 * heads * MERGED, HD), jnp.float32),
            pltpu.VMEM(key.shape, jnp.bfloat16),
            pltpu.VMEM(value.shape, jnp.bfloat16),
            pltpu.SemaphoreType.DMA((2, chunks)),
        ],
        compiler_params=pltpu.CompilerParams(vmem_limit_bytes=56 * 2**20),
        cost_estimate=pl.CostEstimate(flops=2**27, bytes_accessed=2**21, transcendentals=0),
        name="prepare_merged",
    )(key, value, key_exp, value_exp, merge_map.reshape(1, -1), table)


def prepare_queries_kernel(query_ref, exp_ref, table_ref, out_ref):
    heads = exp_ref.shape[0]
    scaling = (jnp.exp2(exp_ref[...].astype(jnp.float32)) * SCALE).T
    for head in range(heads):
        rotated = jnp.dot(
            query_ref[:, head * HD : (head + 1) * HD], table_ref[...], preferred_element_type=jnp.float32
        )
        out_ref[head] = (rotated * scaling[:, head : head + 1]).astype(jnp.bfloat16)


def prepare_queries(query, query_exp, table):
    tokens = query.shape[0]
    heads = query_exp.shape[0]
    return pl.pallas_call(
        prepare_queries_kernel,
        out_shape=jax.ShapeDtypeStruct((heads, tokens, HD), jnp.bfloat16),
        compiler_params=pltpu.CompilerParams(vmem_limit_bytes=16 * 2**20),
        cost_estimate=pl.CostEstimate(flops=2**27, bytes_accessed=2**21, transcendentals=0),
        name="prepare_queries",
    )(query, query_exp, table)


def repack_kernel(in_ref, out_ref):
    sources, height, _ = in_ref.shape
    rows = sources * MERGED
    for kind in range(height // MERGED - 1):
        out_ref[0, kind * rows : (kind + 1) * rows, :] = in_ref[
            :, kind * MERGED : (kind + 1) * MERGED, :
        ].reshape(rows, HD)
    spread = in_ref[:, height - MERGED :, :].reshape(rows, HD)
    ones = jnp.full((16, HD), 1.0 / HD, jnp.bfloat16)
    counts = lax.dot_general(ones, spread, (((1,), (1,)), ((), ())), preferred_element_type=jnp.float32)
    out_ref[0, (height // MERGED - 1) * rows :, :] = counts.astype(jnp.bfloat16)


def repack(received):
    sources, height, _ = received.shape
    rows = sources * MERGED
    return pl.pallas_call(
        repack_kernel,
        out_shape=jax.ShapeDtypeStruct((1, (height // MERGED - 1) * rows + 16, HD), jnp.bfloat16),
        cost_estimate=pl.CostEstimate(flops=2**20, bytes_accessed=2**18, transcendentals=0),
        name="repack",
    )(received)


def attend_kernel(parts, first, last, sub, *refs):
    query_ref = refs[0]
    piece_refs = refs[1 : 1 + parts]
    refs = refs[1 + parts :]
    if not first:
        mixed_ref, aside_ref = refs[:2]
        refs = refs[2:]
    out_refs = refs[: 1 if last else 2]
    keys, values, logs = refs[1 if last else 2 :]
    tokens = query_ref.shape[1]
    step = sub // tokens

    @pl.when(pl.program_id(1) == 0)
    def _():
        base = pl.multiple_of(pl.program_id(0) * 2 * HD, 2 * HD)
        place = 0
        for piece_ref in piece_refs:
            for block in range(piece_ref.shape[0]):
                keys[place : place + HD, :] = piece_ref[block, pl.ds(base, HD), :]
                values[place : place + HD, 0:HD] = piece_ref[block, pl.ds(base + HD, HD), :]
                counts = piece_ref[block, 4 * HD : 4 * HD + 16, :].astype(jnp.float32)
                logs[:, place : place + HD] = jnp.log(counts[0:8]) * LOG2E
                place += HD
        values[:, HD:] = jnp.ones((place, HD), jnp.bfloat16)

    lower = lax.broadcasted_iota(jnp.int32, (sub, HD), 1) < HD // 2
    for index in range(query_ref.shape[0] // step):
        rows = slice(index * sub, (index + 1) * sub)
        scores = lax.dot_general(
            query_ref[index * step : (index + 1) * step].reshape(sub, HD),
            keys[...],
            (((1,), (1,)), ((), ())),
            preferred_element_type=jnp.float32,
        )
        scores = scores * (SCALE * LOG2E) + logs[0:1, :]
        top = jnp.max(scores, axis=1, keepdims=True)
        if not first:
            before = aside_ref[rows, 0:1]
            top = jnp.maximum(top, before)
        weights = jnp.exp2(scores - top).astype(jnp.bfloat16)
        both = jnp.dot(weights, values[...], preferred_element_type=jnp.float32)
        mixed = both[:, 0:HD]
        denominator = both[:, HD:]
        if not first:
            rescale = jnp.exp2(before - top)
            mixed = mixed + mixed_ref[rows, :] * rescale
            denominator = denominator + aside_ref[rows, HD - 1 : HD] * rescale
        if last:
            done = (mixed / denominator).astype(jnp.bfloat16)
            out_refs[0][index * step : (index + 1) * step] = done.reshape(step, tokens, HD)
        else:
            out_refs[0][rows, :] = mixed
            out_refs[1][rows, :] = jnp.where(lower, top, denominator)


def attend(queries, pieces, state, last, sub=256, cuts=2):
    sources, pair, tokens, _ = queries.shape
    rows = sources * tokens // cuts
    parts = len(pieces)
    slots = HD * sum(piece.shape[0] for piece in pieces)
    first = state is None
    by_head = pl.BlockSpec((sources // cuts, None, tokens, HD), lambda head, cut: (cut, head, 0, 0))
    state_specs = [pl.BlockSpec((None, rows, HD), lambda head, cut: (head, cut, 0))] * 2
    if last:
        out_specs = by_head
        out_shape = jax.ShapeDtypeStruct(queries.shape, jnp.bfloat16)
    else:
        out_specs = state_specs
        out_shape = [jax.ShapeDtypeStruct((pair, sources * tokens, HD), jnp.float32)] * 2
    return pl.pallas_call(
        lambda *refs: attend_kernel(parts, first, last, sub, *refs),
        grid=(pair, cuts),
        in_specs=[by_head]
        + [pl.BlockSpec(piece.shape, lambda head, cut: (0, 0, 0)) for piece in pieces]
        + ([] if first else state_specs),
        out_specs=out_specs,
        out_shape=out_shape,
        scratch_shapes=[
            pltpu.VMEM((slots, HD), jnp.bfloat16),
            pltpu.VMEM((slots, 2 * HD), jnp.bfloat16),
            pltpu.VMEM((8, slots), jnp.float32),
        ],
        compiler_params=pltpu.CompilerParams(vmem_limit_bytes=24 * 2**20),
        cost_estimate=pl.CostEstimate(
            flops=8 * pair * cuts * rows * slots * HD,
            bytes_accessed=16 * pair * cuts * rows * HD,
            transcendentals=pair * cuts * rows * slots,
        ),
        name="attend",
    )(queries, *pieces, *(() if first else state))


def place(zh, ya, core):
    return (zh % ZH * (Y // 2) + ya % (Y // 2)) * CORE + core


def first_groups():
    over_z = [[place(zh, ya, 0) for zh in range(ZH)] for ya in range(Y // 2)]
    over_y = [[place(zh, ya, 1) for ya in range(Y // 2)] for zh in range(ZH)]
    return over_z + over_y


def second_ring(by):
    pairs = []
    for zh in range(ZH):
        for ya in range(Y // 2):
            pairs.append((place(zh, ya, 0), place(zh, ya + by, 0)))
            pairs.append((place(zh, ya, 1), place(zh + by, ya, 1)))
    return pairs


def per_device(
    query_mantissa,
    key_mantissa,
    value_mantissa,
    query_exponent,
    key_exponent,
    value_exponent,
    merge_map,
):
    tokens = query_mantissa.shape[0]
    heads = query_exponent.shape[1]
    table = jnp.asarray(sylvester(HD))
    targets = lax.axis_size(GROUP)
    merged = prepare_merged(
        key_mantissa, value_mantissa, key_exponent.T, value_exponent.T, merge_map, table, targets
    )
    queries = prepare_queries(query_mantissa, query_exponent.T, table.astype(jnp.bfloat16))
    received = lax.all_to_all(merged, GROUP, split_axis=0, concat_axis=0, tiled=True)
    head_queries = lax.all_to_all(queries, GROUP, split_axis=0, concat_axis=0, tiled=True)
    head_queries = head_queries.reshape(targets, heads // targets, tokens, HD)
    near = lax.all_gather(repack(received), RING, axis=0, tiled=True, axis_index_groups=first_groups())
    up = lax.ppermute(near, RING, second_ring(1))
    down = lax.ppermute(near, RING, second_ring(-1))
    state = attend(head_queries, (near,), None, False)
    up, down, state = lax.optimization_barrier((up, down, state))
    far_up = lax.ppermute(up[0:2], RING, second_ring(1))
    far_down = lax.ppermute(down[2:4], RING, second_ring(-1))
    state = attend(head_queries, (up, down), state, False)
    attended = attend(head_queries, (far_up, far_down), state, True)
    returned = lax.all_to_all(
        attended.reshape(heads, tokens, HD), GROUP, split_axis=0, concat_axis=0, tiled=True
    )
    return jnp.transpose(returned, (1, 0, 2)).reshape(tokens, heads * HD)


def solution(mesh):
    fine = Mesh(mesh.devices.reshape(ZH, Y // 2, 2, X, CORE, 2), ("zh", "yA", "yB", "x", "core", "rep"))
    tokens = P(("rep", "zh", "yA", "yB", "x", "core"), None)
    return jax.shard_map(
        per_device,
        mesh=fine,
        in_specs=(tokens,) * 6 + (P(("rep", "zh", "yA", "yB", "x", "core")),),
        out_specs=tokens,
        check_vma=False,
    )
```

time: 128 us -> 120 us (0.938)
  blocking collectives: 60.4 us -> 38.6 us
  starting transfers between devices: 24.6 us -> 33.8 us
  Pallas kernels: 25.5 us -> 29.1 us
  waiting for transfers between devices: 14.1 us -> 16.5 us
  local copies, waits for them, and re-layouts: 2.58 us -> 1.18 us
    all_to_all x1, blocking collectives: 42.6 us -> 19.5 us  [per_device(): lax.all_to_all(attended.reshape(heads, tokens, HD), GROUP, split_axis=0,...]
    ppermute x2 -> x4, starting transfers between devices: 6.48 us -> 19.5 us  [the longest x1 10.2 us: per_device(): down = lax.ppermute(near, RING, second_ring(-1))]
    ppermute x2 -> x4, waiting for transfers between devices: 3.38 us -> 11.9 us  [the longest x1 5.93 us: per_device(): up = lax.ppermute(near, RING, second_ring(1))]
    all_to_all x1, waiting for transfers between devices: 10.7 us -> 4.67 us  [per_device(): lax.all_to_all(merged, GROUP, split_axis=0, concat_axis=0, tiled=True)]
    all_to_all x1, starting transfers between devices: 14.4 us -> 10.2 us  [per_device(): lax.all_to_all(merged, GROUP, split_axis=0, concat_axis=0, tiled=True)]
    pallas_call x3 -> x4, Pallas kernels: 19.3 us -> 22.9 us  [the longest x3 21.2 us: attend(): pl.pallas_call(lambda *refs: attend_kernel(parts, first, last, sub, *refs...]
    unnamed x16 -> x8, local copies, waits for them, and re-layouts: 2.55 us -> 0.01 us
    all_gather x1, blocking collectives: 17.8 us -> 19.1 us  [per_device(): lax.all_gather(repack(received), RING, axis=0, tiled=True, axis_index_gro...]
  transfers between devices with their start and end apart: 4 -> 6, of which waited for: 3 -> 3; matrix products, arithmetic and copies ran while one was open for 0% -> 0% of each run, Pallas kernels for 3% -> 13%
where the time goes in v3:
time: 120 us; the launch traced here: 119 us
  blocking collectives  38.6 us (32%)
  starting transfers between devices  33.8 us (28%)
  Pallas kernels  29.1 us (24%)
  waiting for transfers between devices  16.5 us (14%)
    pallas_call x3, Pallas kernels, attend(): pl.pallas_call(lambda *refs: attend_kernel(parts, first, last, sub, *refs...  21.2 us
    all_to_all x1, blocking collectives, per_device(): lax.all_to_all(attended.reshape(heads, tokens, HD), GROUP, split_axis=0,...  19.5 us
    all_gather x1, blocking collectives, per_device(): lax.all_gather(repack(received), RING, axis=0, tiled=True, axis_index_gro...  19.1 us
    all_to_all x1, starting transfers between devices, per_device(): lax.all_to_all(merged, GROUP, split_axis=0, concat_axis=0, tiled=True)  10.2 us
    ppermute x1, starting transfers between devices, per_device(): down = lax.ppermute(near, RING, second_ring(-1))  10.2 us
    ppermute x1, waiting for transfers between devices, per_device(): up = lax.ppermute(near, RING, second_ring(1))  5.93 us
    ppermute x1, waiting for transfers between devices, per_device(): down = lax.ppermute(near, RING, second_ring(-1))  5.92 us
    ppermute x1, starting transfers between devices, per_device(): far_down = lax.ppermute(down[2:4], RING, second_ring(-1))  5.47 us
  transfers between devices with their start and end apart: 6, of which 3 were waited for; matrix products, arithmetic and copies ran while one was open for 0% of the time, Pallas kernels for 13%

profile of v3, /device:TPU:1, one launch (start us, length us, event | category | flops | bytes accessed | tf_op | source)
XLA Modules:
  0.0 119.3 jit_solution(17290856686398116906)
XLA Ops:
  0.0 0.0 copy-start.1
  0.0 0.0 copy-start.2
  0.0 0.0 copy-start
  0.0 4.4 %prepare_merged.1 = bf16[16,40,128]{2,1,0:T(8,128)(2,1)} custom-call(bf16[128,4096]{1,0:T(8,128)(2,1)} %key_ref.1, bf16[128,4096]{1,0:T(8,128)(2,1)} %value_ref.1, s32[32,128]{1,0:T(8,128)} %bitcast.17, s32[32,128]{1,0:T(8,128)} %bitcast.18, s32[1,128]{1,0:T(1,128)} %bitcast.19, f32[128,128]{1,0:T(8,128)} %constant.2.clone.table_ref), custom_call_target="tpu_custom_call" | custom-call | flops 134217728 | bytes 2097152 | tf_op jit(solution)/shard_map/prepare_merged/pallas_call | solution.py:78
  4.4 10.2 %all-to-all-start.1 = ((bf16[16,40,128]{2,1,0:T(8,128)(2,1)}), bf16[16,40,128]{2,1,0:T(8,128)(2,1)S(1)}, u32[]{:S(2)}, u32[]{:S(2)}) async-start(bf16[16,40,128]{2,1,0:T(8,128)(2,1)} %prepare_merged.1), calls=%async_computation.1 | async-start | bytes 327680 | tf_op jit(solution)/shard_map/all_to_all | solution.py:269
  14.6 0.0 copy-done.1
  14.6 0.0 copy-done.2
  14.6 0.0 copy-done
  14.6 1.8 %prepare_queries.1 = bf16[32,128,128]{2,1,0:T(8,128)(2,1)} custom-call(bf16[128,4096]{1,0:T(8,128)(2,1)S(1)} %copy-done, s32[32,128]{1,0:T(8,128)S(1)} %bitcast.16, bf16[128,128]{1,0:T(8,128)(2,1)S(1)} %copy-done.1), custom_call_target="tpu_custom_call" | custom-call | flops 134217728 | bytes 2097152 | tf_op jit(solution)/shard_map/prepare_queries/pallas_call | solution.py:108
  16.4 4.7 %all-to-all-done.1.in_ref = bf16[16,40,128]{2,1,0:T(8,128)(2,1)S(1)} async-done(((bf16[16,40,128]{2,1,0:T(8,128)(2,1)}), bf16[16,40,128]{2,1,0:T(8,128)(2,1)S(1)}, u32[]{:S(2)}, u32[]{:S(2)}) %all-to-all-start.1) | async-done | bytes 163872 | tf_op jit(solution)/shard_map/all_to_all | solution.py:269
  21.1 0.0 copy-start.3
  21.1 4.2 %all-to-all-start = ((bf16[32,128,128]{2,1,0:T(8,128)(2,1)}), bf16[32,128,128]{2,1,0:T(8,128)(2,1)S(1)}, u32[]{:S(2)}, u32[]{:S(2)}) async-start(bf16[32,128,128]{2,1,0:T(8,128)(2,1)} %prepare_queries.1), calls=%async_computation | async-start | bytes 2097152 | tf_op jit(solution)/shard_map/all_to_all | solution.py:270
  25.3 0.0 copy-done.3
  25.3 1.7 %repack.1 = bf16[1,528,128]{2,1,0:T(8,128)(2,1)} custom-call(bf16[16,40,128]{2,1,0:T(8,128)(2,1)} %copy-done.3), custom_call_target="tpu_custom_call" | custom-call | flops 1048576 | bytes 262144 | tf_op jit(solution)/shard_map/repack/pallas_call | solution.py:133
  27.0 19.1 %all_gather.3.refs_1_ = bf16[4,528,128]{2,1,0:T(8,128)(2,1)S(1)} all-gather(bf16[1,528,128]{2,1,0:T(8,128)(2,1)} %repack.1), channel_id=1, replica_groups={{0,128,256,384},{32,160,288,416},{64,192,320,448},{96,224,352,480},{2,3..., dimensions={0}, use_global_device_ids=true | all-gather | bytes 675840 | tf_op jit(solution)/shard_map/all_gather | solution.py:272
  46.1 10.2 %collective-permute-start.1 = (bf16[4,528,128]{2,1,0:T(8,128)(2,1)S(1)}, bf16[4,528,128]{2,1,0:T(8,128)(2,1)S(1)}, u32[]{:S(2)}, u32[]{:S(2)}) collective-permute-start(bf16[4,528,128]{2,1,0:T(8,128)(2,1)S(1)} %all_gather.3.refs_1_), channel_id=1, source_target_pairs={{0,96},{2,386},{32,0},{34,418},{64,32},{66,450},{96,64},{98,482},{... | collective-permute-start | bytes 1622024 | tf_op jit(solution)/shard_map/ppermute | solution.py:274
  56.3 1.9 %collective-permute-start = (bf16[4,528,128]{2,1,0:T(8,128)(2,1)S(1)}, bf16[4,528,128]{2,1,0:T(8,128)(2,1)S(1)}, u32[]{:S(2)}, u32[]{:S(2)}) collective-permute-start(bf16[4,528,128]{2,1,0:T(8,128)(2,1)S(1)} %all_gather.3.refs_1_), channel_id=1, source_target_pairs={{0,32},{2,130},{32,64},{34,162},{64,96},{66,194},{96,0},{98,226},{... | collective-permute-start | bytes 1622024 | tf_op jit(solution)/shard_map/ppermute | solution.py:273
  58.2 0.0 all-to-all-done
  58.2 4.2 %attend.3 = (f32[2,2048,128]{2,1,0:T(8,128)S(1)}, f32[2,2048,128]{2,1,0:T(8,128)S(1)}) custom-call(bf16[16,2,128,128]{3,2,1,0:T(8,128)(2,1)S(1)} %bitcast.12, bf16[4,528,128]{2,1,0:T(8,128)(2,1)S(1)} %all_gather.3.refs_1_), custom_call_target="tpu_custom_call" | custom-call | flops 2147483648 | bytes 8388608 | tf_op jit(solution)/shard_map/attend/pallas_call | solution.py:210
  62.5 5.9 %collective-permute-done.1.refs_2_ = bf16[4,528,128]{2,1,0:T(8,128)(2,1)S(1)} collective-permute-done((bf16[4,528,128]{2,1,0:T(8,128)(2,1)S(1)}, bf16[4,528,128]{2,1,0:T(8,128)(2,1)S(1)}, u32[]{:S(2)}, u32[]{:S(2)}) %collective-permute-start.1) | collective-permute-done | bytes 540704 | tf_op jit(solution)/shard_map/ppermute | solution.py:274
  68.4 5.9 %collective-permute-done.refs_1_ = bf16[4,528,128]{2,1,0:T(8,128)(2,1)S(1)} collective-permute-done((bf16[4,528,128]{2,1,0:T(8,128)(2,1)S(1)}, bf16[4,528,128]{2,1,0:T(8,128)(2,1)S(1)}, u32[]{:S(2)}, u32[]{:S(2)}) %collective-permute-start) | collective-permute-done | bytes 540704 | tf_op jit(solution)/shard_map/ppermute | solution.py:273
  74.4 1.9 %collective-permute-start.2 = (bf16[2,528,128]{2,1,0:T(8,128)(2,1)S(1)}, bf16[2,528,128]{2,1,0:T(8,128)(2,1)S(1)}, u32[]{:S(2)}, u32[]{:S(2)}) collective-permute-start(bf16[2,528,128]{2,1,0:T(8,128)(2,1)S(1)} %slice.6), channel_id=1, source_target_pairs={{0,32},{2,130},{32,64},{34,162},{64,96},{66,194},{96,0},{98,226},{... | collective-permute-start | bytes 811016 | tf_op jit(solution)/shard_map/ppermute | solution.py:277
  76.3 5.5 %collective-permute-start.3 = (bf16[2,528,128]{2,1,0:T(8,128)(2,1)S(1)}, bf16[2,528,128]{2,1,0:T(8,128)(2,1)S(1)}, u32[]{:S(2)}, u32[]{:S(2)}) collective-permute-start(bf16[2,528,128]{2,1,0:T(8,128)(2,1)S(1)} %slice.7), channel_id=1, source_target_pairs={{0,96},{2,386},{32,0},{34,418},{64,32},{66,450},{96,64},{98,482},{... | collective-permute-start | bytes 811016 | tf_op jit(solution)/shard_map/ppermute | solution.py:278
  81.8 8.0 %attend.4 = (f32[2,2048,128]{2,1,0:T(8,128)S(1)}, f32[2,2048,128]{2,1,0:T(8,128)S(1)}) custom-call(bf16[16,2,128,128]{3,2,1,0:T(8,128)(2,1)S(1)} %bitcast.13, bf16[4,528,128]{2,1,0:T(8,128)(2,1)S(1)} %collective-permute-done.refs_1_, bf16[4,528,128]{2,1,0:T(8,128)(2,1)S(1)} %collective-permute-done.1.refs_2_, f32[2,2048,128]{2,1,0:T(8,128)S(1)} %get-tuple-element.17.refs_3_, ...), custom_call_target="tpu_custom_call" | custom-call | flops 4294967296 | bytes 8388608 | tf_op jit(solution)/shard_map/attend/pallas_call | solution.py:210
  89.8 0.0 collective-permute-done.2.refs_1_
  89.8 0.0 collective-permute-done.3.refs_2_
  89.8 8.9 %attend.5 = bf16[16,2,128,128]{3,2,1,0:T(8,128)(2,1)S(1)} custom-call(bf16[16,2,128,128]{3,2,1,0:T(8,128)(2,1)S(1)} %bitcast.14, bf16[2,528,128]{2,1,0:T(8,128)(2,1)S(1)} %collective-permute-done.2.refs_1_, bf16[2,528,128]{2,1,0:T(8,128)(2,1)S(1)} %collective-permute-done.3.refs_2_, f32[2,2048,128]{2,1,0:T(8,128)S(1)} %get-tuple-element.19.refs_3_, ...), custom_call_target="tpu_custom_call" | custom-call | flops 2147483648 | bytes 8388608 | tf_op jit(solution)/shard_map/attend/pallas_call | solution.py:210
  98.8 19.5 %all_to_all.15 = bf16[32,128,128]{2,1,0:T(8,128)(2,1)S(1)} all-to-all(bf16[32,128,128]{2,1,0:T(8,128)(2,1)S(1)} %bitcast.15), channel_id=1, replica_groups=mesh['zh'=4,'yA'=4,'yB'=2,'x'=4,'core'=2,'rep'=2] {'yB','x','core'}, dimensions={0} | all-to-all | bytes 2097152 | tf_op jit(solution)/shard_map/all_to_all | solution.py:281
  118.2 1.1 copy_bitcast_fusion
  (2 shorter events, 0.0 us)
Async XLA Ops:
  0.0 14.6 %copy-start.1 = (bf16[128,128]{1,0:T(8,128)(2,1)S(1)}, bf16[128,128]{1,0:T(8,128)(2,1)}, u32[]{:S(2)}) copy-start(bf16[128,128]{1,0:T(8,128)(2,1)} %constant.10.table_ref) | copy-start | bytes 98308
  0.0 14.6 %copy-start.2 = (s32[128,32]{0,1:T(8,128)S(1)}, s32[128,32]{0,1:T(8,128)}, u32[]{:S(2)}) copy-start(s32[128,32]{0,1:T(8,128)} %param.11) | copy-start | bytes 49156
  0.0 14.6 %copy-start = (bf16[128,4096]{1,0:T(8,128)(2,1)S(1)}, bf16[128,4096]{1,0:T(8,128)(2,1)}, u32[]{:S(2)}) copy-start(bf16[128,4096]{1,0:T(8,128)(2,1)} %query_ref.1) | copy-start | bytes 3145732
  4.4 16.7 %all-to-all-start.1 = ((bf16[16,40,128]{2,1,0:T(8,128)(2,1)}), bf16[16,40,128]{2,1,0:T(8,128)(2,1)S(1)}, u32[]{:S(2)}, u32[]{:S(2)}) async-start(bf16[16,40,128]{2,1,0:T(8,128)(2,1)} %prepare_merged.1), calls=%async_computation.1 | async-start | bytes 327680 | tf_op jit(solution)/shard_map/all_to_all | solution.py:269
  21.1 4.2 %copy-start.3 = (bf16[16,40,128]{2,1,0:T(8,128)(2,1)}, bf16[16,40,128]{2,1,0:T(8,128)(2,1)S(1)}, u32[]{:S(2)}) copy-start(bf16[16,40,128]{2,1,0:T(8,128)(2,1)S(1)} %all-to-all-done.1.in_ref) | copy-start | bytes 491524
  21.1 37.1 %all-to-all-start = ((bf16[32,128,128]{2,1,0:T(8,128)(2,1)}), bf16[32,128,128]{2,1,0:T(8,128)(2,1)S(1)}, u32[]{:S(2)}, u32[]{:S(2)}) async-start(bf16[32,128,128]{2,1,0:T(8,128)(2,1)} %prepare_queries.1), calls=%async_computation | async-start | bytes 2097152 | tf_op jit(solution)/shard_map/all_to_all | solution.py:270
  46.1 22.2 %collective-permute-start.1 = (bf16[4,528,128]{2,1,0:T(8,128)(2,1)S(1)}, bf16[4,528,128]{2,1,0:T(8,128)(2,1)S(1)}, u32[]{:S(2)}, u32[]{:S(2)}) collective-permute-start(bf16[4,528,128]{2,1,0:T(8,128)(2,1)S(1)} %all_gather.3.refs_1_), channel_id=1, source_target_pairs={{0,96},{2,386},{32,0},{34,418},{64,32},{66,450},{96,64},{98,482},{... | collective-permute-start | bytes 1622024 | tf_op jit(solution)/shard_map/ppermute | solution.py:274
  56.3 18.0 %collective-permute-start = (bf16[4,528,128]{2,1,0:T(8,128)(2,1)S(1)}, bf16[4,528,128]{2,1,0:T(8,128)(2,1)S(1)}, u32[]{:S(2)}, u32[]{:S(2)}) collective-permute-start(bf16[4,528,128]{2,1,0:T(8,128)(2,1)S(1)} %all_gather.3.refs_1_), channel_id=1, source_target_pairs={{0,32},{2,130},{32,64},{34,162},{64,96},{66,194},{96,0},{98,226},{... | collective-permute-start | bytes 1622024 | tf_op jit(solution)/shard_map/ppermute | solution.py:273
  74.4 15.5 %collective-permute-start.2 = (bf16[2,528,128]{2,1,0:T(8,128)(2,1)S(1)}, bf16[2,528,128]{2,1,0:T(8,128)(2,1)S(1)}, u32[]{:S(2)}, u32[]{:S(2)}) collective-permute-start(bf16[2,528,128]{2,1,0:T(8,128)(2,1)S(1)} %slice.6), channel_id=1, source_target_pairs={{0,32},{2,130},{32,64},{34,162},{64,96},{66,194},{96,0},{98,226},{... | collective-permute-start | bytes 811016 | tf_op jit(solution)/shard_map/ppermute | solution.py:277
  76.3 13.5 %collective-permute-start.3 = (bf16[2,528,128]{2,1,0:T(8,128)(2,1)S(1)}, bf16[2,528,128]{2,1,0:T(8,128)(2,1)S(1)}, u32[]{:S(2)}, u32[]{:S(2)}) collective-permute-start(bf16[2,528,128]{2,1,0:T(8,128)(2,1)S(1)} %slice.7), channel_id=1, source_target_pairs={{0,96},{2,386},{32,0},{34,418},{64,32},{66,450},{96,64},{98,482},{... | collective-permute-start | bytes 811016 | tf_op jit(solution)/shard_map/ppermute | solution.py:278

commit v4 on v3

v4 whole, which is shorter than its diff:
```python
import math

import jax
import jax.numpy as jnp
import numpy as np
from jax import lax
from jax.experimental import pallas as pl
from jax.experimental.pallas import tpu as pltpu
from jax.sharding import Mesh
from jax.sharding import PartitionSpec as P

HD = 128
MERGED = 8
ZH, Y, X, CORE = 4, 8, 4, 2
GROUP = ("yB", "x", "core")
RING = ("zh", "yA", "yB", "core", "rep")
REP = 2
SCALE = 1.0 / math.sqrt(HD)
LOG2E = math.log2(math.e)


def sylvester():
    row = lax.broadcasted_iota(jnp.int32, (HD, HD), 0)
    column = lax.broadcasted_iota(jnp.int32, (HD, HD), 1)
    both = row & column
    odd = both
    for bit in range(1, HD.bit_length() - 1):
        odd = odd ^ (both >> bit)
    return (1 - 2 * (odd & 1)).astype(jnp.float32)


def columns_of(source, held, arrived, chunks):
    piece = held.shape[1] // chunks
    copies = []
    for chunk in range(chunks):
        columns = pl.ds(chunk * piece, piece)
        copies.append(pltpu.make_async_copy(source.at[:, columns], held.at[:, columns], arrived.at[chunk]))
    return copies


def prepare_merged_kernel(
    chunks, key_ref, value_ref, key_exp_ref, value_exp_ref, map_ref, out_ref, sums, held, exps, where, arrived, small
):
    tokens, width = held.shape[1:]
    heads = width // HD
    exponents = [
        pltpu.make_async_copy(key_exp_ref, exps.at[0], small.at[0]),
        pltpu.make_async_copy(value_exp_ref, exps.at[1], small.at[1]),
    ]
    mapped = pltpu.make_async_copy(map_ref, where, small.at[2])
    sides = [
        columns_of(source, held.at[side], arrived.at[side], chunks)
        for side, source in enumerate((key_ref, value_ref))
    ]
    mapped.start()
    exponents[0].start()
    for copy in sides[0]:
        copy.start()
    exponents[1].start()
    for copy in sides[1]:
        copy.start()
    table = sylvester()
    mapped.wait()
    slot = lax.broadcasted_iota(jnp.int32, (MERGED, tokens), 0)
    onehot = (where[...] == slot).astype(jnp.float32)
    counts = jnp.sum(onehot, axis=1, keepdims=True)
    spread = jnp.where(
        lax.broadcasted_iota(jnp.int32, (MERGED, HD), 1)
        == lax.broadcasted_iota(jnp.int32, (MERGED, HD), 0) + MERGED * lax.axis_index(GROUP),
        counts,
        0.0,
    )
    count_rows = jnp.broadcast_to(jnp.sum(spread, axis=0, keepdims=True), (MERGED, HD)).astype(jnp.bfloat16)
    for side in range(2):
        exponents[side].wait()
        scaling = jnp.exp2(exps[side].astype(jnp.float32))
        for head in range(heads):
            if head * chunks % heads == 0:
                sides[side][head * chunks // heads].wait()
            chosen = (onehot * scaling[head : head + 1, :]).astype(jnp.bfloat16)
            start = (side * heads + head) * MERGED
            sums[start : start + MERGED, :] = jnp.dot(
                chosen, held[side, :, head * HD : (head + 1) * HD], preferred_element_type=jnp.float32
            )
    rotated = jnp.dot(
        sums[...], table, precision=lax.Precision.HIGHEST, preferred_element_type=jnp.float32
    ).reshape(2, heads, MERGED, HD)
    merged = (rotated / counts[None, None, :, :] * SCALE).astype(jnp.bfloat16)
    pair = out_ref.shape[1] // (2 * MERGED)
    for head in range(heads):
        target, place = head // pair, head % pair * 2 * MERGED
        out_ref[target, place : place + MERGED, :] = merged[0, head]
        out_ref[target, place + MERGED : place + 2 * MERGED, :] = merged[1, head]
    for target in range(heads // pair):
        out_ref[target, pair * 2 * MERGED :, :] = count_rows


def prepare_merged(key, value, key_exp, value_exp, merge_map, targets, chunks=2):
    heads = key_exp.shape[0]
    rows = heads // targets * 2 * MERGED + MERGED
    merge_map = merge_map.reshape(1, -1)
    return pl.pallas_call(
        lambda *refs: prepare_merged_kernel(chunks, *refs),
        in_specs=[pl.BlockSpec(memory_space=pl.ANY)] * 5,
        out_specs=pl.BlockSpec(memory_space=pltpu.VMEM),
        out_shape=jax.ShapeDtypeStruct((targets, rows, HD), jnp.bfloat16),
        scratch_shapes=[
            pltpu.VMEM((2 * heads * MERGED, HD), jnp.float32),
            pltpu.VMEM((2, *key.shape), jnp.bfloat16),
            pltpu.VMEM((2, *key_exp.shape), jnp.int32),
            pltpu.VMEM(merge_map.shape, jnp.int32),
            pltpu.SemaphoreType.DMA((2, chunks)),
            pltpu.SemaphoreType.DMA((3,)),
        ],
        compiler_params=pltpu.CompilerParams(vmem_limit_bytes=56 * 2**20),
        cost_estimate=pl.CostEstimate(flops=2**27, bytes_accessed=2**21, transcendentals=0),
        name="prepare_merged",
    )(key, value, key_exp, value_exp, merge_map)


def prepare_queries_kernel(chunks, query_ref, exp_ref, out_ref, held, exps, arrived, small):
    heads = exps.shape[0]
    exponents = pltpu.make_async_copy(exp_ref, exps, small.at[0])
    copies = columns_of(query_ref, held, arrived, chunks)
    exponents.start()
    for copy in copies:
        copy.start()
    table = sylvester().astype(jnp.bfloat16)
    exponents.wait()
    scaling = (jnp.exp2(exps[...].astype(jnp.float32)) * SCALE).T
    for head in range(heads):
        if head * chunks % heads == 0:
            copies[head * chunks // heads].wait()
        rotated = jnp.dot(
            held[:, head * HD : (head + 1) * HD], table, preferred_element_type=jnp.float32
        )
        out_ref[head] = (rotated * scaling[:, head : head + 1]).astype(jnp.bfloat16)


def prepare_queries(query, query_exp, chunks=2):
    tokens = query.shape[0]
    heads = query_exp.shape[0]
    return pl.pallas_call(
        lambda *refs: prepare_queries_kernel(chunks, *refs),
        in_specs=[pl.BlockSpec(memory_space=pl.ANY)] * 2,
        out_specs=pl.BlockSpec(memory_space=pltpu.VMEM),
        out_shape=jax.ShapeDtypeStruct((heads, tokens, HD), jnp.bfloat16),
        scratch_shapes=[
            pltpu.VMEM(query.shape, jnp.bfloat16),
            pltpu.VMEM(query_exp.shape, jnp.int32),
            pltpu.SemaphoreType.DMA((chunks,)),
            pltpu.SemaphoreType.DMA((1,)),
        ],
        compiler_params=pltpu.CompilerParams(vmem_limit_bytes=56 * 2**20),
        cost_estimate=pl.CostEstimate(flops=2**27, bytes_accessed=2**21, transcendentals=0),
        name="prepare_queries",
    )(query, query_exp)


def repack_kernel(in_ref, out_ref):
    sources, height, _ = in_ref.shape
    rows = sources * MERGED
    for kind in range(height // MERGED - 1):
        out_ref[0, kind * rows : (kind + 1) * rows, :] = in_ref[
            :, kind * MERGED : (kind + 1) * MERGED, :
        ].reshape(rows, HD)
    counts = jnp.sum(in_ref[:, height - MERGED :, :].astype(jnp.float32), axis=0)
    out_ref[0, (height // MERGED - 1) * rows :, :] = jnp.concatenate([counts] * 2, axis=0).astype(jnp.bfloat16)


def repack(received):
    sources, height, _ = received.shape
    rows = sources * MERGED
    return pl.pallas_call(
        repack_kernel,
        out_shape=jax.ShapeDtypeStruct((1, (height // MERGED - 1) * rows + 16, HD), jnp.bfloat16),
        cost_estimate=pl.CostEstimate(flops=2**20, bytes_accessed=2**18, transcendentals=0),
        name="repack",
    )(received)


def attend_kernel(parts, first, last, sub, *refs):
    query_ref = refs[0]
    piece_refs = refs[1 : 1 + parts]
    refs = refs[1 + parts :]
    if not first:
        both_ref, top_ref = refs[:2]
        refs = refs[2:]
    out_refs = refs[: 1 if last else 2]
    keys, values, logs = refs[1 if last else 2 :]
    sources, pair, tokens, _ = query_ref.shape
    step = sub // tokens
    place = 0
    for piece_ref in piece_refs:
        for block in range(piece_ref.shape[0]):
            for head in range(pair):
                base = head * 2 * HD
                keys[head, place : place + HD, :] = piece_ref[block, base : base + HD, :]
                values[head, place : place + HD, 0:HD] = piece_ref[block, base + HD : base + 2 * HD, :]
            counts = piece_ref[block, 2 * pair * HD : 2 * pair * HD + 16, :].astype(jnp.float32)
            logs[:, place : place + HD] = jnp.log(counts[0:8]) * LOG2E
            place += HD
    values[:, :, HD:] = jnp.ones((pair, place, HD), jnp.bfloat16)

    def score(head, index):
        scores = lax.dot_general(
            query_ref[index * step : (index + 1) * step, head].reshape(sub, HD),
            keys[head],
            (((1,), (1,)), ((), ())),
            preferred_element_type=jnp.float32,
        )
        return scores * (SCALE * LOG2E) + logs[0:1, :]

    def mix(head, index, scores):
        rows = slice(index * sub, (index + 1) * sub)
        top = jnp.broadcast_to(jnp.max(scores, axis=1, keepdims=True), (sub, HD))
        if not first:
            before = top_ref[head, rows, :]
            top = jnp.maximum(top, before)
            rescale = jnp.exp2(before - top)
        weights = jnp.exp2(scores - jnp.concatenate([top] * (place // HD), axis=1)).astype(jnp.bfloat16)
        both = jnp.dot(weights, values[head], preferred_element_type=jnp.float32)
        if not first:
            both = both + both_ref[head, rows, :] * jnp.concatenate([rescale] * 2, axis=1)
        if last:
            done = (both[:, 0:HD] / both[:, HD:]).astype(jnp.bfloat16)
            out_refs[0][index * step : (index + 1) * step, head] = done.reshape(step, tokens, HD)
        else:
            out_refs[0][head, rows, :] = both
            out_refs[1][head, rows, :] = top

    tiles = [(head, index) for head in range(pair) for index in range(sources // step)]
    upcoming = score(*tiles[0])
    for number, tile in enumerate(tiles):
        scores = upcoming
        if number + 1 < len(tiles):
            upcoming = score(*tiles[number + 1])
        mix(*tile, scores)


def attend(queries, pieces, state, last, sub=256):
    sources, pair, tokens, _ = queries.shape
    rows = sources * tokens
    parts = len(pieces)
    slots = HD * sum(piece.shape[0] for piece in pieces)
    first = state is None
    if last:
        out_shape = jax.ShapeDtypeStruct(queries.shape, jnp.bfloat16)
    else:
        out_shape = [jax.ShapeDtypeStruct((pair, rows, width), jnp.float32) for width in (2 * HD, HD)]
    return pl.pallas_call(
        lambda *refs: attend_kernel(parts, first, last, sub, *refs),
        out_shape=out_shape,
        scratch_shapes=[
            pltpu.VMEM((pair, slots, HD), jnp.bfloat16),
            pltpu.VMEM((pair, slots, 2 * HD), jnp.bfloat16),
            pltpu.VMEM((8, slots), jnp.float32),
        ],
        compiler_params=pltpu.CompilerParams(vmem_limit_bytes=24 * 2**20),
        cost_estimate=pl.CostEstimate(
            flops=8 * pair * rows * slots * HD,
            bytes_accessed=16 * pair * rows * HD,
            transcendentals=pair * rows * slots,
        ),
        name="attend",
    )(queries, *pieces, *(() if first else state))


def place(zh, ya, yb, core, rep):
    return (((zh % ZH * (Y // 2) + ya % (Y // 2)) * 2 + yb) * CORE + core) * REP + rep


def ring(by, over_y):
    pairs = []
    for zh, ya, yb, core, rep in np.ndindex(ZH, Y // 2, 2, CORE, REP):
        if core == over_y:
            moved = (zh, ya + (by if yb == 0 else -by))
        else:
            moved = (zh + (by if rep == 0 else -by), ya)
        pairs.append((place(zh, ya, yb, core, rep), place(*moved, yb, core, rep)))
    return pairs


def first_ring(by):
    return ring(by, 1)


def second_ring(by):
    return ring(by, 0)


def per_device(
    query_mantissa,
    key_mantissa,
    value_mantissa,
    query_exponent,
    key_exponent,
    value_exponent,
    merge_map,
):
    tokens = query_mantissa.shape[0]
    heads = query_exponent.shape[1]
    targets = lax.axis_size(GROUP)
    merged = prepare_merged(key_mantissa, value_mantissa, key_exponent.T, value_exponent.T, merge_map, targets)
    queries = prepare_queries(query_mantissa, query_exponent.T)
    received = lax.all_to_all(merged, GROUP, split_axis=0, concat_axis=0, tiled=True)
    received, queries = lax.optimization_barrier((received, queries))
    own = repack(received)
    queries, own = lax.optimization_barrier((queries, own))
    head_queries = lax.all_to_all(queries, GROUP, split_axis=0, concat_axis=0, tiled=True)
    head_queries = head_queries.reshape(targets, heads // targets, tokens, HD)
    near = jnp.concatenate([own] + [lax.ppermute(own, RING, first_ring(by)) for by in (1, -1, 2)], axis=0)
    up = lax.ppermute(near, RING, second_ring(1))
    down = lax.ppermute(near, RING, second_ring(-1))
    state = attend(head_queries, (near,), None, False)
    up, state = lax.optimization_barrier((up, state))
    far = lax.ppermute(up, RING, second_ring(1))
    state = attend(head_queries, (up, down), state, False)
    attended = attend(head_queries, (far,), state, True)
    returned = lax.all_to_all(
        attended.reshape(heads, tokens, HD), GROUP, split_axis=0, concat_axis=0, tiled=True
    )
    return jnp.transpose(returned, (1, 0, 2)).reshape(tokens, heads * HD)


def solution(mesh):
    fine = Mesh(mesh.devices.reshape(ZH, Y // 2, 2, X, CORE, 2), ("zh", "yA", "yB", "x", "core", "rep"))
    tokens = P(("rep", "zh", "yA", "yB", "x", "core"), None)
    return jax.shard_map(
        per_device,
        mesh=fine,
        in_specs=(tokens,) * 6 + (P(("rep", "zh", "yA", "yB", "x", "core")),),
        out_specs=tokens,
        check_vma=False,
    )
```

time: 120 us -> 105 us (0.88)
  blocking collectives: 38.6 us -> 23.1 us
  Pallas kernels: 29.1 us -> 18.8 us
  starting transfers between devices: 33.8 us -> 42.3 us
  local copies, waits for them, and re-layouts: 1.18 us -> 2.77 us
    all_gather x1 -> x0, blocking collectives: 19.1 us -> none  [per_device(): lax.all_gather(repack(received), RING, axis=0, tiled=True, axis_index_gro...]
    ppermute x2 -> x4, waiting for transfers between devices: 0.01 us -> 11.5 us  [the longest x3 7.98 us: per_device(): lax.ppermute(own, RING, first_ring(by))]
    ppermute x2 -> x4, starting transfers between devices: 7.39 us -> 18.1 us  [the longest x3 10.5 us: per_device(): lax.ppermute(own, RING, first_ring(by))]
    pallas_call x3, Pallas kernels: 21.2 us -> 11.3 us  [attend(): pl.pallas_call(lambda *refs: attend_kernel(parts, first, last, sub, *refs...]
    ppermute x1, waiting for transfers between devices: 5.92 us -> 0.01 us  [per_device(): down = lax.ppermute(near, RING, second_ring(-1))]
    all_to_all x1, blocking collectives: 19.5 us -> 23.1 us  [per_device(): lax.all_to_all(attended.reshape(heads, tokens, HD), GROUP, split_axis=0,...]
    ppermute x1, waiting for transfers between devices: 5.93 us -> 2.27 us  [per_device(): up = lax.ppermute(near, RING, second_ring(1))]
    ppermute x1, starting transfers between devices: 10.2 us -> 6.77 us  [per_device(): down = lax.ppermute(near, RING, second_ring(-1))]
  transfers between devices with their start and end apart: 6 -> 8, of which waited for: 3 -> 6; matrix products, arithmetic and copies ran while one was open for 0% -> 1% of each run, Pallas kernels for 13% -> 11%
where the time goes in v4:
time: 105 us
  starting transfers between devices  42.3 us (40%)
  blocking collectives  23.1 us (22%)
  Pallas kernels  18.8 us (18%)
  waiting for transfers between devices  17.5 us (17%)
  local copies, waits for them, and re-layouts  2.77 us (3%)
    all_to_all x1, blocking collectives, per_device(): lax.all_to_all(attended.reshape(heads, tokens, HD), GROUP, split_axis=0,...  23.1 us
    pallas_call x3, Pallas kernels, attend(): pl.pallas_call(lambda *refs: attend_kernel(parts, first, last, sub, *refs...  11.3 us
    ppermute x3, starting transfers between devices, per_device(): lax.ppermute(own, RING, first_ring(by))  10.5 us
    all_to_all x1, starting transfers between devices, per_device(): lax.all_to_all(merged, GROUP, split_axis=0, concat_axis=0, tiled=True)  10.2 us
    ppermute x3, waiting for transfers between devices, per_device(): lax.ppermute(own, RING, first_ring(by))  7.98 us
    ppermute x1, starting transfers between devices, per_device(): far = lax.ppermute(up, RING, second_ring(1))  7.58 us
    ppermute x1, starting transfers between devices, per_device(): down = lax.ppermute(near, RING, second_ring(-1))  6.77 us
    all_to_all x1, starting transfers between devices, per_device(): lax.all_to_all(queries, GROUP, split_axis=0, concat_axis=0, tiled=True)  4.18 us
  transfers between devices with their start and end apart: 8, of which 6 were waited for; matrix products, arithmetic and copies ran while one was open for 1% of the time, Pallas kernels for 11%

profile of v4, /device:TPU:1, one launch (start us, length us, event | category | flops | bytes accessed | tf_op | source)
XLA Modules:
  0.0 104.6 jit_solution(4061470286282474440)
XLA Ops:
  0.0 3.1 %prepare_merged.1 = bf16[16,40,128]{2,1,0:T(8,128)(2,1)} custom-call(bf16[128,4096]{1,0:T(8,128)(2,1)} %refs_0_.2, bf16[128,4096]{1,0:T(8,128)(2,1)} %refs_1_.1, s32[32,128]{1,0:T(8,128)} %bitcast.16, s32[32,128]{1,0:T(8,128)} %bitcast.17, s32[1,128]{1,0:T(1,128)} %bitcast.19), custom_call_target="tpu_custom_call" | custom-call | flops 134217728 | bytes 2097152 | tf_op jit(solution)/shard_map/prepare_merged/pallas_call | solution.py:102
  3.1 10.2 %all-to-all-start = ((bf16[16,40,128]{2,1,0:T(8,128)(2,1)}), bf16[16,40,128]{2,1,0:T(8,128)(2,1)S(1)}, u32[]{:S(2)}, u32[]{:S(2)}) async-start(bf16[16,40,128]{2,1,0:T(8,128)(2,1)} %prepare_merged.1), calls=%async_computation | async-start | bytes 327680 | tf_op jit(solution)/shard_map/all_to_all | solution.py:306
  13.3 2.8 %prepare_queries.1 = bf16[32,128,128]{2,1,0:T(8,128)(2,1)} custom-call(bf16[128,4096]{1,0:T(8,128)(2,1)} %refs_0_.3, s32[32,128]{1,0:T(8,128)} %bitcast.18), custom_call_target="tpu_custom_call" | custom-call | flops 134217728 | bytes 2097152 | tf_op jit(solution)/shard_map/prepare_queries/pallas_call | solution.py:143
  16.1 3.7 %all-to-all-done.in_ref = bf16[16,40,128]{2,1,0:T(8,128)(2,1)S(1)} async-done(((bf16[16,40,128]{2,1,0:T(8,128)(2,1)}), bf16[16,40,128]{2,1,0:T(8,128)(2,1)S(1)}, u32[]{:S(2)}, u32[]{:S(2)}) %all-to-all-start) | async-done | bytes 163872 | tf_op jit(solution)/shard_map/all_to_all | solution.py:306
  19.8 0.0 copy-start
  19.8 0.7 copy-done
  20.4 1.6 %repack.1 = bf16[1,528,128]{2,1,0:T(8,128)(2,1)} custom-call(bf16[16,40,128]{2,1,0:T(8,128)(2,1)} %copy-done), custom_call_target="tpu_custom_call" | custom-call | flops 1048576 | bytes 262144 | tf_op jit(solution)/shard_map/repack/pallas_call | solution.py:174
  22.1 4.2 %all-to-all-start.1 = ((bf16[32,128,128]{2,1,0:T(8,128)(2,1)}), bf16[32,128,128]{2,1,0:T(8,128)(2,1)S(1)}, u32[]{:S(2)}, u32[]{:S(2)}) async-start(bf16[32,128,128]{2,1,0:T(8,128)(2,1)} %prepare_queries.1), calls=%async_computation.1 | async-start | bytes 2097152 | tf_op jit(solution)/shard_map/all_to_all | solution.py:310
  26.2 1.9 %collective-permute-start = (bf16[1,528,128]{2,1,0:T(8,128)(2,1)}, bf16[1,528,128]{2,1,0:T(8,128)(2,1)S(1)}, u32[]{:S(2)}, u32[]{:S(2)}) collective-permute-start(bf16[1,528,128]{2,1,0:T(8,128)(2,1)} %repack.1), channel_id=1, source_target_pairs={{0,128},{1,385},{2,34},{3,35},{16,144},{17,401},{18,114},{19,115},... | collective-permute-start | bytes 405512 | tf_op jit(solution)/shard_map/ppermute | solution.py:312
  28.2 3.6 %collective-permute-start.2 = (bf16[1,528,128]{2,1,0:T(8,128)(2,1)}, bf16[1,528,128]{2,1,0:T(8,128)(2,1)S(1)}, u32[]{:S(2)}, u32[]{:S(2)}) collective-permute-start(bf16[1,528,128]{2,1,0:T(8,128)(2,1)} %repack.1), channel_id=1, source_target_pairs={{0,256},{1,257},{2,66},{3,67},{16,272},{17,273},{18,82},{19,83},{3... | collective-permute-start | bytes 405512 | tf_op jit(solution)/shard_map/ppermute | solution.py:312
  31.8 5.0 %collective-permute-start.1 = (bf16[1,528,128]{2,1,0:T(8,128)(2,1)}, bf16[1,528,128]{2,1,0:T(8,128)(2,1)S(1)}, u32[]{:S(2)}, u32[]{:S(2)}) collective-permute-start(bf16[1,528,128]{2,1,0:T(8,128)(2,1)} %repack.1), channel_id=1, source_target_pairs={{0,384},{1,129},{2,98},{3,99},{16,400},{17,145},{18,50},{19,51},{3... | collective-permute-start | bytes 405512 | tf_op jit(solution)/shard_map/ppermute | solution.py:312
  36.8 0.9 constant_dynamic-update-slice_fusion.3
  37.7 3.8 %collective-permute-done = bf16[1,528,128]{2,1,0:T(8,128)(2,1)S(1)} collective-permute-done((bf16[1,528,128]{2,1,0:T(8,128)(2,1)}, bf16[1,528,128]{2,1,0:T(8,128)(2,1)S(1)}, u32[]{:S(2)}, u32[]{:S(2)}) %collective-permute-start) | collective-permute-done | bytes 135200 | tf_op jit(solution)/shard_map/ppermute | solution.py:312
  41.5 1.7 %collective-permute-done.1 = bf16[1,528,128]{2,1,0:T(8,128)(2,1)S(1)} collective-permute-done((bf16[1,528,128]{2,1,0:T(8,128)(2,1)}, bf16[1,528,128]{2,1,0:T(8,128)(2,1)S(1)}, u32[]{:S(2)}, u32[]{:S(2)}) %collective-permute-start.1) | collective-permute-done | bytes 135200 | tf_op jit(solution)/shard_map/ppermute | solution.py:312
  43.2 2.5 %collective-permute-done.2 = bf16[1,528,128]{2,1,0:T(8,128)(2,1)S(1)} collective-permute-done((bf16[1,528,128]{2,1,0:T(8,128)(2,1)}, bf16[1,528,128]{2,1,0:T(8,128)(2,1)S(1)}, u32[]{:S(2)}, u32[]{:S(2)}) %collective-permute-start.2) | collective-permute-done | bytes 135200 | tf_op jit(solution)/shard_map/ppermute | solution.py:312
  45.7 3.1 %collective-permute-start.3 = (bf16[4,528,128]{2,1,0:T(8,128)(2,1)S(1)}, bf16[4,528,128]{2,1,0:T(8,128)(2,1)S(1)}, u32[]{:S(2)}, u32[]{:S(2)}) collective-permute-start(bf16[4,528,128]{2,1,0:T(8,128)(2,1)S(1)} %constant_dynamic-update-slice_fusion.refs_1_), channel_id=1, source_target_pairs={{0,32},{1,33},{2,130},{3,387},{16,112},{17,113},{18,146},{19,403},... | collective-permute-start | bytes 1622024 | tf_op jit(solution)/shard_map/ppermute | solution.py:313
  48.8 6.8 %collective-permute-start.5 = (bf16[4,528,128]{2,1,0:T(8,128)(2,1)S(1)}, bf16[4,528,128]{2,1,0:T(8,128)(2,1)S(1)}, u32[]{:S(2)}, u32[]{:S(2)}) collective-permute-start(bf16[4,528,128]{2,1,0:T(8,128)(2,1)S(1)} %constant_dynamic-update-slice_fusion.refs_1_), channel_id=1, source_target_pairs={{0,96},{1,97},{2,386},{3,131},{16,48},{17,49},{18,402},{19,147},{3... | collective-permute-start | bytes 1622024 | tf_op jit(solution)/shard_map/ppermute | solution.py:314
  55.6 0.0 all-to-all-done.1
  55.6 2.7 %attend.3 = (f32[2,2048,256]{2,1,0:T(8,128)S(1)}, f32[2,2048,128]{2,1,0:T(8,128)S(1)}) custom-call(bf16[16,2,128,128]{3,2,1,0:T(8,128)(2,1)S(1)} %bitcast.12, bf16[4,528,128]{2,1,0:T(8,128)(2,1)S(1)} %constant_dynamic-update-slice_fusion.refs_1_), custom_call_target="tpu_custom_call" | custom-call | flops 2147483648 | bytes 8388608 | tf_op jit(solution)/shard_map/attend/pallas_call | solution.py:251
  58.3 2.3 %collective-permute-done.3.refs_1_ = bf16[4,528,128]{2,1,0:T(8,128)(2,1)S(1)} collective-permute-done((bf16[4,528,128]{2,1,0:T(8,128)(2,1)S(1)}, bf16[4,528,128]{2,1,0:T(8,128)(2,1)S(1)}, u32[]{:S(2)}, u32[]{:S(2)}) %collective-permute-start.3) | collective-permute-done | bytes 540704 | tf_op jit(solution)/shard_map/ppermute | solution.py:313
  60.5 7.6 %collective-permute-start.4 = (bf16[4,528,128]{2,1,0:T(8,128)(2,1)S(1)}, bf16[4,528,128]{2,1,0:T(8,128)(2,1)S(1)}, u32[]{:S(2)}, u32[]{:S(2)}) collective-permute-start(bf16[4,528,128]{2,1,0:T(8,128)(2,1)S(1)} %collective-permute-done.3.refs_1_), channel_id=1, source_target_pairs={{0,32},{1,33},{2,130},{3,387},{16,112},{17,113},{18,146},{19,403},... | collective-permute-start | bytes 1622024 | tf_op jit(solution)/shard_map/ppermute | solution.py:317
  68.1 0.0 collective-permute-done.5.refs_2_
  68.1 5.5 %attend.4 = (f32[2,2048,256]{2,1,0:T(8,128)S(1)}, f32[2,2048,128]{2,1,0:T(8,128)S(1)}) custom-call(bf16[16,2,128,128]{3,2,1,0:T(8,128)(2,1)S(1)} %bitcast.13, bf16[4,528,128]{2,1,0:T(8,128)(2,1)S(1)} %collective-permute-done.3.refs_1_, bf16[4,528,128]{2,1,0:T(8,128)(2,1)S(1)} %collective-permute-done.5.refs_2_, ...), custom_call_target="tpu_custom_call" | custom-call | flops 4294967296 | bytes 8388608 | tf_op jit(solution)/shard_map/attend/pallas_call | solution.py:251
  73.7 3.5 %collective-permute-done.4.refs_1_ = bf16[4,528,128]{2,1,0:T(8,128)(2,1)S(1)} collective-permute-done((bf16[4,528,128]{2,1,0:T(8,128)(2,1)S(1)}, bf16[4,528,128]{2,1,0:T(8,128)(2,1)S(1)}, u32[]{:S(2)}, u32[]{:S(2)}) %collective-permute-start.4) | collective-permute-done | bytes 540704 | tf_op jit(solution)/shard_map/ppermute | solution.py:317
  77.2 3.2 %attend.5 = bf16[16,2,128,128]{3,2,1,0:T(8,128)(2,1)S(1)} custom-call(bf16[16,2,128,128]{3,2,1,0:T(8,128)(2,1)S(1)} %bitcast.14, bf16[4,528,128]{2,1,0:T(8,128)(2,1)S(1)} %collective-permute-done.4.refs_1_, f32[2,2048,256]{2,1,0:T(8,128)S(1)} %get-tuple-element.25.refs_2_, f32[2,2048,128]{2,1,0:T(8,128)S(1)} %get-tuple-element.26.refs_3_), custom_call_target="tpu_custom_call" | custom-call | flops 2147483648 | bytes 8388608 | tf_op jit(solution)/shard_map/attend/pallas_call | solution.py:251
  80.4 23.1 %all_to_all.15 = bf16[32,128,128]{2,1,0:T(8,128)(2,1)S(1)} all-to-all(bf16[32,128,128]{2,1,0:T(8,128)(2,1)S(1)} %bitcast.15), channel_id=1, replica_groups=mesh['zh'=4,'yA'=4,'yB'=2,'x'=4,'core'=2,'rep'=2] {'yB','x','core'}, dimensions={0} | all-to-all | bytes 2097152 | tf_op jit(solution)/shard_map/all_to_all | solution.py:320
  103.5 1.1 %copy_bitcast_fusion = bf16[128,4096]{1,0:T(8,128)(2,1)} fusion(bf16[32,128,128]{2,1,0:T(8,128)(2,1)S(1)} %all_to_all.15), kind=kLoop, calls=%fused_computation | loop fusion | bytes 2097152 | tf_op jit(solution)/shard_map/reshape | solution.py:323
  (3 shorter events, 0.1 us)
Async XLA Ops:
  3.1 16.7 %all-to-all-start = ((bf16[16,40,128]{2,1,0:T(8,128)(2,1)}), bf16[16,40,128]{2,1,0:T(8,128)(2,1)S(1)}, u32[]{:S(2)}, u32[]{:S(2)}) async-start(bf16[16,40,128]{2,1,0:T(8,128)(2,1)} %prepare_merged.1), calls=%async_computation | async-start | bytes 327680 | tf_op jit(solution)/shard_map/all_to_all | solution.py:306
  19.8 0.7 copy-start
  22.1 33.6 %all-to-all-start.1 = ((bf16[32,128,128]{2,1,0:T(8,128)(2,1)}), bf16[32,128,128]{2,1,0:T(8,128)(2,1)S(1)}, u32[]{:S(2)}, u32[]{:S(2)}) async-start(bf16[32,128,128]{2,1,0:T(8,128)(2,1)} %prepare_queries.1), calls=%async_computation.1 | async-start | bytes 2097152 | tf_op jit(solution)/shard_map/all_to_all | solution.py:310
  26.2 15.3 %collective-permute-start = (bf16[1,528,128]{2,1,0:T(8,128)(2,1)}, bf16[1,528,128]{2,1,0:T(8,128)(2,1)S(1)}, u32[]{:S(2)}, u32[]{:S(2)}) collective-permute-start(bf16[1,528,128]{2,1,0:T(8,128)(2,1)} %repack.1), channel_id=1, source_target_pairs={{0,128},{1,385},{2,34},{3,35},{16,144},{17,401},{18,114},{19,115},... | collective-permute-start | bytes 405512 | tf_op jit(solution)/shard_map/ppermute | solution.py:312
  28.2 17.6 %collective-permute-start.2 = (bf16[1,528,128]{2,1,0:T(8,128)(2,1)}, bf16[1,528,128]{2,1,0:T(8,128)(2,1)S(1)}, u32[]{:S(2)}, u32[]{:S(2)}) collective-permute-start(bf16[1,528,128]{2,1,0:T(8,128)(2,1)} %repack.1), channel_id=1, source_target_pairs={{0,256},{1,257},{2,66},{3,67},{16,272},{17,273},{18,82},{19,83},{3... | collective-permute-start | bytes 405512 | tf_op jit(solution)/shard_map/ppermute | solution.py:312
  31.8 11.4 %collective-permute-start.1 = (bf16[1,528,128]{2,1,0:T(8,128)(2,1)}, bf16[1,528,128]{2,1,0:T(8,128)(2,1)S(1)}, u32[]{:S(2)}, u32[]{:S(2)}) collective-permute-start(bf16[1,528,128]{2,1,0:T(8,128)(2,1)} %repack.1), channel_id=1, source_target_pairs={{0,384},{1,129},{2,98},{3,99},{16,400},{17,145},{18,50},{19,51},{3... | collective-permute-start | bytes 405512 | tf_op jit(solution)/shard_map/ppermute | solution.py:312
  45.7 14.8 %collective-permute-start.3 = (bf16[4,528,128]{2,1,0:T(8,128)(2,1)S(1)}, bf16[4,528,128]{2,1,0:T(8,128)(2,1)S(1)}, u32[]{:S(2)}, u32[]{:S(2)}) collective-permute-start(bf16[4,528,128]{2,1,0:T(8,128)(2,1)S(1)} %constant_dynamic-update-slice_fusion.refs_1_), channel_id=1, source_target_pairs={{0,32},{1,33},{2,130},{3,387},{16,112},{17,113},{18,146},{19,403},... | collective-permute-start | bytes 1622024 | tf_op jit(solution)/shard_map/ppermute | solution.py:313
  48.8 19.3 %collective-permute-start.5 = (bf16[4,528,128]{2,1,0:T(8,128)(2,1)S(1)}, bf16[4,528,128]{2,1,0:T(8,128)(2,1)S(1)}, u32[]{:S(2)}, u32[]{:S(2)}) collective-permute-start(bf16[4,528,128]{2,1,0:T(8,128)(2,1)S(1)} %constant_dynamic-update-slice_fusion.refs_1_), channel_id=1, source_target_pairs={{0,96},{1,97},{2,386},{3,131},{16,48},{17,49},{18,402},{19,147},{3... | collective-permute-start | bytes 1622024 | tf_op jit(solution)/shard_map/ppermute | solution.py:314
  60.5 16.6 %collective-permute-start.4 = (bf16[4,528,128]{2,1,0:T(8,128)(2,1)S(1)}, bf16[4,528,128]{2,1,0:T(8,128)(2,1)S(1)}, u32[]{:S(2)}, u32[]{:S(2)}) collective-permute-start(bf16[4,528,128]{2,1,0:T(8,128)(2,1)S(1)} %collective-permute-done.3.refs_1_), channel_id=1, source_target_pairs={{0,32},{1,33},{2,130},{3,387},{16,112},{17,113},{18,146},{19,403},... | collective-permute-start | bytes 1622024 | tf_op jit(solution)/shard_map/ppermute | solution.py:317

commit v5 on v4

--- a/solution.py
+++ b/solution.py
@@ -103,7 +103,7 @@
         lambda *refs: prepare_merged_kernel(chunks, *refs),
         in_specs=[pl.BlockSpec(memory_space=pl.ANY)] * 5,
         out_specs=pl.BlockSpec(memory_space=pltpu.VMEM),
-        out_shape=jax.ShapeDtypeStruct((targets, rows, HD), jnp.bfloat16),
+        out_shape=pltpu.VMEM((targets, rows, HD), jnp.bfloat16),
         scratch_shapes=[
             pltpu.VMEM((2 * heads * MERGED, HD), jnp.float32),
             pltpu.VMEM((2, *key.shape), jnp.bfloat16),
@@ -144,7 +144,7 @@
         lambda *refs: prepare_queries_kernel(chunks, *refs),
         in_specs=[pl.BlockSpec(memory_space=pl.ANY)] * 2,
         out_specs=pl.BlockSpec(memory_space=pltpu.VMEM),
-        out_shape=jax.ShapeDtypeStruct((heads, tokens, HD), jnp.bfloat16),
+        out_shape=pltpu.VMEM((heads, tokens, HD), jnp.bfloat16),
         scratch_shapes=[
             pltpu.VMEM(query.shape, jnp.bfloat16),
             pltpu.VMEM(query_exp.shape, jnp.int32),
@@ -174,6 +174,7 @@
     return pl.pallas_call(
         repack_kernel,
         out_shape=jax.ShapeDtypeStruct((1, (height // MERGED - 1) * rows + 16, HD), jnp.bfloat16),
+        compiler_params=pltpu.CompilerParams(vmem_limit_bytes=4 * 2**20),
         cost_estimate=pl.CostEstimate(flops=2**20, bytes_accessed=2**18, transcendentals=0),
         name="repack",
     )(received)

time: 105 us -> 103 us (0.981)
  local copies, waits for them, and re-layouts: 2.77 us -> 1.19 us
  Pallas kernels: 18.8 us -> 17.3 us
    unnamed x5 -> x3, local copies, waits for them, and re-layouts: 1.63 us -> 0.05 us
    pallas_call x1, Pallas kernels: 1.6 us -> 0.04 us  [repack(): pl.pallas_call(repack_kernel, out_shape=jax.ShapeDtypeStruct((1, (height...]
  transfers between devices with their start and end apart: 8 -> 8, of which waited for: 6 -> 6; matrix products, arithmetic and copies ran while one was open for 1% -> 0% of each run, Pallas kernels for 11% -> 11%
where the time goes in v5:
time: 103 us; the launch traced here: 102 us
  starting transfers between devices  42.3 us (41%)
  blocking collectives  23.2 us (23%)
  waiting for transfers between devices  18.3 us (18%)
  Pallas kernels  17.3 us (17%)
  local copies, waits for them, and re-layouts  1.19 us (1%)
    all_to_all x1, blocking collectives, per_device(): lax.all_to_all(attended.reshape(heads, tokens, HD), GROUP, split_axis=0,...  23.2 us
    pallas_call x3, Pallas kernels, attend(): pl.pallas_call(lambda *refs: attend_kernel(parts, first, last, sub, *refs...  11.4 us
    ppermute x3, starting transfers between devices, per_device(): lax.ppermute(own, RING, first_ring(by))  10.5 us
    all_to_all x1, starting transfers between devices, per_device(): lax.all_to_all(merged, GROUP, split_axis=0, concat_axis=0, tiled=True)  10.2 us
    ppermute x3, waiting for transfers between devices, per_device(): lax.ppermute(own, RING, first_ring(by))  8.89 us
    ppermute x1, starting transfers between devices, per_device(): far = lax.ppermute(up, RING, second_ring(1))  7.58 us
    ppermute x1, starting transfers between devices, per_device(): down = lax.ppermute(near, RING, second_ring(-1))  6.77 us
    all_to_all x1, starting transfers between devices, per_device(): lax.all_to_all(queries, GROUP, split_axis=0, concat_axis=0, tiled=True)  4.19 us
  transfers between devices with their start and end apart: 8, of which 6 were waited for; matrix products, arithmetic and copies ran while one was open for 0% of the time, Pallas kernels for 11%

profile of v5, /device:TPU:1, one launch (start us, length us, event | category | flops | bytes accessed | tf_op | source)
XLA Modules:
  0.0 102.5 jit_solution(13589928654888113504)
XLA Ops:
  0.0 3.1 %prepare_merged.1 = bf16[16,40,128]{2,1,0:T(8,128)(2,1)} custom-call(bf16[128,4096]{1,0:T(8,128)(2,1)} %refs_0_.2, bf16[128,4096]{1,0:T(8,128)(2,1)} %refs_1_.1, s32[32,128]{1,0:T(8,128)} %bitcast.16, s32[32,128]{1,0:T(8,128)} %bitcast.17, s32[1,128]{1,0:T(1,128)} %bitcast.19), custom_call_target="tpu_custom_call" | custom-call | flops 134217728 | bytes 2097152 | tf_op jit(solution)/shard_map/prepare_merged/pallas_call | solution.py:102
  3.1 10.2 %all-to-all-start = ((bf16[16,40,128]{2,1,0:T(8,128)(2,1)}), bf16[16,40,128]{2,1,0:T(8,128)(2,1)S(1)}, u32[]{:S(2)}, u32[]{:S(2)}) async-start(bf16[16,40,128]{2,1,0:T(8,128)(2,1)} %prepare_merged.1), calls=%async_computation | async-start | bytes 327680 | tf_op jit(solution)/shard_map/all_to_all | solution.py:307
  13.3 2.8 %prepare_queries.1 = bf16[32,128,128]{2,1,0:T(8,128)(2,1)} custom-call(bf16[128,4096]{1,0:T(8,128)(2,1)} %refs_0_.3, s32[32,128]{1,0:T(8,128)} %bitcast.18), custom_call_target="tpu_custom_call" | custom-call | flops 134217728 | bytes 2097152 | tf_op jit(solution)/shard_map/prepare_queries/pallas_call | solution.py:143
  16.1 3.7 %all-to-all-done.in_ref = bf16[16,40,128]{2,1,0:T(8,128)(2,1)S(1)} async-done(((bf16[16,40,128]{2,1,0:T(8,128)(2,1)}), bf16[16,40,128]{2,1,0:T(8,128)(2,1)S(1)}, u32[]{:S(2)}, u32[]{:S(2)}) %all-to-all-start) | async-done | bytes 163872 | tf_op jit(solution)/shard_map/all_to_all | solution.py:307
  19.8 4.2 %all-to-all-start.1 = ((bf16[32,128,128]{2,1,0:T(8,128)(2,1)}), bf16[32,128,128]{2,1,0:T(8,128)(2,1)S(1)}, u32[]{:S(2)}, u32[]{:S(2)}) async-start(bf16[32,128,128]{2,1,0:T(8,128)(2,1)} %prepare_queries.1), calls=%async_computation.1 | async-start | bytes 2097152 | tf_op jit(solution)/shard_map/all_to_all | solution.py:311
  24.0 1.9 %collective-permute-start = (bf16[1,528,128]{2,1,0:T(8,128)(2,1)S(1)}, bf16[1,528,128]{2,1,0:T(8,128)(2,1)S(1)}, u32[]{:S(2)}, u32[]{:S(2)}) collective-permute-start(bf16[1,528,128]{2,1,0:T(8,128)(2,1)S(1)} %repack.1), channel_id=1, source_target_pairs={{0,128},{1,385},{2,34},{3,35},{16,144},{17,401},{18,114},{19,115},... | collective-permute-start | bytes 405512 | tf_op jit(solution)/shard_map/ppermute | solution.py:313
  25.9 3.6 %collective-permute-start.2 = (bf16[1,528,128]{2,1,0:T(8,128)(2,1)S(1)}, bf16[1,528,128]{2,1,0:T(8,128)(2,1)S(1)}, u32[]{:S(2)}, u32[]{:S(2)}) collective-permute-start(bf16[1,528,128]{2,1,0:T(8,128)(2,1)S(1)} %repack.1), channel_id=1, source_target_pairs={{0,256},{1,257},{2,66},{3,67},{16,272},{17,273},{18,82},{19,83},{3... | collective-permute-start | bytes 405512 | tf_op jit(solution)/shard_map/ppermute | solution.py:313
  29.6 5.0 %collective-permute-start.1 = (bf16[1,528,128]{2,1,0:T(8,128)(2,1)S(1)}, bf16[1,528,128]{2,1,0:T(8,128)(2,1)S(1)}, u32[]{:S(2)}, u32[]{:S(2)}) collective-permute-start(bf16[1,528,128]{2,1,0:T(8,128)(2,1)S(1)} %repack.1), channel_id=1, source_target_pairs={{0,384},{1,129},{2,98},{3,99},{16,400},{17,145},{18,50},{19,51},{3... | collective-permute-start | bytes 405512 | tf_op jit(solution)/shard_map/ppermute | solution.py:313
  34.6 4.6 %collective-permute-done = bf16[1,528,128]{2,1,0:T(8,128)(2,1)S(1)} collective-permute-done((bf16[1,528,128]{2,1,0:T(8,128)(2,1)S(1)}, bf16[1,528,128]{2,1,0:T(8,128)(2,1)S(1)}, u32[]{:S(2)}, u32[]{:S(2)}) %collective-permute-start) | collective-permute-done | bytes 135200 | tf_op jit(solution)/shard_map/ppermute | solution.py:313
  39.2 1.7 %collective-permute-done.1 = bf16[1,528,128]{2,1,0:T(8,128)(2,1)S(1)} collective-permute-done((bf16[1,528,128]{2,1,0:T(8,128)(2,1)S(1)}, bf16[1,528,128]{2,1,0:T(8,128)(2,1)S(1)}, u32[]{:S(2)}, u32[]{:S(2)}) %collective-permute-start.1) | collective-permute-done | bytes 135200 | tf_op jit(solution)/shard_map/ppermute | solution.py:313
  40.9 2.6 %collective-permute-done.2 = bf16[1,528,128]{2,1,0:T(8,128)(2,1)S(1)} collective-permute-done((bf16[1,528,128]{2,1,0:T(8,128)(2,1)S(1)}, bf16[1,528,128]{2,1,0:T(8,128)(2,1)S(1)}, u32[]{:S(2)}, u32[]{:S(2)}) %collective-permute-start.2) | collective-permute-done | bytes 135200 | tf_op jit(solution)/shard_map/ppermute | solution.py:313
  43.5 3.1 %collective-permute-start.3 = (bf16[4,528,128]{2,1,0:T(8,128)(2,1)S(1)}, bf16[4,528,128]{2,1,0:T(8,128)(2,1)S(1)}, u32[]{:S(2)}, u32[]{:S(2)}) collective-permute-start(bf16[4,528,128]{2,1,0:T(8,128)(2,1)S(1)} %constant_dynamic-update-slice_fusion.refs_1_), channel_id=1, source_target_pairs={{0,32},{1,33},{2,130},{3,387},{16,112},{17,113},{18,146},{19,403},... | collective-permute-start | bytes 1622024 | tf_op jit(solution)/shard_map/ppermute | solution.py:314
  46.6 6.8 %collective-permute-start.5 = (bf16[4,528,128]{2,1,0:T(8,128)(2,1)S(1)}, bf16[4,528,128]{2,1,0:T(8,128)(2,1)S(1)}, u32[]{:S(2)}, u32[]{:S(2)}) collective-permute-start(bf16[4,528,128]{2,1,0:T(8,128)(2,1)S(1)} %constant_dynamic-update-slice_fusion.refs_1_), channel_id=1, source_target_pairs={{0,96},{1,97},{2,386},{3,131},{16,48},{17,49},{18,402},{19,147},{3... | collective-permute-start | bytes 1622024 | tf_op jit(solution)/shard_map/ppermute | solution.py:315
  53.4 0.0 all-to-all-done.1
  53.4 2.7 %attend.3 = (f32[2,2048,256]{2,1,0:T(8,128)S(1)}, f32[2,2048,128]{2,1,0:T(8,128)S(1)}) custom-call(bf16[16,2,128,128]{3,2,1,0:T(8,128)(2,1)S(1)} %bitcast.12, bf16[4,528,128]{2,1,0:T(8,128)(2,1)S(1)} %constant_dynamic-update-slice_fusion.refs_1_), custom_call_target="tpu_custom_call" | custom-call | flops 2147483648 | bytes 8388608 | tf_op jit(solution)/shard_map/attend/pallas_call | solution.py:252
  56.1 2.2 %collective-permute-done.3.refs_1_ = bf16[4,528,128]{2,1,0:T(8,128)(2,1)S(1)} collective-permute-done((bf16[4,528,128]{2,1,0:T(8,128)(2,1)S(1)}, bf16[4,528,128]{2,1,0:T(8,128)(2,1)S(1)}, u32[]{:S(2)}, u32[]{:S(2)}) %collective-permute-start.3) | collective-permute-done | bytes 540704 | tf_op jit(solution)/shard_map/ppermute | solution.py:314
  58.3 7.6 %collective-permute-start.4 = (bf16[4,528,128]{2,1,0:T(8,128)(2,1)S(1)}, bf16[4,528,128]{2,1,0:T(8,128)(2,1)S(1)}, u32[]{:S(2)}, u32[]{:S(2)}) collective-permute-start(bf16[4,528,128]{2,1,0:T(8,128)(2,1)S(1)} %collective-permute-done.3.refs_1_), channel_id=1, source_target_pairs={{0,32},{1,33},{2,130},{3,387},{16,112},{17,113},{18,146},{19,403},... | collective-permute-start | bytes 1622024 | tf_op jit(solution)/shard_map/ppermute | solution.py:318
  65.9 0.0 collective-permute-done.5.refs_2_
  65.9 5.6 %attend.4 = (f32[2,2048,256]{2,1,0:T(8,128)S(1)}, f32[2,2048,128]{2,1,0:T(8,128)S(1)}) custom-call(bf16[16,2,128,128]{3,2,1,0:T(8,128)(2,1)S(1)} %bitcast.13, bf16[4,528,128]{2,1,0:T(8,128)(2,1)S(1)} %collective-permute-done.3.refs_1_, bf16[4,528,128]{2,1,0:T(8,128)(2,1)S(1)} %collective-permute-done.5.refs_2_, ...), custom_call_target="tpu_custom_call" | custom-call | flops 4294967296 | bytes 8388608 | tf_op jit(solution)/shard_map/attend/pallas_call | solution.py:252
  71.5 3.5 %collective-permute-done.4.refs_1_ = bf16[4,528,128]{2,1,0:T(8,128)(2,1)S(1)} collective-permute-done((bf16[4,528,128]{2,1,0:T(8,128)(2,1)S(1)}, bf16[4,528,128]{2,1,0:T(8,128)(2,1)S(1)}, u32[]{:S(2)}, u32[]{:S(2)}) %collective-permute-start.4) | collective-permute-done | bytes 540704 | tf_op jit(solution)/shard_map/ppermute | solution.py:318
  75.0 3.2 %attend.5 = bf16[16,2,128,128]{3,2,1,0:T(8,128)(2,1)S(1)} custom-call(bf16[16,2,128,128]{3,2,1,0:T(8,128)(2,1)S(1)} %bitcast.14, bf16[4,528,128]{2,1,0:T(8,128)(2,1)S(1)} %collective-permute-done.4.refs_1_, f32[2,2048,256]{2,1,0:T(8,128)S(1)} %get-tuple-element.25.refs_2_, f32[2,2048,128]{2,1,0:T(8,128)S(1)} %get-tuple-element.26.refs_3_), custom_call_target="tpu_custom_call" | custom-call | flops 2147483648 | bytes 8388608 | tf_op jit(solution)/shard_map/attend/pallas_call | solution.py:252
  78.1 23.2 %all_to_all.15 = bf16[32,128,128]{2,1,0:T(8,128)(2,1)S(1)} all-to-all(bf16[32,128,128]{2,1,0:T(8,128)(2,1)S(1)} %bitcast.15), channel_id=1, replica_groups=mesh['zh'=4,'yA'=4,'yB'=2,'x'=4,'core'=2,'rep'=2] {'yB','x','core'}, dimensions={0} | all-to-all | bytes 2097152 | tf_op jit(solution)/shard_map/all_to_all | solution.py:321
  101.4 1.1 %copy_bitcast_fusion = bf16[128,4096]{1,0:T(8,128)(2,1)} fusion(bf16[32,128,128]{2,1,0:T(8,128)(2,1)S(1)} %all_to_all.15), kind=kLoop, calls=%fused_computation | loop fusion | bytes 2097152 | tf_op jit(solution)/shard_map/reshape | solution.py:324
  (5 shorter events, 0.1 us)
Async XLA Ops:
  3.1 16.7 %all-to-all-start = ((bf16[16,40,128]{2,1,0:T(8,128)(2,1)}), bf16[16,40,128]{2,1,0:T(8,128)(2,1)S(1)}, u32[]{:S(2)}, u32[]{:S(2)}) async-start(bf16[16,40,128]{2,1,0:T(8,128)(2,1)} %prepare_merged.1), calls=%async_computation | async-start | bytes 327680 | tf_op jit(solution)/shard_map/all_to_all | solution.py:307
  19.8 33.6 %all-to-all-start.1 = ((bf16[32,128,128]{2,1,0:T(8,128)(2,1)}), bf16[32,128,128]{2,1,0:T(8,128)(2,1)S(1)}, u32[]{:S(2)}, u32[]{:S(2)}) async-start(bf16[32,128,128]{2,1,0:T(8,128)(2,1)} %prepare_queries.1), calls=%async_computation.1 | async-start | bytes 2097152 | tf_op jit(solution)/shard_map/all_to_all | solution.py:311
  24.0 15.2 %collective-permute-start = (bf16[1,528,128]{2,1,0:T(8,128)(2,1)S(1)}, bf16[1,528,128]{2,1,0:T(8,128)(2,1)S(1)}, u32[]{:S(2)}, u32[]{:S(2)}) collective-permute-start(bf16[1,528,128]{2,1,0:T(8,128)(2,1)S(1)} %repack.1), channel_id=1, source_target_pairs={{0,128},{1,385},{2,34},{3,35},{16,144},{17,401},{18,114},{19,115},... | collective-permute-start | bytes 405512 | tf_op jit(solution)/shard_map/ppermute | solution.py:313
  25.9 17.6 %collective-permute-start.2 = (bf16[1,528,128]{2,1,0:T(8,128)(2,1)S(1)}, bf16[1,528,128]{2,1,0:T(8,128)(2,1)S(1)}, u32[]{:S(2)}, u32[]{:S(2)}) collective-permute-start(bf16[1,528,128]{2,1,0:T(8,128)(2,1)S(1)} %repack.1), channel_id=1, source_target_pairs={{0,256},{1,257},{2,66},{3,67},{16,272},{17,273},{18,82},{19,83},{3... | collective-permute-start | bytes 405512 | tf_op jit(solution)/shard_map/ppermute | solution.py:313
  29.6 11.3 %collective-permute-start.1 = (bf16[1,528,128]{2,1,0:T(8,128)(2,1)S(1)}, bf16[1,528,128]{2,1,0:T(8,128)(2,1)S(1)}, u32[]{:S(2)}, u32[]{:S(2)}) collective-permute-start(bf16[1,528,128]{2,1,0:T(8,128)(2,1)S(1)} %repack.1), channel_id=1, source_target_pairs={{0,384},{1,129},{2,98},{3,99},{16,400},{17,145},{18,50},{19,51},{3... | collective-permute-start | bytes 405512 | tf_op jit(solution)/shard_map/ppermute | solution.py:313
  43.5 14.8 %collective-permute-start.3 = (bf16[4,528,128]{2,1,0:T(8,128)(2,1)S(1)}, bf16[4,528,128]{2,1,0:T(8,128)(2,1)S(1)}, u32[]{:S(2)}, u32[]{:S(2)}) collective-permute-start(bf16[4,528,128]{2,1,0:T(8,128)(2,1)S(1)} %constant_dynamic-update-slice_fusion.refs_1_), channel_id=1, source_target_pairs={{0,32},{1,33},{2,130},{3,387},{16,112},{17,113},{18,146},{19,403},... | collective-permute-start | bytes 1622024 | tf_op jit(solution)/shard_map/ppermute | solution.py:314
  46.6 19.3 %collective-permute-start.5 = (bf16[4,528,128]{2,1,0:T(8,128)(2,1)S(1)}, bf16[4,528,128]{2,1,0:T(8,128)(2,1)S(1)}, u32[]{:S(2)}, u32[]{:S(2)}) collective-permute-start(bf16[4,528,128]{2,1,0:T(8,128)(2,1)S(1)} %constant_dynamic-update-slice_fusion.refs_1_), channel_id=1, source_target_pairs={{0,96},{1,97},{2,386},{3,131},{16,48},{17,49},{18,402},{19,147},{3... | collective-permute-start | bytes 1622024 | tf_op jit(solution)/shard_map/ppermute | solution.py:315
  58.3 16.6 %collective-permute-start.4 = (bf16[4,528,128]{2,1,0:T(8,128)(2,1)S(1)}, bf16[4,528,128]{2,1,0:T(8,128)(2,1)S(1)}, u32[]{:S(2)}, u32[]{:S(2)}) collective-permute-start(bf16[4,528,128]{2,1,0:T(8,128)(2,1)S(1)} %collective-permute-done.3.refs_1_), channel_id=1, source_target_pairs={{0,32},{1,33},{2,130},{3,387},{16,112},{17,113},{18,146},{19,403},... | collective-permute-start | bytes 1622024 | tf_op jit(solution)/shard_map/ppermute | solution.py:318

commit v6 on v5

--- a/solution.py
+++ b/solution.py
@@ -310,7 +310,7 @@
     queries, own = lax.optimization_barrier((queries, own))
     head_queries = lax.all_to_all(queries, GROUP, split_axis=0, concat_axis=0, tiled=True)
     head_queries = head_queries.reshape(targets, heads // targets, tokens, HD)
-    near = jnp.concatenate([own] + [lax.ppermute(own, RING, first_ring(by)) for by in (1, -1, 2)], axis=0)
+    near = jnp.concatenate([own] + [lax.ppermute(own, RING, first_ring(by)) for by in (2, -1, 1)], axis=0)
     up = lax.ppermute(near, RING, second_ring(1))
     down = lax.ppermute(near, RING, second_ring(-1))
     state = attend(head_queries, (near,), None, False)

time: 103 us -> 102 us (level)
  starting transfers between devices: 42.3 us -> 44.9 us
  blocking collectives: 23.2 us -> 20.7 us
  waiting for transfers between devices: 18.3 us -> 17.2 us
    all_to_all x1, blocking collectives: 23.2 us -> 20.7 us  [per_device(): lax.all_to_all(attended.reshape(heads, tokens, HD), GROUP, split_axis=0,...]
    ppermute x1, starting transfers between devices: 3.07 us -> 5.62 us  [per_device(): up = lax.ppermute(near, RING, second_ring(1))]
    ppermute x3, waiting for transfers between devices: 8.89 us -> 7.49 us  [per_device(): lax.ppermute(own, RING, first_ring(by))]
  transfers between devices with their start and end apart: 8 -> 8, of which waited for: 6 -> 4; matrix products, arithmetic and copies ran while one was open for 0% -> 0% of each run, Pallas kernels for 11% -> 11%
where the time goes in v6:
time: 102 us; the launch traced here: 101 us
  starting transfers between devices  44.9 us (44%)
  blocking collectives  20.7 us (20%)
  Pallas kernels  17.3 us (17%)
  waiting for transfers between devices  17.2 us (17%)
  local copies, waits for them, and re-layouts  1.19 us (1%)
    all_to_all x1, blocking collectives, per_device(): lax.all_to_all(attended.reshape(heads, tokens, HD), GROUP, split_axis=0,...  20.7 us
    pallas_call x3, Pallas kernels, attend(): pl.pallas_call(lambda *refs: attend_kernel(parts, first, last, sub, *refs...  11.4 us
    ppermute x3, starting transfers between devices, per_device(): lax.ppermute(own, RING, first_ring(by))  10.5 us
    all_to_all x1, starting transfers between devices, per_device(): lax.all_to_all(merged, GROUP, split_axis=0, concat_axis=0, tiled=True)  10.2 us
    ppermute x1, starting transfers between devices, per_device(): far = lax.ppermute(up, RING, second_ring(1))  7.58 us
    ppermute x3, waiting for transfers between devices, per_device(): lax.ppermute(own, RING, first_ring(by))  7.49 us
    ppermute x1, starting transfers between devices, per_device(): down = lax.ppermute(near, RING, second_ring(-1))  6.77 us
    ppermute x1, starting transfers between devices, per_device(): up = lax.ppermute(near, RING, second_ring(1))  5.62 us
  transfers between devices with their start and end apart: 8, of which 4 were waited for; matrix products, arithmetic and copies ran while one was open for 0% of the time, Pallas kernels for 11%

profile of v6, /device:TPU:1, one launch (start us, length us, event | category | flops | bytes accessed | tf_op | source)
XLA Modules:
  0.0 101.4 jit_solution(12801592302446991291)
XLA Ops:
  0.0 3.1 %prepare_merged.1 = bf16[16,40,128]{2,1,0:T(8,128)(2,1)} custom-call(bf16[128,4096]{1,0:T(8,128)(2,1)} %refs_0_.2, bf16[128,4096]{1,0:T(8,128)(2,1)} %refs_1_.1, s32[32,128]{1,0:T(8,128)} %bitcast.16, s32[32,128]{1,0:T(8,128)} %bitcast.17, s32[1,128]{1,0:T(1,128)} %bitcast.19), custom_call_target="tpu_custom_call" | custom-call | flops 134217728 | bytes 2097152 | tf_op jit(solution)/shard_map/prepare_merged/pallas_call | solution.py:102
  3.1 10.2 %all-to-all-start = ((bf16[16,40,128]{2,1,0:T(8,128)(2,1)}), bf16[16,40,128]{2,1,0:T(8,128)(2,1)S(1)}, u32[]{:S(2)}, u32[]{:S(2)}) async-start(bf16[16,40,128]{2,1,0:T(8,128)(2,1)} %prepare_merged.1), calls=%async_computation | async-start | bytes 327680 | tf_op jit(solution)/shard_map/all_to_all | solution.py:307
  13.3 2.8 %prepare_queries.1 = bf16[32,128,128]{2,1,0:T(8,128)(2,1)} custom-call(bf16[128,4096]{1,0:T(8,128)(2,1)} %refs_0_.3, s32[32,128]{1,0:T(8,128)} %bitcast.18), custom_call_target="tpu_custom_call" | custom-call | flops 134217728 | bytes 2097152 | tf_op jit(solution)/shard_map/prepare_queries/pallas_call | solution.py:143
  16.1 3.7 %all-to-all-done.in_ref = bf16[16,40,128]{2,1,0:T(8,128)(2,1)S(1)} async-done(((bf16[16,40,128]{2,1,0:T(8,128)(2,1)}), bf16[16,40,128]{2,1,0:T(8,128)(2,1)S(1)}, u32[]{:S(2)}, u32[]{:S(2)}) %all-to-all-start) | async-done | bytes 163872 | tf_op jit(solution)/shard_map/all_to_all | solution.py:307
  19.8 4.2 %all-to-all-start.1 = ((bf16[32,128,128]{2,1,0:T(8,128)(2,1)}), bf16[32,128,128]{2,1,0:T(8,128)(2,1)S(1)}, u32[]{:S(2)}, u32[]{:S(2)}) async-start(bf16[32,128,128]{2,1,0:T(8,128)(2,1)} %prepare_queries.1), calls=%async_computation.1 | async-start | bytes 2097152 | tf_op jit(solution)/shard_map/all_to_all | solution.py:311
  24.0 3.1 %collective-permute-start = (bf16[1,528,128]{2,1,0:T(8,128)(2,1)S(1)}, bf16[1,528,128]{2,1,0:T(8,128)(2,1)S(1)}, u32[]{:S(2)}, u32[]{:S(2)}) collective-permute-start(bf16[1,528,128]{2,1,0:T(8,128)(2,1)S(1)} %repack.1), channel_id=1, source_target_pairs={{0,256},{1,257},{2,66},{3,67},{16,272},{17,273},{18,82},{19,83},{3... | collective-permute-start | bytes 405512 | tf_op jit(solution)/shard_map/ppermute | solution.py:313
  27.1 2.4 %collective-permute-start.2 = (bf16[1,528,128]{2,1,0:T(8,128)(2,1)S(1)}, bf16[1,528,128]{2,1,0:T(8,128)(2,1)S(1)}, u32[]{:S(2)}, u32[]{:S(2)}) collective-permute-start(bf16[1,528,128]{2,1,0:T(8,128)(2,1)S(1)} %repack.1), channel_id=1, source_target_pairs={{0,128},{1,385},{2,34},{3,35},{16,144},{17,401},{18,114},{19,115},... | collective-permute-start | bytes 405512 | tf_op jit(solution)/shard_map/ppermute | solution.py:313
  29.6 5.0 %collective-permute-start.1 = (bf16[1,528,128]{2,1,0:T(8,128)(2,1)S(1)}, bf16[1,528,128]{2,1,0:T(8,128)(2,1)S(1)}, u32[]{:S(2)}, u32[]{:S(2)}) collective-permute-start(bf16[1,528,128]{2,1,0:T(8,128)(2,1)S(1)} %repack.1), channel_id=1, source_target_pairs={{0,384},{1,129},{2,98},{3,99},{16,400},{17,145},{18,50},{19,51},{3... | collective-permute-start | bytes 405512 | tf_op jit(solution)/shard_map/ppermute | solution.py:313
  34.6 7.5 %collective-permute-done = bf16[1,528,128]{2,1,0:T(8,128)(2,1)S(1)} collective-permute-done((bf16[1,528,128]{2,1,0:T(8,128)(2,1)S(1)}, bf16[1,528,128]{2,1,0:T(8,128)(2,1)S(1)}, u32[]{:S(2)}, u32[]{:S(2)}) %collective-permute-start) | collective-permute-done | bytes 135200 | tf_op jit(solution)/shard_map/ppermute | solution.py:313
  42.1 0.0 collective-permute-done.1
  42.1 0.0 collective-permute-done.2
  42.1 5.6 %collective-permute-start.3 = (bf16[4,528,128]{2,1,0:T(8,128)(2,1)S(1)}, bf16[4,528,128]{2,1,0:T(8,128)(2,1)S(1)}, u32[]{:S(2)}, u32[]{:S(2)}) collective-permute-start(bf16[4,528,128]{2,1,0:T(8,128)(2,1)S(1)} %constant_dynamic-update-slice_fusion.refs_1_), channel_id=1, source_target_pairs={{0,32},{1,33},{2,130},{3,387},{16,112},{17,113},{18,146},{19,403},... | collective-permute-start | bytes 1622024 | tf_op jit(solution)/shard_map/ppermute | solution.py:314
  47.8 6.8 %collective-permute-start.5 = (bf16[4,528,128]{2,1,0:T(8,128)(2,1)S(1)}, bf16[4,528,128]{2,1,0:T(8,128)(2,1)S(1)}, u32[]{:S(2)}, u32[]{:S(2)}) collective-permute-start(bf16[4,528,128]{2,1,0:T(8,128)(2,1)S(1)} %constant_dynamic-update-slice_fusion.refs_1_), channel_id=1, source_target_pairs={{0,96},{1,97},{2,386},{3,131},{16,48},{17,49},{18,402},{19,147},{3... | collective-permute-start | bytes 1622024 | tf_op jit(solution)/shard_map/ppermute | solution.py:315
  54.5 0.0 all-to-all-done.1
  54.6 2.7 %attend.3 = (f32[2,2048,256]{2,1,0:T(8,128)S(1)}, f32[2,2048,128]{2,1,0:T(8,128)S(1)}) custom-call(bf16[16,2,128,128]{3,2,1,0:T(8,128)(2,1)S(1)} %bitcast.12, bf16[4,528,128]{2,1,0:T(8,128)(2,1)S(1)} %constant_dynamic-update-slice_fusion.refs_1_), custom_call_target="tpu_custom_call" | custom-call | flops 2147483648 | bytes 8388608 | tf_op jit(solution)/shard_map/attend/pallas_call | solution.py:252
  57.2 2.3 %collective-permute-done.3.refs_1_ = bf16[4,528,128]{2,1,0:T(8,128)(2,1)S(1)} collective-permute-done((bf16[4,528,128]{2,1,0:T(8,128)(2,1)S(1)}, bf16[4,528,128]{2,1,0:T(8,128)(2,1)S(1)}, u32[]{:S(2)}, u32[]{:S(2)}) %collective-permute-start.3) | collective-permute-done | bytes 540704 | tf_op jit(solution)/shard_map/ppermute | solution.py:314
  59.5 7.6 %collective-permute-start.4 = (bf16[4,528,128]{2,1,0:T(8,128)(2,1)S(1)}, bf16[4,528,128]{2,1,0:T(8,128)(2,1)S(1)}, u32[]{:S(2)}, u32[]{:S(2)}) collective-permute-start(bf16[4,528,128]{2,1,0:T(8,128)(2,1)S(1)} %collective-permute-done.3.refs_1_), channel_id=1, source_target_pairs={{0,32},{1,33},{2,130},{3,387},{16,112},{17,113},{18,146},{19,403},... | collective-permute-start | bytes 1622024 | tf_op jit(solution)/shard_map/ppermute | solution.py:318
  67.1 0.0 collective-permute-done.5.refs_2_
  67.1 5.5 %attend.4 = (f32[2,2048,256]{2,1,0:T(8,128)S(1)}, f32[2,2048,128]{2,1,0:T(8,128)S(1)}) custom-call(bf16[16,2,128,128]{3,2,1,0:T(8,128)(2,1)S(1)} %bitcast.13, bf16[4,528,128]{2,1,0:T(8,128)(2,1)S(1)} %collective-permute-done.3.refs_1_, bf16[4,528,128]{2,1,0:T(8,128)(2,1)S(1)} %collective-permute-done.5.refs_2_, ...), custom_call_target="tpu_custom_call" | custom-call | flops 4294967296 | bytes 8388608 | tf_op jit(solution)/shard_map/attend/pallas_call | solution.py:252
  72.6 3.8 %collective-permute-done.4.refs_1_ = bf16[4,528,128]{2,1,0:T(8,128)(2,1)S(1)} collective-permute-done((bf16[4,528,128]{2,1,0:T(8,128)(2,1)S(1)}, bf16[4,528,128]{2,1,0:T(8,128)(2,1)S(1)}, u32[]{:S(2)}, u32[]{:S(2)}) %collective-permute-start.4) | collective-permute-done | bytes 540704 | tf_op jit(solution)/shard_map/ppermute | solution.py:318
  76.4 3.2 %attend.5 = bf16[16,2,128,128]{3,2,1,0:T(8,128)(2,1)S(1)} custom-call(bf16[16,2,128,128]{3,2,1,0:T(8,128)(2,1)S(1)} %bitcast.14, bf16[4,528,128]{2,1,0:T(8,128)(2,1)S(1)} %collective-permute-done.4.refs_1_, f32[2,2048,256]{2,1,0:T(8,128)S(1)} %get-tuple-element.25.refs_2_, f32[2,2048,128]{2,1,0:T(8,128)S(1)} %get-tuple-element.26.refs_3_), custom_call_target="tpu_custom_call" | custom-call | flops 2147483648 | bytes 8388608 | tf_op jit(solution)/shard_map/attend/pallas_call | solution.py:252
  79.6 20.7 %all_to_all.15 = bf16[32,128,128]{2,1,0:T(8,128)(2,1)S(1)} all-to-all(bf16[32,128,128]{2,1,0:T(8,128)(2,1)S(1)} %bitcast.15), channel_id=1, replica_groups=mesh['zh'=4,'yA'=4,'yB'=2,'x'=4,'core'=2,'rep'=2] {'yB','x','core'}, dimensions={0} | all-to-all | bytes 2097152 | tf_op jit(solution)/shard_map/all_to_all | solution.py:321
  100.3 1.1 %copy_bitcast_fusion = bf16[128,4096]{1,0:T(8,128)(2,1)} fusion(bf16[32,128,128]{2,1,0:T(8,128)(2,1)S(1)} %all_to_all.15), kind=kLoop, calls=%fused_computation | loop fusion | bytes 2097152 | tf_op jit(solution)/shard_map/reshape | solution.py:324
  (5 shorter events, 0.1 us)
Async XLA Ops:
  3.1 16.7 %all-to-all-start = ((bf16[16,40,128]{2,1,0:T(8,128)(2,1)}), bf16[16,40,128]{2,1,0:T(8,128)(2,1)S(1)}, u32[]{:S(2)}, u32[]{:S(2)}) async-start(bf16[16,40,128]{2,1,0:T(8,128)(2,1)} %prepare_merged.1), calls=%async_computation | async-start | bytes 327680 | tf_op jit(solution)/shard_map/all_to_all | solution.py:307
  19.8 34.7 %all-to-all-start.1 = ((bf16[32,128,128]{2,1,0:T(8,128)(2,1)}), bf16[32,128,128]{2,1,0:T(8,128)(2,1)S(1)}, u32[]{:S(2)}, u32[]{:S(2)}) async-start(bf16[32,128,128]{2,1,0:T(8,128)(2,1)} %prepare_queries.1), calls=%async_computation.1 | async-start | bytes 2097152 | tf_op jit(solution)/shard_map/all_to_all | solution.py:311
  24.0 18.0 %collective-permute-start = (bf16[1,528,128]{2,1,0:T(8,128)(2,1)S(1)}, bf16[1,528,128]{2,1,0:T(8,128)(2,1)S(1)}, u32[]{:S(2)}, u32[]{:S(2)}) collective-permute-start(bf16[1,528,128]{2,1,0:T(8,128)(2,1)S(1)} %repack.1), channel_id=1, source_target_pairs={{0,256},{1,257},{2,66},{3,67},{16,272},{17,273},{18,82},{19,83},{3... | collective-permute-start | bytes 405512 | tf_op jit(solution)/shard_map/ppermute | solution.py:313
  27.1 15.0 %collective-permute-start.2 = (bf16[1,528,128]{2,1,0:T(8,128)(2,1)S(1)}, bf16[1,528,128]{2,1,0:T(8,128)(2,1)S(1)}, u32[]{:S(2)}, u32[]{:S(2)}) collective-permute-start(bf16[1,528,128]{2,1,0:T(8,128)(2,1)S(1)} %repack.1), channel_id=1, source_target_pairs={{0,128},{1,385},{2,34},{3,35},{16,144},{17,401},{18,114},{19,115},... | collective-permute-start | bytes 405512 | tf_op jit(solution)/shard_map/ppermute | solution.py:313
  29.6 12.5 %collective-permute-start.1 = (bf16[1,528,128]{2,1,0:T(8,128)(2,1)S(1)}, bf16[1,528,128]{2,1,0:T(8,128)(2,1)S(1)}, u32[]{:S(2)}, u32[]{:S(2)}) collective-permute-start(bf16[1,528,128]{2,1,0:T(8,128)(2,1)S(1)} %repack.1), channel_id=1, source_target_pairs={{0,384},{1,129},{2,98},{3,99},{16,400},{17,145},{18,50},{19,51},{3... | collective-permute-start | bytes 405512 | tf_op jit(solution)/shard_map/ppermute | solution.py:313
  42.1 17.3 %collective-permute-start.3 = (bf16[4,528,128]{2,1,0:T(8,128)(2,1)S(1)}, bf16[4,528,128]{2,1,0:T(8,128)(2,1)S(1)}, u32[]{:S(2)}, u32[]{:S(2)}) collective-permute-start(bf16[4,528,128]{2,1,0:T(8,128)(2,1)S(1)} %constant_dynamic-update-slice_fusion.refs_1_), channel_id=1, source_target_pairs={{0,32},{1,33},{2,130},{3,387},{16,112},{17,113},{18,146},{19,403},... | collective-permute-start | bytes 1622024 | tf_op jit(solution)/shard_map/ppermute | solution.py:314
  47.8 19.3 %collective-permute-start.5 = (bf16[4,528,128]{2,1,0:T(8,128)(2,1)S(1)}, bf16[4,528,128]{2,1,0:T(8,128)(2,1)S(1)}, u32[]{:S(2)}, u32[]{:S(2)}) collective-permute-start(bf16[4,528,128]{2,1,0:T(8,128)(2,1)S(1)} %constant_dynamic-update-slice_fusion.refs_1_), channel_id=1, source_target_pairs={{0,96},{1,97},{2,386},{3,131},{16,48},{17,49},{18,402},{19,147},{3... | collective-permute-start | bytes 1622024 | tf_op jit(solution)/shard_map/ppermute | solution.py:315
  59.5 16.9 %collective-permute-start.4 = (bf16[4,528,128]{2,1,0:T(8,128)(2,1)S(1)}, bf16[4,528,128]{2,1,0:T(8,128)(2,1)S(1)}, u32[]{:S(2)}, u32[]{:S(2)}) collective-permute-start(bf16[4,528,128]{2,1,0:T(8,128)(2,1)S(1)} %collective-permute-done.3.refs_1_), channel_id=1, source_target_pairs={{0,32},{1,33},{2,130},{3,387},{16,112},{17,113},{18,146},{19,403},... | collective-permute-start | bytes 1622024 | tf_op jit(solution)/shard_map/ppermute | solution.py:318

commit v7 on v6

--- a/solution.py
+++ b/solution.py
@@ -12,7 +12,7 @@
 HD = 128
 MERGED = 8
 ZH, Y, X, CORE = 4, 8, 4, 2
-GROUP = ("yB", "x", "core")
+GROUP = ("core", "x", "yB")
 RING = ("zh", "yA", "yB", "core", "rep")
 REP = 2
 SCALE = 1.0 / math.sqrt(HD)
@@ -310,7 +310,7 @@
     queries, own = lax.optimization_barrier((queries, own))
     head_queries = lax.all_to_all(queries, GROUP, split_axis=0, concat_axis=0, tiled=True)
     head_queries = head_queries.reshape(targets, heads // targets, tokens, HD)
-    near = jnp.concatenate([own] + [lax.ppermute(own, RING, first_ring(by)) for by in (2, -1, 1)], axis=0)
+    near = jnp.concatenate([own] + [lax.ppermute(own, RING, first_ring(by)) for by in (2, 1, -1)], axis=0)
     up = lax.ppermute(near, RING, second_ring(1))
     down = lax.ppermute(near, RING, second_ring(-1))
     state = attend(head_queries, (near,), None, False)

time: 102 us -> 101 us (level)
  blocking collectives: 20.7 us -> 19.2 us
    all_to_all x1, blocking collectives: 20.7 us -> 19.2 us  [per_device(): lax.all_to_all(attended.reshape(heads, tokens, HD), GROUP, split_axis=0,...]
    ppermute x3, waiting for transfers between devices: 7.49 us -> 8.75 us  [per_device(): lax.ppermute(own, RING, first_ring(by))]
    ppermute x3, starting transfers between devices: 10.5 us -> 9.32 us  [per_device(): lax.ppermute(own, RING, first_ring(by))]
where the time goes in v7:
time: 101 us; the launch traced here: 100 us
  starting transfers between devices  44.4 us (44%)
  blocking collectives  19.2 us (19%)
  waiting for transfers between devices  17.8 us (18%)
  Pallas kernels  17.3 us (17%)
  local copies, waits for them, and re-layouts  1.19 us (1%)
    all_to_all x1, blocking collectives, per_device(): lax.all_to_all(attended.reshape(heads, tokens, HD), GROUP, split_axis=0,...  19.2 us
    pallas_call x3, Pallas kernels, attend(): pl.pallas_call(lambda *refs: attend_kernel(parts, first, last, sub, *refs...  11.4 us
    all_to_all x1, starting transfers between devices, per_device(): lax.all_to_all(merged, GROUP, split_axis=0, concat_axis=0, tiled=True)  10.2 us
    ppermute x3, starting transfers between devices, per_device(): lax.ppermute(own, RING, first_ring(by))  9.32 us
    ppermute x3, waiting for transfers between devices, per_device(): lax.ppermute(own, RING, first_ring(by))  8.75 us
    ppermute x1, starting transfers between devices, per_device(): far = lax.ppermute(up, RING, second_ring(1))  7.58 us
    ppermute x1, starting transfers between devices, per_device(): down = lax.ppermute(near, RING, second_ring(-1))  6.77 us
    ppermute x1, starting transfers between devices, per_device(): up = lax.ppermute(near, RING, second_ring(1))  5.63 us
  transfers between devices with their start and end apart: 8, of which 4 were waited for; matrix products, arithmetic and copies ran while one was open for 0% of the time, Pallas kernels for 11%

profile of v7, /device:TPU:1, one launch (start us, length us, event | category | flops | bytes accessed | tf_op | source)
XLA Modules:
  0.0 100.1 jit_solution(9791977739218443835)
XLA Ops:
  0.0 3.1 %prepare_merged.1 = bf16[16,40,128]{2,1,0:T(8,128)(2,1)} custom-call(bf16[128,4096]{1,0:T(8,128)(2,1)} %refs_0_.2, bf16[128,4096]{1,0:T(8,128)(2,1)} %refs_1_.1, s32[32,128]{1,0:T(8,128)} %bitcast.16, s32[32,128]{1,0:T(8,128)} %bitcast.17, s32[1,128]{1,0:T(1,128)} %bitcast.19), custom_call_target="tpu_custom_call" | custom-call | flops 134217728 | bytes 2097152 | tf_op jit(solution)/shard_map/prepare_merged/pallas_call | solution.py:102
  3.1 10.2 %all-to-all-start = ((bf16[16,40,128]{2,1,0:T(8,128)(2,1)}), bf16[16,40,128]{2,1,0:T(8,128)(2,1)S(1)}, u32[]{:S(2)}, u32[]{:S(2)}) async-start(bf16[16,40,128]{2,1,0:T(8,128)(2,1)} %prepare_merged.1), calls=%async_computation | async-start | bytes 327680 | tf_op jit(solution)/shard_map/all_to_all | solution.py:307
  13.3 2.8 %prepare_queries.1 = bf16[32,128,128]{2,1,0:T(8,128)(2,1)} custom-call(bf16[128,4096]{1,0:T(8,128)(2,1)} %refs_0_.3, s32[32,128]{1,0:T(8,128)} %bitcast.18), custom_call_target="tpu_custom_call" | custom-call | flops 134217728 | bytes 2097152 | tf_op jit(solution)/shard_map/prepare_queries/pallas_call | solution.py:143
  16.1 3.0 %all-to-all-done.in_ref = bf16[16,40,128]{2,1,0:T(8,128)(2,1)S(1)} async-done(((bf16[16,40,128]{2,1,0:T(8,128)(2,1)}), bf16[16,40,128]{2,1,0:T(8,128)(2,1)S(1)}, u32[]{:S(2)}, u32[]{:S(2)}) %all-to-all-start) | async-done | bytes 163872 | tf_op jit(solution)/shard_map/all_to_all | solution.py:307
  19.2 4.8 %all-to-all-start.1 = ((bf16[32,128,128]{2,1,0:T(8,128)(2,1)}), bf16[32,128,128]{2,1,0:T(8,128)(2,1)S(1)}, u32[]{:S(2)}, u32[]{:S(2)}) async-start(bf16[32,128,128]{2,1,0:T(8,128)(2,1)} %prepare_queries.1), calls=%async_computation.1 | async-start | bytes 2097152 | tf_op jit(solution)/shard_map/all_to_all | solution.py:311
  24.0 3.1 %collective-permute-start = (bf16[1,528,128]{2,1,0:T(8,128)(2,1)S(1)}, bf16[1,528,128]{2,1,0:T(8,128)(2,1)S(1)}, u32[]{:S(2)}, u32[]{:S(2)}) collective-permute-start(bf16[1,528,128]{2,1,0:T(8,128)(2,1)S(1)} %repack.1), channel_id=1, source_target_pairs={{0,256},{1,257},{2,66},{3,67},{16,272},{17,273},{18,82},{19,83},{3... | collective-permute-start | bytes 405512 | tf_op jit(solution)/shard_map/ppermute | solution.py:313
  27.2 2.9 %collective-permute-start.2 = (bf16[1,528,128]{2,1,0:T(8,128)(2,1)S(1)}, bf16[1,528,128]{2,1,0:T(8,128)(2,1)S(1)}, u32[]{:S(2)}, u32[]{:S(2)}) collective-permute-start(bf16[1,528,128]{2,1,0:T(8,128)(2,1)S(1)} %repack.1), channel_id=1, source_target_pairs={{0,384},{1,129},{2,98},{3,99},{16,400},{17,145},{18,50},{19,51},{3... | collective-permute-start | bytes 405512 | tf_op jit(solution)/shard_map/ppermute | solution.py:313
  30.0 3.3 %collective-permute-start.1 = (bf16[1,528,128]{2,1,0:T(8,128)(2,1)S(1)}, bf16[1,528,128]{2,1,0:T(8,128)(2,1)S(1)}, u32[]{:S(2)}, u32[]{:S(2)}) collective-permute-start(bf16[1,528,128]{2,1,0:T(8,128)(2,1)S(1)} %repack.1), channel_id=1, source_target_pairs={{0,128},{1,385},{2,34},{3,35},{16,144},{17,401},{18,114},{19,115},... | collective-permute-start | bytes 405512 | tf_op jit(solution)/shard_map/ppermute | solution.py:313
  33.4 8.7 %collective-permute-done = bf16[1,528,128]{2,1,0:T(8,128)(2,1)S(1)} collective-permute-done((bf16[1,528,128]{2,1,0:T(8,128)(2,1)S(1)}, bf16[1,528,128]{2,1,0:T(8,128)(2,1)S(1)}, u32[]{:S(2)}, u32[]{:S(2)}) %collective-permute-start) | collective-permute-done | bytes 135200 | tf_op jit(solution)/shard_map/ppermute | solution.py:313
  42.2 0.0 collective-permute-done.1
  42.2 0.0 collective-permute-done.2
  42.2 5.6 %collective-permute-start.3 = (bf16[4,528,128]{2,1,0:T(8,128)(2,1)S(1)}, bf16[4,528,128]{2,1,0:T(8,128)(2,1)S(1)}, u32[]{:S(2)}, u32[]{:S(2)}) collective-permute-start(bf16[4,528,128]{2,1,0:T(8,128)(2,1)S(1)} %constant_dynamic-update-slice_fusion.refs_1_), channel_id=1, source_target_pairs={{0,32},{1,33},{2,130},{3,387},{16,112},{17,113},{18,146},{19,403},... | collective-permute-start | bytes 1622024 | tf_op jit(solution)/shard_map/ppermute | solution.py:314
  47.9 6.8 %collective-permute-start.5 = (bf16[4,528,128]{2,1,0:T(8,128)(2,1)S(1)}, bf16[4,528,128]{2,1,0:T(8,128)(2,1)S(1)}, u32[]{:S(2)}, u32[]{:S(2)}) collective-permute-start(bf16[4,528,128]{2,1,0:T(8,128)(2,1)S(1)} %constant_dynamic-update-slice_fusion.refs_1_), channel_id=1, source_target_pairs={{0,96},{1,97},{2,386},{3,131},{16,48},{17,49},{18,402},{19,147},{3... | collective-permute-start | bytes 1622024 | tf_op jit(solution)/shard_map/ppermute | solution.py:315
  54.6 0.0 all-to-all-done.1
  54.7 2.7 %attend.3 = (f32[2,2048,256]{2,1,0:T(8,128)S(1)}, f32[2,2048,128]{2,1,0:T(8,128)S(1)}) custom-call(bf16[16,2,128,128]{3,2,1,0:T(8,128)(2,1)S(1)} %bitcast.12, bf16[4,528,128]{2,1,0:T(8,128)(2,1)S(1)} %constant_dynamic-update-slice_fusion.refs_1_), custom_call_target="tpu_custom_call" | custom-call | flops 2147483648 | bytes 8388608 | tf_op jit(solution)/shard_map/attend/pallas_call | solution.py:252
  57.3 2.3 %collective-permute-done.3.refs_1_ = bf16[4,528,128]{2,1,0:T(8,128)(2,1)S(1)} collective-permute-done((bf16[4,528,128]{2,1,0:T(8,128)(2,1)S(1)}, bf16[4,528,128]{2,1,0:T(8,128)(2,1)S(1)}, u32[]{:S(2)}, u32[]{:S(2)}) %collective-permute-start.3) | collective-permute-done | bytes 540704 | tf_op jit(solution)/shard_map/ppermute | solution.py:314
  59.6 7.6 %collective-permute-start.4 = (bf16[4,528,128]{2,1,0:T(8,128)(2,1)S(1)}, bf16[4,528,128]{2,1,0:T(8,128)(2,1)S(1)}, u32[]{:S(2)}, u32[]{:S(2)}) collective-permute-start(bf16[4,528,128]{2,1,0:T(8,128)(2,1)S(1)} %collective-permute-done.3.refs_1_), channel_id=1, source_target_pairs={{0,32},{1,33},{2,130},{3,387},{16,112},{17,113},{18,146},{19,403},... | collective-permute-start | bytes 1622024 | tf_op jit(solution)/shard_map/ppermute | solution.py:318
  67.2 0.0 collective-permute-done.5.refs_2_
  67.2 5.5 %attend.4 = (f32[2,2048,256]{2,1,0:T(8,128)S(1)}, f32[2,2048,128]{2,1,0:T(8,128)S(1)}) custom-call(bf16[16,2,128,128]{3,2,1,0:T(8,128)(2,1)S(1)} %bitcast.13, bf16[4,528,128]{2,1,0:T(8,128)(2,1)S(1)} %collective-permute-done.3.refs_1_, bf16[4,528,128]{2,1,0:T(8,128)(2,1)S(1)} %collective-permute-done.5.refs_2_, ...), custom_call_target="tpu_custom_call" | custom-call | flops 4294967296 | bytes 8388608 | tf_op jit(solution)/shard_map/attend/pallas_call | solution.py:252
  72.7 3.8 %collective-permute-done.4.refs_1_ = bf16[4,528,128]{2,1,0:T(8,128)(2,1)S(1)} collective-permute-done((bf16[4,528,128]{2,1,0:T(8,128)(2,1)S(1)}, bf16[4,528,128]{2,1,0:T(8,128)(2,1)S(1)}, u32[]{:S(2)}, u32[]{:S(2)}) %collective-permute-start.4) | collective-permute-done | bytes 540704 | tf_op jit(solution)/shard_map/ppermute | solution.py:318
  76.5 3.2 %attend.5 = bf16[16,2,128,128]{3,2,1,0:T(8,128)(2,1)S(1)} custom-call(bf16[16,2,128,128]{3,2,1,0:T(8,128)(2,1)S(1)} %bitcast.14, bf16[4,528,128]{2,1,0:T(8,128)(2,1)S(1)} %collective-permute-done.4.refs_1_, f32[2,2048,256]{2,1,0:T(8,128)S(1)} %get-tuple-element.25.refs_2_, f32[2,2048,128]{2,1,0:T(8,128)S(1)} %get-tuple-element.26.refs_3_), custom_call_target="tpu_custom_call" | custom-call | flops 2147483648 | bytes 8388608 | tf_op jit(solution)/shard_map/attend/pallas_call | solution.py:252
  79.7 19.2 %all_to_all.15 = bf16[32,128,128]{2,1,0:T(8,128)(2,1)S(1)} all-to-all(bf16[32,128,128]{2,1,0:T(8,128)(2,1)S(1)} %bitcast.15), channel_id=1, replica_groups=mesh['zh'=4,'yA'=4,'yB'=2,'x'=4,'core'=2,'rep'=2] {'core','x','yB'}, dimensions={0} | all-to-all | bytes 2097152 | tf_op jit(solution)/shard_map/all_to_all | solution.py:321
  99.0 1.1 %copy_bitcast_fusion = bf16[128,4096]{1,0:T(8,128)(2,1)} fusion(bf16[32,128,128]{2,1,0:T(8,128)(2,1)S(1)} %all_to_all.15), kind=kLoop, calls=%fused_computation | loop fusion | bytes 2097152 | tf_op jit(solution)/shard_map/reshape | solution.py:324
  (5 shorter events, 0.1 us)
Async XLA Ops:
  3.1 16.1 %all-to-all-start = ((bf16[16,40,128]{2,1,0:T(8,128)(2,1)}), bf16[16,40,128]{2,1,0:T(8,128)(2,1)S(1)}, u32[]{:S(2)}, u32[]{:S(2)}) async-start(bf16[16,40,128]{2,1,0:T(8,128)(2,1)} %prepare_merged.1), calls=%async_computation | async-start | bytes 327680 | tf_op jit(solution)/shard_map/all_to_all | solution.py:307
  19.2 35.5 %all-to-all-start.1 = ((bf16[32,128,128]{2,1,0:T(8,128)(2,1)}), bf16[32,128,128]{2,1,0:T(8,128)(2,1)S(1)}, u32[]{:S(2)}, u32[]{:S(2)}) async-start(bf16[32,128,128]{2,1,0:T(8,128)(2,1)} %prepare_queries.1), calls=%async_computation.1 | async-start | bytes 2097152 | tf_op jit(solution)/shard_map/all_to_all | solution.py:311
  24.0 18.1 %collective-permute-start = (bf16[1,528,128]{2,1,0:T(8,128)(2,1)S(1)}, bf16[1,528,128]{2,1,0:T(8,128)(2,1)S(1)}, u32[]{:S(2)}, u32[]{:S(2)}) collective-permute-start(bf16[1,528,128]{2,1,0:T(8,128)(2,1)S(1)} %repack.1), channel_id=1, source_target_pairs={{0,256},{1,257},{2,66},{3,67},{16,272},{17,273},{18,82},{19,83},{3... | collective-permute-start | bytes 405512 | tf_op jit(solution)/shard_map/ppermute | solution.py:313
  27.2 15.0 %collective-permute-start.2 = (bf16[1,528,128]{2,1,0:T(8,128)(2,1)S(1)}, bf16[1,528,128]{2,1,0:T(8,128)(2,1)S(1)}, u32[]{:S(2)}, u32[]{:S(2)}) collective-permute-start(bf16[1,528,128]{2,1,0:T(8,128)(2,1)S(1)} %repack.1), channel_id=1, source_target_pairs={{0,384},{1,129},{2,98},{3,99},{16,400},{17,145},{18,50},{19,51},{3... | collective-permute-start | bytes 405512 | tf_op jit(solution)/shard_map/ppermute | solution.py:313
  30.0 12.1 %collective-permute-start.1 = (bf16[1,528,128]{2,1,0:T(8,128)(2,1)S(1)}, bf16[1,528,128]{2,1,0:T(8,128)(2,1)S(1)}, u32[]{:S(2)}, u32[]{:S(2)}) collective-permute-start(bf16[1,528,128]{2,1,0:T(8,128)(2,1)S(1)} %repack.1), channel_id=1, source_target_pairs={{0,128},{1,385},{2,34},{3,35},{16,144},{17,401},{18,114},{19,115},... | collective-permute-start | bytes 405512 | tf_op jit(solution)/shard_map/ppermute | solution.py:313
  42.2 17.4 %collective-permute-start.3 = (bf16[4,528,128]{2,1,0:T(8,128)(2,1)S(1)}, bf16[4,528,128]{2,1,0:T(8,128)(2,1)S(1)}, u32[]{:S(2)}, u32[]{:S(2)}) collective-permute-start(bf16[4,528,128]{2,1,0:T(8,128)(2,1)S(1)} %constant_dynamic-update-slice_fusion.refs_1_), channel_id=1, source_target_pairs={{0,32},{1,33},{2,130},{3,387},{16,112},{17,113},{18,146},{19,403},... | collective-permute-start | bytes 1622024 | tf_op jit(solution)/shard_map/ppermute | solution.py:314
  47.9 19.3 %collective-permute-start.5 = (bf16[4,528,128]{2,1,0:T(8,128)(2,1)S(1)}, bf16[4,528,128]{2,1,0:T(8,128)(2,1)S(1)}, u32[]{:S(2)}, u32[]{:S(2)}) collective-permute-start(bf16[4,528,128]{2,1,0:T(8,128)(2,1)S(1)} %constant_dynamic-update-slice_fusion.refs_1_), channel_id=1, source_target_pairs={{0,96},{1,97},{2,386},{3,131},{16,48},{17,49},{18,402},{19,147},{3... | collective-permute-start | bytes 1622024 | tf_op jit(solution)/shard_map/ppermute | solution.py:315
  59.6 16.9 %collective-permute-start.4 = (bf16[4,528,128]{2,1,0:T(8,128)(2,1)S(1)}, bf16[4,528,128]{2,1,0:T(8,128)(2,1)S(1)}, u32[]{:S(2)}, u32[]{:S(2)}) collective-permute-start(bf16[4,528,128]{2,1,0:T(8,128)(2,1)S(1)} %collective-permute-done.3.refs_1_), channel_id=1, source_target_pairs={{0,32},{1,33},{2,130},{3,387},{16,112},{17,113},{18,146},{19,403},... | collective-permute-start | bytes 1622024 | tf_op jit(solution)/shard_map/ppermute | solution.py:318
